TPU v7x, 32 devices: a whole 2x2x4 slice. The times are simulated.
32 devices in a mesh: req: 8 (over z, y), tp: 4 (over x, core).
Axes of the slice: x: 2, y: 2, z: 4, core: 2. Of those that a mesh axis runs over, the one named last changes fastest.
Arguments:
- tokens: bfloat16 [64, 16, 1792], P('req'), may hold values from -6 to 6
- conv_edge: bfloat16 [64, 2, 1792], P('req'), may hold values from -6 to 6
- state_start: float32 [16, 1956864], P('tp', 'req'), may hold values from -60 to 60
- norm_start: float32 [16, 64, 273], P('tp', 'req'), may hold values from -200 to 200, as said below
- accepted: int32 [64], P('req'), may hold values from 0 to 16
- owner: int32 [64], P('req'), may hold values from 0 to 7, as said below
- attn_gain: float32 [1792], replicated, may hold values from 0.5 to 1.5
- conv_weight: float32 [3, 1792], replicated, may hold values from -3 to 3
- w_query: bfloat16 [1792, 256], P(None, 'tp'), may hold values from -0.125 to 0.125
- w_key: bfloat16 [1792, 256], P(None, 'tp'), may hold values from -0.125 to 0.125
- w_value: bfloat16 [1792, 1792], P('tp'), may hold values from -0.125 to 0.125
- w_out: bfloat16 [1792, 1792], P('tp'), may hold values from -0.125 to 0.125
- mlp_gain: float32 [1792], replicated, may hold values from 0.5 to 1.5
- w_gate: bfloat16 [1792, 2048], P(None, 'tp'), may hold values from -0.125 to 0.125
- w_up: bfloat16 [1792, 2048], P(None, 'tp'), may hold values from -0.125 to 0.125
- w_down: bfloat16 [2048, 1792], P('tp'), may hold values from -0.125 to 0.125
Outputs:
- hidden_out: bfloat16 [64, 16, 1792], P('req')
- kept_state: float32 [16, 3913728], P('tp', 'req')
- kept_norm: float32 [16, 128, 273], P('tp', 'req')
- kept_edge: bfloat16 [128, 2, 1792], P('req', None, 'tp')
Inputs may be any that keep to these rules, and one draw needn't show every extreme that they name: The requests of one device go to one owner at most 2 times, and some device sends exactly 2 to one owner; an owner receives at most 16 requests in all, and some owner exactly 16. Each norm_start[h, r] is a sum of key features: c times [1, m, (m_i m_j + v_i delta_ij) / sqrt(2) for i then j] with a count c from 4 to 48 (its first entry), a mean m of 16 entries and v_i from 0.2 to 1, so that phi(u) . norm_start[h, r] >= c / 2 for every vector u.
All inputs are finite; a program needn't handle non-finite values.
Results may differ from a plain program's by a relative error of at most 0.015.
Values may be sent and summed in bfloat16 or wider, within the bound.
No kernel may reach another device: no remote copies, remote signals or barrier semaphores. Data moves between devices by JAX's collectives and lax.ppermute only.
A program may use at most 128 MiB of HBM per device.

v0:
```python
import math

import jax
import jax.numpy as jnp
from jax import lax
from jax.sharding import PartitionSpec as P

FD = 16
DV = 112
F = 273
CAP = 16


EPSILON = 1e-05
HIGHEST = lax.Precision.HIGHEST


def carried_in(x, axis, combine, identity):
    count, here = (lax.axis_size(axis), lax.axis_index(axis))
    everything = lax.all_gather(x, axis)
    start = jnp.broadcast_to(jnp.asarray(identity, x.dtype), x.shape)

    def turn(k, before):
        reached = k < here
        new = combine(before, everything[k])
        return jnp.where(reached, new, before)

    return lax.fori_loop(0, count, turn, start)


def features(values, width):
    scaled = values * width ** (-0.25)
    leading = values.shape[:-1]
    square = (scaled[..., :, None] * scaled[..., None, :]).reshape(
        leading + (width * width,)
    ) * math.sqrt(0.5)
    return jnp.concatenate([jnp.ones(leading + (1,), jnp.float32), scaled, square], axis=-1)


def rms_scaled(row_block, gain_row):
    widened = row_block.astype(jnp.float32)
    return (
        widened
        * lax.rsqrt(jnp.mean(widened * widened, axis=-1, keepdims=True) + EPSILON)
        * gain_row
    )


def shards(
    tokens,
    conv_edge,
    state_start,
    norm_start,
    accepted,
    owner,
    attn_gain,
    conv_weight,
    w_query,
    w_key,
    w_value,
    w_out,
    mlp_gain,
    w_gate,
    w_up,
    w_down,
):
    requests, draft_steps, model_width = tokens.shape
    owners = lax.axis_size("req")
    pair_cap = (CAP + owners - 1) // owners
    local_heads = w_query.shape[1] // FD
    column_width = model_width // lax.axis_size("tp")
    tap_count = conv_weight.shape[0]
    state_four = state_start.reshape(local_heads, requests, F, DV)
    marked = (owner[:, None] == jnp.arange(owners)[None, :]).astype(jnp.int32)
    offsets = carried_in(
        jnp.sum(marked, axis=0),
        "req",
        lambda earlier, later: earlier + later,
        jnp.zeros((owners,), jnp.int32),
    )
    local_rank = jnp.sum((jnp.cumsum(marked, axis=0) - marked) * marked, axis=1)
    slot_index = jnp.sum(offsets[None, :] * marked, axis=1) + local_rank
    position = owner * pair_cap + local_rank
    lane_count = owners * pair_cap
    chooser = (
        jnp.full((lane_count,), requests, jnp.int32)
        .at[position]
        .set(jnp.arange(requests, dtype=jnp.int32))
    )
    slot_sent = jnp.full((lane_count,), CAP, jnp.int32).at[position].set(slot_index)

    def packed_lanes(lane_block):
        extended = jnp.concatenate(
            [
                lane_block,
                jnp.zeros((lane_block.shape[0], 1) + lane_block.shape[2:], lane_block.dtype),
            ],
            axis=1,
        )
        return extended[:, chooser]

    def settle_lanes(lane_block, slot_rows):
        return (
            jnp.zeros((lane_block.shape[0], CAP) + lane_block.shape[2:], lane_block.dtype)
            .at[:, slot_rows]
            .set(lane_block, mode="drop")
        )

    normed = rms_scaled(tokens, attn_gain).astype(jnp.bfloat16)
    padded = jnp.concatenate([conv_edge, normed], axis=1)
    normed_wide = normed.astype(jnp.float32)
    convolved = jnp.zeros(normed.shape, jnp.float32)
    for tap_index in range(tap_count):
        convolved = convolved + conv_weight[tap_index] * padded[
            :, tap_index : tap_index + draft_steps
        ].astype(jnp.float32)
    mixed_rows = (normed_wide + convolved * jax.nn.sigmoid(normed_wide)).astype(jnp.bfloat16)
    flat_rows = mixed_rows.reshape(requests * draft_steps, model_width)
    query_rows = jnp.dot(flat_rows, w_query, preferred_element_type=jnp.float32).astype(
        jnp.bfloat16
    )
    key_rows = jnp.dot(flat_rows, w_key, preferred_element_type=jnp.float32).astype(jnp.bfloat16)
    value_rows = lax.dot_general(
        flat_rows, w_value, (((1,), (1,)), ((), ())), preferred_element_type=jnp.float32
    ).astype(jnp.bfloat16)
    query_features = features(
        query_rows.astype(jnp.float32).reshape(requests, draft_steps, local_heads, FD), FD
    )
    key_features = features(
        key_rows.astype(jnp.float32).reshape(requests, draft_steps, local_heads, FD), FD
    )
    value_wide = value_rows.astype(jnp.float32).reshape(requests, draft_steps, local_heads, DV)

    def advance(carry, inputs):
        state_sum, totals, held_state, held_norm = carry
        step_index, query_step, key_step, value_step = inputs
        key_heads = jnp.swapaxes(key_step, 0, 1)
        value_heads = jnp.swapaxes(value_step, 0, 1)
        state_sum = state_sum + key_heads[..., :, None] * value_heads[..., None, :]
        totals = totals + key_heads
        numerator = jnp.einsum("rhf,hrfd->rhd", query_step, state_sum, precision=HIGHEST)
        denominator = jnp.einsum("rhf,hrf->rh", query_step, totals, precision=HIGHEST)
        landed = accepted == step_index + 1
        held_state = jnp.where(landed[None, :, None, None], state_sum, held_state)
        held_norm = jnp.where(landed[None, :, None], totals, held_norm)
        return ((state_sum, totals, held_state, held_norm), numerator / denominator[..., None])

    initial = (state_four, norm_start, state_four, norm_start)
    inputs = (
        jnp.arange(draft_steps, dtype=jnp.int32),
        jnp.swapaxes(query_features, 0, 1),
        jnp.swapaxes(key_features, 0, 1),
        jnp.swapaxes(value_wide, 0, 1),
    )
    final_carry, outputs = lax.scan(advance, initial, inputs)
    chosen_state, chosen_norm = (final_carry[2], final_carry[3])
    attended = jnp.swapaxes(outputs, 0, 1)
    merged = attended.astype(jnp.bfloat16).reshape(requests * draft_steps, local_heads * DV)
    attn_part = jnp.dot(merged, w_out, preferred_element_type=jnp.float32)
    residual = tokens.reshape(requests * draft_steps, model_width).astype(jnp.float32) + lax.psum(
        attn_part, "tp"
    )
    second = rms_scaled(residual, mlp_gain).astype(jnp.bfloat16)
    gate_rows = jnp.dot(second, w_gate, preferred_element_type=jnp.float32)
    upward = jnp.dot(second, w_up, preferred_element_type=jnp.float32)
    hidden = (jax.nn.silu(gate_rows) * upward).astype(jnp.bfloat16)
    mlp_part = jnp.dot(hidden, w_down, preferred_element_type=jnp.float32)
    hidden_out = (
        (residual + lax.psum(mlp_part, "tp"))
        .astype(jnp.bfloat16)
        .reshape(requests, draft_steps, model_width)
    )
    edge_index = accepted[:, None] + jnp.arange(tap_count - 1)[None, :]
    column_start = lax.axis_index("tp") * column_width
    columns = lax.dynamic_slice_in_dim(padded, column_start, column_width, 2)
    chosen_edge = jnp.take_along_axis(columns, edge_index[:, :, None], axis=1)
    edge_heads = jnp.transpose(
        chosen_edge.astype(jnp.float32).reshape(requests, tap_count - 1, local_heads, DV),
        (2, 0, 1, 3),
    ).reshape(local_heads, requests, (tap_count - 1) * DV)
    arrived_state, arrived_norm, arrived_edge, arrived_slot_row = (
        lax.all_to_all(packed_lanes(chosen_state), "req", split_axis=1, concat_axis=1, tiled=True),
        lax.all_to_all(packed_lanes(chosen_norm), "req", split_axis=1, concat_axis=1, tiled=True),
        lax.all_to_all(packed_lanes(edge_heads), "req", split_axis=1, concat_axis=1, tiled=True),
        lax.all_to_all(slot_sent[None, :], "req", split_axis=1, concat_axis=1, tiled=True),
    )
    arrived_slot = arrived_slot_row[0]
    kept_state = settle_lanes(arrived_state, arrived_slot).reshape(local_heads, CAP * F * DV)
    kept_norm = settle_lanes(arrived_norm, arrived_slot)
    edge_back = settle_lanes(arrived_edge, arrived_slot).reshape(
        local_heads, CAP, tap_count - 1, DV
    )
    kept_edge = (
        jnp.transpose(edge_back, (1, 2, 0, 3))
        .reshape(CAP, tap_count - 1, column_width)
        .astype(jnp.bfloat16)
    )
    return (hidden_out, kept_state, kept_norm, kept_edge)


def solution(mesh):
    placed = (
        P("req", None, None),
        P("req", None, None),
        P("tp", "req"),
        P("tp", "req", None),
        P("req"),
        P("req"),
        P(),
        P(),
        P(None, "tp"),
        P(None, "tp"),
        P("tp", None),
        P("tp", None),
        P(),
        P(None, "tp"),
        P(None, "tp"),
        P("tp", None),
    )
    return jax.shard_map(
        shards,
        mesh=mesh,
        in_specs=placed,
        out_specs=(
            P("req", None, None),
            P("tp", "req"),
            P("tp", "req", None),
            P("req", None, "tp"),
        ),
        check_vma=False,
    )
```

profile of v0, /device:TPU:8, one launch (start us, length us, event | category | flops | bytes accessed | tf_op | source)
XLA Modules:
  0.0 594.4 jit_solution(13107008110304697121)
XLA Ops:
  11.7 10.5 %all-reduce.3 = s32[64]{0:T(128)S(1)} all-reduce(s32[64]{0:T(128)S(1)} %dynamic-update-slice), channel_id=2, replica_groups=mesh['req'=8,'tp'=4] {'req'}, use_global_device_ids=true, to_apply=%add.3 | all-reduce | flops 64 | bytes 512
  25.4 4.8 all-to-all-start
  58.9 8.6 %reshape.203 = f32[4,8,273,112]{3,2,1,0:T(8,128)} reshape(f32[4,244608]{1,0:T(4,128)} %param.22) | data formatting | bytes 7827456 | tf_op jit(solution)/shard_map/reshape | solution.py:73
  71.5 4.7 copy.163
  77.5 6.3 %all-to-all-start.3 = ((f32[4,16,224]{2,0,1:T(4,128)}), f32[4,16,224]{2,0,1:T(4,128)S(1)}, u32[]{:S(2)}, u32[]{:S(2)}) async-start(f32[4,16,224]{2,0,1:T(4,128)} %bitcast.27), calls=%async_computation.3 | async-start | bytes 131072 | tf_op jit(solution)/shard_map/all_to_all | solution.py:184
  83.8 237.0 %while.32 = (s32[]{:T(128)}, f32[4,8,273,112]{3,2,1,0:T(8,128)}, f32[4,8,273]{2,1,0:T(8,128)S(1)}, f32[4,8,273,112]{3,2,1,0:T(8,128)}, f32[4,8,273]{2,1,0:T(8,12...) while((s32[]{:T(128)}, f32[4,8,273,112]{3,2,1,0:T(8,128)}, ...), condition=%wide.region_2.3_spmd, body=%wide.region_1.2_spmd.sunk | while | flops 14714987 | bytes 20146408 | solution.py:155
  87.7 6.6 %broadcast_select_fusion.8 = (f32[4,8,273,112]{3,2,1,0:T(8,128)}, f32[4,8,273,112]{3,2,1,0:T(8,128)}) fusion(f32[4,8,273,112]{3,2,1,0:T(8,128)} %get-tuple-element.393, pred[8]{0:T(512)(128)(4,1)S(1)} %broadcast_compare_fusion.2, f32[4,8,273,112]{3,2,1,0:T(8,128)} %get-tuple-element.391, f32[4,8,112]{2,1,0:T(8,128)S(1)} %bitcast.103, ...), kind=kLoop, calls=%fused_computation.14.clone.1 | loop fusion | flops 2935296 | bytes 15704200 | tf_op jit(solution)/shard_map/while/body/eval_jaxpr/jit(_where)/select_n | solution.py:144
  94.3 4.2 fusion.59
  102.5 6.6 %broadcast_select_fusion.8 = (f32[4,8,273,112]{3,2,1,0:T(8,128)}, f32[4,8,273,112]{3,2,1,0:T(8,128)}) fusion(f32[4,8,273,112]{3,2,1,0:T(8,128)} %get-tuple-element.393, pred[8]{0:T(512)(128)(4,1)S(1)} %broadcast_compare_fusion.2, f32[4,8,273,112]{3,2,1,0:T(8,128)} %get-tuple-element.391, f32[4,8,112]{2,1,0:T(8,128)S(1)} %bitcast.103, ...), kind=kLoop, calls=%fused_computation.14.clone.1 | loop fusion | flops 2935296 | bytes 15704200 | tf_op jit(solution)/shard_map/while/body/eval_jaxpr/jit(_where)/select_n | solution.py:144
  109.1 4.2 fusion.59
  117.3 6.6 %broadcast_select_fusion.8 = (f32[4,8,273,112]{3,2,1,0:T(8,128)}, f32[4,8,273,112]{3,2,1,0:T(8,128)}) fusion(f32[4,8,273,112]{3,2,1,0:T(8,128)} %get-tuple-element.393, pred[8]{0:T(512)(128)(4,1)S(1)} %broadcast_compare_fusion.2, f32[4,8,273,112]{3,2,1,0:T(8,128)} %get-tuple-element.391, f32[4,8,112]{2,1,0:T(8,128)S(1)} %bitcast.103, ...), kind=kLoop, calls=%fused_computation.14.clone.1 | loop fusion | flops 2935296 | bytes 15704200 | tf_op jit(solution)/shard_map/while/body/eval_jaxpr/jit(_where)/select_n | solution.py:144
  123.9 4.2 fusion.59
  132.1 6.6 %broadcast_select_fusion.8 = (f32[4,8,273,112]{3,2,1,0:T(8,128)}, f32[4,8,273,112]{3,2,1,0:T(8,128)}) fusion(f32[4,8,273,112]{3,2,1,0:T(8,128)} %get-tuple-element.393, pred[8]{0:T(512)(128)(4,1)S(1)} %broadcast_compare_fusion.2, f32[4,8,273,112]{3,2,1,0:T(8,128)} %get-tuple-element.391, f32[4,8,112]{2,1,0:T(8,128)S(1)} %bitcast.103, ...), kind=kLoop, calls=%fused_computation.14.clone.1 | loop fusion | flops 2935296 | bytes 15704200 | tf_op jit(solution)/shard_map/while/body/eval_jaxpr/jit(_where)/select_n | solution.py:144
  138.7 4.2 fusion.59
  146.9 6.6 %broadcast_select_fusion.8 = (f32[4,8,273,112]{3,2,1,0:T(8,128)}, f32[4,8,273,112]{3,2,1,0:T(8,128)}) fusion(f32[4,8,273,112]{3,2,1,0:T(8,128)} %get-tuple-element.393, pred[8]{0:T(512)(128)(4,1)S(1)} %broadcast_compare_fusion.2, f32[4,8,273,112]{3,2,1,0:T(8,128)} %get-tuple-element.391, f32[4,8,112]{2,1,0:T(8,128)S(1)} %bitcast.103, ...), kind=kLoop, calls=%fused_computation.14.clone.1 | loop fusion | flops 2935296 | bytes 15704200 | tf_op jit(solution)/shard_map/while/body/eval_jaxpr/jit(_where)/select_n | solution.py:144
  153.5 4.2 fusion.59
  161.7 6.6 %broadcast_select_fusion.8 = (f32[4,8,273,112]{3,2,1,0:T(8,128)}, f32[4,8,273,112]{3,2,1,0:T(8,128)}) fusion(f32[4,8,273,112]{3,2,1,0:T(8,128)} %get-tuple-element.393, pred[8]{0:T(512)(128)(4,1)S(1)} %broadcast_compare_fusion.2, f32[4,8,273,112]{3,2,1,0:T(8,128)} %get-tuple-element.391, f32[4,8,112]{2,1,0:T(8,128)S(1)} %bitcast.103, ...), kind=kLoop, calls=%fused_computation.14.clone.1 | loop fusion | flops 2935296 | bytes 15704200 | tf_op jit(solution)/shard_map/while/body/eval_jaxpr/jit(_where)/select_n | solution.py:144
  168.3 4.2 fusion.59
  176.5 6.6 %broadcast_select_fusion.8 = (f32[4,8,273,112]{3,2,1,0:T(8,128)}, f32[4,8,273,112]{3,2,1,0:T(8,128)}) fusion(f32[4,8,273,112]{3,2,1,0:T(8,128)} %get-tuple-element.393, pred[8]{0:T(512)(128)(4,1)S(1)} %broadcast_compare_fusion.2, f32[4,8,273,112]{3,2,1,0:T(8,128)} %get-tuple-element.391, f32[4,8,112]{2,1,0:T(8,128)S(1)} %bitcast.103, ...), kind=kLoop, calls=%fused_computation.14.clone.1 | loop fusion | flops 2935296 | bytes 15704200 | tf_op jit(solution)/shard_map/while/body/eval_jaxpr/jit(_where)/select_n | solution.py:144
  183.1 4.2 fusion.59
  191.3 6.6 %broadcast_select_fusion.8 = (f32[4,8,273,112]{3,2,1,0:T(8,128)}, f32[4,8,273,112]{3,2,1,0:T(8,128)}) fusion(f32[4,8,273,112]{3,2,1,0:T(8,128)} %get-tuple-element.393, pred[8]{0:T(512)(128)(4,1)S(1)} %broadcast_compare_fusion.2, f32[4,8,273,112]{3,2,1,0:T(8,128)} %get-tuple-element.391, f32[4,8,112]{2,1,0:T(8,128)S(1)} %bitcast.103, ...), kind=kLoop, calls=%fused_computation.14.clone.1 | loop fusion | flops 2935296 | bytes 15704200 | tf_op jit(solution)/shard_map/while/body/eval_jaxpr/jit(_where)/select_n | solution.py:144
  197.9 4.2 fusion.59
  206.2 6.6 %broadcast_select_fusion.8 = (f32[4,8,273,112]{3,2,1,0:T(8,128)}, f32[4,8,273,112]{3,2,1,0:T(8,128)}) fusion(f32[4,8,273,112]{3,2,1,0:T(8,128)} %get-tuple-element.393, pred[8]{0:T(512)(128)(4,1)S(1)} %broadcast_compare_fusion.2, f32[4,8,273,112]{3,2,1,0:T(8,128)} %get-tuple-element.391, f32[4,8,112]{2,1,0:T(8,128)S(1)} %bitcast.103, ...), kind=kLoop, calls=%fused_computation.14.clone.1 | loop fusion | flops 2935296 | bytes 15704200 | tf_op jit(solution)/shard_map/while/body/eval_jaxpr/jit(_where)/select_n | solution.py:144
  212.8 4.2 fusion.59
  221.0 6.6 %broadcast_select_fusion.8 = (f32[4,8,273,112]{3,2,1,0:T(8,128)}, f32[4,8,273,112]{3,2,1,0:T(8,128)}) fusion(f32[4,8,273,112]{3,2,1,0:T(8,128)} %get-tuple-element.393, pred[8]{0:T(512)(128)(4,1)S(1)} %broadcast_compare_fusion.2, f32[4,8,273,112]{3,2,1,0:T(8,128)} %get-tuple-element.391, f32[4,8,112]{2,1,0:T(8,128)S(1)} %bitcast.103, ...), kind=kLoop, calls=%fused_computation.14.clone.1 | loop fusion | flops 2935296 | bytes 15704200 | tf_op jit(solution)/shard_map/while/body/eval_jaxpr/jit(_where)/select_n | solution.py:144
  227.6 4.2 fusion.59
  235.8 6.6 %broadcast_select_fusion.8 = (f32[4,8,273,112]{3,2,1,0:T(8,128)}, f32[4,8,273,112]{3,2,1,0:T(8,128)}) fusion(f32[4,8,273,112]{3,2,1,0:T(8,128)} %get-tuple-element.393, pred[8]{0:T(512)(128)(4,1)S(1)} %broadcast_compare_fusion.2, f32[4,8,273,112]{3,2,1,0:T(8,128)} %get-tuple-element.391, f32[4,8,112]{2,1,0:T(8,128)S(1)} %bitcast.103, ...), kind=kLoop, calls=%fused_computation.14.clone.1 | loop fusion | flops 2935296 | bytes 15704200 | tf_op jit(solution)/shard_map/while/body/eval_jaxpr/jit(_where)/select_n | solution.py:144
  242.4 4.2 fusion.59
  250.6 6.6 %broadcast_select_fusion.8 = (f32[4,8,273,112]{3,2,1,0:T(8,128)}, f32[4,8,273,112]{3,2,1,0:T(8,128)}) fusion(f32[4,8,273,112]{3,2,1,0:T(8,128)} %get-tuple-element.393, pred[8]{0:T(512)(128)(4,1)S(1)} %broadcast_compare_fusion.2, f32[4,8,273,112]{3,2,1,0:T(8,128)} %get-tuple-element.391, f32[4,8,112]{2,1,0:T(8,128)S(1)} %bitcast.103, ...), kind=kLoop, calls=%fused_computation.14.clone.1 | loop fusion | flops 2935296 | bytes 15704200 | tf_op jit(solution)/shard_map/while/body/eval_jaxpr/jit(_where)/select_n | solution.py:144
  257.2 4.2 fusion.59
  265.4 6.6 %broadcast_select_fusion.8 = (f32[4,8,273,112]{3,2,1,0:T(8,128)}, f32[4,8,273,112]{3,2,1,0:T(8,128)}) fusion(f32[4,8,273,112]{3,2,1,0:T(8,128)} %get-tuple-element.393, pred[8]{0:T(512)(128)(4,1)S(1)} %broadcast_compare_fusion.2, f32[4,8,273,112]{3,2,1,0:T(8,128)} %get-tuple-element.391, f32[4,8,112]{2,1,0:T(8,128)S(1)} %bitcast.103, ...), kind=kLoop, calls=%fused_computation.14.clone.1 | loop fusion | flops 2935296 | bytes 15704200 | tf_op jit(solution)/shard_map/while/body/eval_jaxpr/jit(_where)/select_n | solution.py:144
  272.0 4.2 fusion.59
  280.2 6.6 %broadcast_select_fusion.8 = (f32[4,8,273,112]{3,2,1,0:T(8,128)}, f32[4,8,273,112]{3,2,1,0:T(8,128)}) fusion(f32[4,8,273,112]{3,2,1,0:T(8,128)} %get-tuple-element.393, pred[8]{0:T(512)(128)(4,1)S(1)} %broadcast_compare_fusion.2, f32[4,8,273,112]{3,2,1,0:T(8,128)} %get-tuple-element.391, f32[4,8,112]{2,1,0:T(8,128)S(1)} %bitcast.103, ...), kind=kLoop, calls=%fused_computation.14.clone.1 | loop fusion | flops 2935296 | bytes 15704200 | tf_op jit(solution)/shard_map/while/body/eval_jaxpr/jit(_where)/select_n | solution.py:144
  295.0 6.6 %broadcast_select_fusion.8 = (f32[4,8,273,112]{3,2,1,0:T(8,128)}, f32[4,8,273,112]{3,2,1,0:T(8,128)}) fusion(f32[4,8,273,112]{3,2,1,0:T(8,128)} %get-tuple-element.393, pred[8]{0:T(512)(128)(4,1)S(1)} %broadcast_compare_fusion.2, f32[4,8,273,112]{3,2,1,0:T(8,128)} %get-tuple-element.391, f32[4,8,112]{2,1,0:T(8,128)S(1)} %bitcast.103, ...), kind=kLoop, calls=%fused_computation.14.clone.1 | loop fusion | flops 2935296 | bytes 15704200 | tf_op jit(solution)/shard_map/while/body/eval_jaxpr/jit(_where)/select_n | solution.py:144
  301.6 4.2 fusion.59
  309.8 6.6 %broadcast_select_fusion.8 = (f32[4,8,273,112]{3,2,1,0:T(8,128)}, f32[4,8,273,112]{3,2,1,0:T(8,128)}) fusion(f32[4,8,273,112]{3,2,1,0:T(8,128)} %get-tuple-element.393, pred[8]{0:T(512)(128)(4,1)S(1)} %broadcast_compare_fusion.2, f32[4,8,273,112]{3,2,1,0:T(8,128)} %get-tuple-element.391, f32[4,8,112]{2,1,0:T(8,128)S(1)} %bitcast.103, ...), kind=kLoop, calls=%fused_computation.14.clone.1 | loop fusion | flops 2935296 | bytes 15704200 | tf_op jit(solution)/shard_map/while/body/eval_jaxpr/jit(_where)/select_n | solution.py:144
  316.4 4.2 fusion.59
  322.0 6.0 %all-to-all-start.2 = ((f32[4,16,273]{2,0,1:T(4,128)}), f32[4,16,273]{2,0,1:T(4,128)S(1)}, u32[]{:S(2)}, u32[]{:S(2)}) async-start(f32[4,16,273]{2,0,1:T(4,128)} %bitcast.24), calls=%async_computation.2 | async-start | bytes 196608 | tf_op jit(solution)/shard_map/all_to_all | solution.py:183
  328.0 5.2 copy.119
  336.3 9.9 %gather_fusion = f32[16,4,273,112]{3,1,2,0:T(4,128)} fusion(f32[4,9,273,112]{3,0,2,1:T(4,128)} %concatenate.23, s32[1024]{0:T(1024)S(1)} %pad_clamp_fusion), kind=kCustom, calls=%fused_computation | custom fusion | bytes 15654976 | tf_op jit(solution)/shard_map/gather | solution.py:100
  346.3 6.1 %all-to-all-start.1 = ((f32[4,16,273,112]{3,0,2,1:T(4,128)}), f32[4,16,273,112]{3,0,2,1:T(4,128)}, u32[]{:S(2)}, u32[]{:S(2)}) async-start(f32[4,16,273,112]{3,0,2,1:T(4,128)} %bitcast.98), calls=%async_computation.1 | async-start | bytes 17891328 | tf_op jit(solution)/shard_map/all_to_all | solution.py:182
  356.9 35.6 %all-reduce.7.cloned.1.call-done = f32[128,1792]{1,0:T(8,128)} async-done(((f32[128,1792]{1,0:T(8,128)}), f32[128,1792]{1,0:T(8,128)}) %all-reduce.7.cloned.1.call-update) | async-done | bytes 917520 | tf_op jit(solution)/shard_map/psum | solution.py:160
  404.6 30.5 %all-reduce.9.cloned.1.call-done = f32[128,1792]{1,0:T(8,128)} async-done(((f32[128,1792]{1,0:T(8,128)}), f32[128,1792]{1,0:T(8,128)}) %all-reduce.9.cloned.1.call-update) | async-done | bytes 917520 | tf_op jit(solution)/shard_map/psum | solution.py:169
  437.1 103.5 %all-to-all-done.1 = f32[4,16,273,112]{3,0,2,1:T(4,128)} async-done(((f32[4,16,273,112]{3,0,2,1:T(4,128)}), f32[4,16,273,112]{3,0,2,1:T(4,128)}, u32[]{:S(2)}, u32[]{:S(2)}) %all-to-all-start.1) | async-done | bytes 7827488 | tf_op jit(solution)/shard_map/all_to_all | solution.py:182
  540.7 4.6 broadcast_in_dim.44
  545.3 19.6 %scatter_fusion = f32[4,16,273,112]{3,0,2,1:T(4,128)} fusion(f32[4,16,273,112]{3,0,2,1:T(4,128)} %broadcast_in_dim.44, s32[16]{0:T(128)S(1)} %fusion.34, f32[16,4,273,112]{3,1,2,0:T(4,128)} %bitcast.23), kind=kCustom, calls=%fused_computation.6 | custom fusion | bytes 23482432 | tf_op jit(solution)/shard_map/scatter | solution.py:106
  564.9 7.7 %copy.120 = f32[4,16,273,112]{3,2,1,0:T(8,128)} copy(f32[4,16,273,112]{3,0,2,1:T(4,128)} %scatter_fusion) | data formatting | bytes 15654912 | tf_op jit(solution)/shard_map/scatter | solution.py:106
  572.6 14.6 %reshape.208 = f32[4,489216]{1,0:T(4,128)} reshape(f32[4,16,273,112]{3,2,1,0:T(8,128)} %copy.120) | data formatting | bytes 15654912 | tf_op jit(solution)/shard_map/reshape | solution.py:188
  (256 shorter events, 121.0 us)
Async XLA Ops:
  7.2 388.9 %copy-start = (bf16[512,1792]{1,0:T(8,128)(2,1)S(1)}, bf16[512,1792]{1,0:T(8,128)(2,1)}, u32[]{:S(2)}) copy-start(bf16[512,1792]{1,0:T(8,128)(2,1)} %param.35) | copy-start | bytes 5505028
  25.4 52.1 %all-to-all-start = ((s32[1,8,2]{2,0,1:T(1,128)}), s32[1,8,2]{2,0,1:T(1,128)S(1)}, u32[]{:S(2)}, u32[]{:S(2)}) async-start(s32[1,8,2]{2,0,1:T(1,128)} %bitcast.20), calls=%async_computation | async-start | bytes 8192 | tf_op jit(solution)/shard_map/all_to_all | solution.py:185
  58.9 10.3 %copy-start.2 = (f32[8,16,4,16]{3,0,2,1:T(8,128)S(1)}, f32[8,16,4,16]{3,0,2,1:T(8,128)}, u32[]{:S(2)}) copy-start(f32[8,16,4,16]{3,0,2,1:T(8,128)} %copy.111) | copy-start | bytes 98308
  71.5 12.2 %copy-start.3 = (bf16[16,8,4,112]{3,2,1,0:T(4,128)(2,1)S(1)}, bf16[16,8,4,112]{3,2,1,0:T(4,128)(2,1)}, u32[]{:S(2)}) copy-start(bf16[16,8,4,112]{3,2,1,0:T(4,128)(2,1)} %custom-call.9) | copy-start | bytes 344068
  71.5 12.2 %copy-start.5 = (s32[8]{0:T(128)S(1)}, s32[8]{0:T(128)}, u32[]{:S(2)}) copy-start(s32[8]{0:T(128)} %param.24) | copy-start | bytes 100
  77.5 244.6 %all-to-all-start.3 = ((f32[4,16,224]{2,0,1:T(4,128)}), f32[4,16,224]{2,0,1:T(4,128)S(1)}, u32[]{:S(2)}, u32[]{:S(2)}) async-start(f32[4,16,224]{2,0,1:T(4,128)} %bitcast.27), calls=%async_computation.3 | async-start | bytes 131072 | tf_op jit(solution)/shard_map/all_to_all | solution.py:184
  322.0 24.2 %all-to-all-start.2 = ((f32[4,16,273]{2,0,1:T(4,128)}), f32[4,16,273]{2,0,1:T(4,128)S(1)}, u32[]{:S(2)}, u32[]{:S(2)}) async-start(f32[4,16,273]{2,0,1:T(4,128)} %bitcast.24), calls=%async_computation.2 | async-start | bytes 196608 | tf_op jit(solution)/shard_map/all_to_all | solution.py:183
  346.3 9.2 %copy-start.1 = (bf16[8,16,1792]{2,1,0:T(8,128)(2,1)S(1)}, bf16[8,16,1792]{2,1,0:T(8,128)(2,1)}, u32[]{:S(2)}) copy-start(bf16[8,16,1792]{2,1,0:T(8,128)(2,1)} %param.20) | copy-start | bytes 1376260
  346.3 194.4 %all-to-all-start.1 = ((f32[4,16,273,112]{3,0,2,1:T(4,128)}), f32[4,16,273,112]{3,0,2,1:T(4,128)}, u32[]{:S(2)}, u32[]{:S(2)}) async-start(f32[4,16,273,112]{3,0,2,1:T(4,128)} %bitcast.98), calls=%async_computation.1 | async-start | bytes 17891328 | tf_op jit(solution)/shard_map/all_to_all | solution.py:182
  352.4 40.1 %all-reduce.7.cloned.1.call-start = ((), (), s32[]{:S(2)}) async-start(), calls=%async_computation.4 | async-start | bytes 1835008 | tf_op jit(solution)/shard_map/psum | solution.py:160
  352.6 41.5 %copy-start.4 = (f32[1792]{0:T(1024)S(1)}, f32[1792]{0:T(1024)}, u32[]{:S(2)}) copy-start(f32[1792]{0:T(1024)} %param.32) | copy-start | bytes 21508
  355.4 79.7 %all-reduce.9.cloned.1.call-start = ((), (), s32[]{:S(2)}) async-start(), calls=%async_computation.5 | async-start | bytes 1835008 | tf_op jit(solution)/shard_map/psum | solution.py:169
Sparse Core Ops, SparseCore 0:
  356.2 36.2 all-reduce.6
  399.5 35.5 all-reduce.8
where the time goes:
time: 605 us; the launch traced here: 594 us
  waiting for transfers between devices  170 us (28%)
  other arithmetic  145 us (24%)
  local copies, waits for them, and re-layouts  140 us (23%)
  matrix products  79.7 us (13%)
  starting transfers between devices  23.2 us (4%)
  between operations  15.5 us (3%)
  loops' own time  11.2 us (2%)
  blocking collectives  10.5 us (2%)
    select_n x16, other arithmetic, advance(): held_state = jnp.where(landed[None, :, None, None], state_sum, held_state)  106 us
    all_to_all x1, waiting for transfers between devices, shards(): lax.all_to_all(packed_lanes(chosen_state), 'req', split_axis=1, concat_ax...  104 us
    dot_general x16, matrix products, advance(): jnp.einsum('rhf,hrfd->rhd', query_step, state_sum, precision=HIGHEST)  67.3 us
    psum x1, waiting for transfers between devices, shards(): lax.psum(attn_part, 'tp')  35.6 us
    psum x1, waiting for transfers between devices, shards(): lax.psum(mlp_part, 'tp')  30.5 us
    scatter x4, local copies, waits for them, and re-layouts, settle_lanes(): return jnp.zeros((lane_block.shape[0], CAP) + lane_block.shape[2:], lane_...  29.6 us
    dynamic_slice x48, local copies, waits for them, and re-layouts, shards(): final_carry, outputs = lax.scan(advance, initial, inputs)  21.1 us
    while x16, other arithmetic  14.7 us
  transfers between devices with their start and end apart: 6, of which 3 were waited for; matrix products, arithmetic and copies ran while one was open for 52% of the time, Pallas kernels for 0%

commit v1 on v0

v1 whole, which is shorter than its diff:
```python
import functools
import math

import jax
import jax.numpy as jnp
import numpy as np
from jax import lax
from jax.experimental import pallas as pl
from jax.experimental.pallas import tpu as pltpu
from jax.sharding import PartitionSpec as P

FD = 16
DV = 112
F = 273
CAP = 16
EPSILON = 1e-05

SPAN = F * DV
LINES = 240
WIDE = 256
PHASES = 7
EXTRA = 16
BF16 = jnp.bfloat16
F32 = jnp.float32


def grid_of(count):
    narrow = 1
    for size in range(1, count + 1):
        if count % size == 0 and 2 * size * size <= count:
            narrow = size
    return count // narrow, narrow


def line_of(index):
    return (index * SPAN) // 128, (index * SPAN) % 128


@functools.lru_cache(None)
def tables():
    scale_two = 0.25 * math.sqrt(0.5)

    def feature(column, f, left, right, bias):
        if f == 0:
            bias[0, column] = bias[1, column] = bias[2, column] = 1.0
        elif f <= FD:
            left[f - 1, column] = 1.0
            bias[1, column] = 1.0
            bias[2, column] = 0.5
        elif f < F:
            left[(f - 1 - FD) // FD, column] = 1.0
            right[(f - 1 - FD) % FD, column] = 1.0
            bias[2, column] = scale_two

    def build(width, places):
        left, right = np.zeros((FD, width)), np.zeros((FD, width))
        bias = np.zeros((8, width), np.float32)
        for column, f in places:
            feature(column, f, left, right, bias)
        return np.concatenate([left, right], 1).astype(BF16), bias

    lined = [
        (part * WIDE + m, 8 * (m // PHASES) + m % PHASES + part)
        for part in range(2)
        for m in range(LINES)
    ]
    line_pick, line_bias = build(2 * WIDE, lined)
    plain_pick, plain_bias = build(384, [(f, f) for f in range(F)])
    phase_mask = np.zeros((8, WIDE))
    for k in range(PHASES):
        phase_mask[k, k::PHASES] = 1.0
    turn = np.zeros((DV, PHASES * 128))
    for k in range(PHASES):
        for lane in range(128):
            turn[(16 * k + lane) % DV, 128 * k + lane] = 1.0
    return (
        line_pick,
        line_bias,
        plain_pick,
        plain_bias,
        phase_mask.astype(BF16),
        turn.astype(BF16),
    )


def dot_nt(a, b):
    return lax.dot_general(a, b, (((1,), (1,)), ((), ())), preferred_element_type=F32)


def dot_tn(a, b):
    return lax.dot_general(a, b, (((0,), (0,)), ((), ())), preferred_element_type=F32)


def dot_nn(a, b):
    return jnp.dot(a, b, preferred_element_type=F32)


def expand(x, pick_ref, bias_ref):
    width = bias_ref.shape[1]
    both = dot_nn(x, pick_ref[...])
    left = both[:, :width] + bias_ref[0:1, :]
    right = both[:, width:] + bias_ref[1:2, :]
    return left * right * bias_ref[2:3, :]


def spread(phi, mask_ref):
    pieces = []
    for k in range(PHASES):
        chosen = mask_ref[k : k + 1, :]
        for part in range(2):
            pieces.append(phi[:, part * WIDE : (part + 1) * WIDE] * chosen)
    return jnp.concatenate(pieces, axis=0)


def pack_kernel(
    heads, shape, pair_cap, tp_size,
    owner_ref, accepted_ref, state_ref, tokens_ref, edge_ref, norm_ref, gain_ref, conv_ref,
    wq_ref, wk_ref, wv_ref, pick_ref, bias_ref, plain_pick_ref, plain_bias_ref, mask_ref, turn_ref,
    *rest,
):
    nz, ny = shape
    count = nz * ny
    pieces = rest[:count]
    q_ref, k_ref, v_ref, start_ref = rest[count : count + 4]
    flat, padded, mixed, phi, plain, turned, edges, extra, stage, state_sem, out_sem = rest[count + 4 :]
    requests = owner_ref.shape[0]
    steps = tokens_ref.shape[0] // requests
    body = heads * LINES
    lines = state_ref.shape[0]
    loads = [
        pltpu.make_async_copy(state_ref.at[:, h], flat.at[h, pl.ds(0, lines)], state_sem.at[h])
        for h in range(heads)
    ]
    for load in loads:
        load.start()

    here = lax.axis_index("req")
    tp_here = lax.axis_index("tp")
    row_here, column_here = here // ny, here % ny

    for lane in range(count * pair_cap):
        stage[lane, body : body + EXTRA, :] = jnp.zeros((EXTRA, 128), BF16)

    for r in range(requests):
        base = 24 * r
        wide = tokens_ref[steps * r : steps * (r + 1), :].astype(F32)
        mean = jnp.mean(wide * wide, axis=-1, keepdims=True)
        normed = (wide * lax.rsqrt(mean + EPSILON) * gain_ref[...]).astype(BF16).astype(F32)
        padded[base + 8 : base + 8 + steps, :] = normed
        padded[base : base + 8, :] = jnp.zeros((8, wide.shape[1]), F32)
        padded[base + 6 : base + 8, :] = edge_ref[r].astype(F32)
        convolved = conv_ref[2:3, :] * normed
        for tap in range(2):
            convolved = convolved + conv_ref[tap : tap + 1, :] * padded[base + 6 + tap : base + 6 + tap + steps, :]
        blend = normed + convolved / (1.0 + jnp.exp(-normed))
        mixed[steps * r : steps * (r + 1), :] = blend.astype(BF16)

    queries = dot_nt(mixed[...], wq_ref[...]).astype(BF16)
    keys = dot_nt(mixed[...], wk_ref[...]).astype(BF16)
    values = dot_nt(mixed[...], wv_ref[...]).astype(BF16)
    q_ref[...] = queries
    k_ref[...] = keys
    v_ref[...] = values

    for h in range(heads):
        key = keys[:, FD * h : FD * (h + 1)]
        phi[h] = expand(key, pick_ref, bias_ref)
        plain[h] = expand(key, plain_pick_ref, plain_bias_ref)
        turned[h] = dot_nn(values[:, DV * h : DV * (h + 1)], turn_ref[...]).astype(BF16)

    column_width = tokens_ref.shape[1] // tp_size
    edge_rows = lax.broadcasted_iota(jnp.int32, (2 * requests, 24 * requests), 0)
    edge_columns = lax.broadcasted_iota(jnp.int32, (2 * requests, 24 * requests), 1)
    wanted = jnp.zeros(edge_rows.shape, jnp.int32)
    for r in range(requests):
        wanted = jnp.where(edge_rows // 2 == r, 24 * r + 6 + accepted_ref[r] + edge_rows % 2, wanted)
    choose = (edge_columns == wanted).astype(F32).astype(BF16)
    for i in range(tp_size):
        @pl.when(tp_here == i)
        def _():
            window = padded[:, column_width * i : column_width * (i + 1)].astype(BF16)
            edges[:, :column_width] = dot_nn(choose, window)

    lane_ids = lax.broadcasted_iota(jnp.int32, (LINES, 128), 1)
    one_line = lax.broadcasted_iota(jnp.int32, (EXTRA, 128), 1)
    one_row = lax.broadcasted_iota(jnp.int32, (EXTRA, 128), 0)
    step_ids = lax.broadcasted_iota(jnp.int32, (steps, 1), 0)
    edge_lines = -(-column_width // 128)
    for load in loads:
        load.wait()
    for r in range(requests):
        owner = owner_ref[r]
        rank = jnp.int32(0)
        for earlier in range(r):
            rank = rank + (owner_ref[earlier] == owner).astype(jnp.int32)
        far = lax.rem(owner // ny - row_here + nz, nz) * ny + lax.rem(owner % ny - column_here + ny, ny)
        lane = far * pair_cap + rank
        taken = (step_ids < accepted_ref[r]).astype(F32)
        first, shift = line_of(r)
        extra[...] = jnp.zeros((EXTRA, 128), F32)
        for h in range(heads):
            rows = slice(steps * r, steps * (r + 1))
            spread_keys = spread((phi[h, rows, :] * taken).astype(BF16), mask_ref)
            value_rows = turned[h, rows, :]
            parts = []
            for k in range(PHASES):
                block = value_rows[:, 128 * k : 128 * (k + 1)]
                early = one_line < DV - 16 * k
                zero = jnp.zeros((steps, 128), BF16)
                parts.append(jnp.where(early, block, zero))
                parts.append(jnp.where(early, zero, block))
            added = dot_tn(spread_keys, jnp.concatenate(parts, axis=0))[:LINES]
            start = flat[h, first : first + LINES, :]
            if shift:
                following = flat[h, first + 1 : first + 1 + LINES, :]
                start = pltpu.roll(jnp.where(lane_ids >= shift, start, following), 128 - shift, 1)
            start_ref[r, h] = start.astype(BF16)
            kept = start + added
            sums = jnp.sum(plain[h, rows, :] * taken, axis=0, keepdims=True)[:, :F] + norm_ref[h, r : r + 1, :]
            extra[2 * h : 2 * h + 1, :] = sums[:, :128]
            extra[2 * h + 1 : 2 * h + 2, :] = sums[:, 128:256]
            tail = jnp.concatenate([sums[:, 256:], jnp.zeros((1, 128 - (F - 256)), F32)], axis=1)
            stage[lane, h * LINES : (h + 1) * LINES - 16, :] = kept[: LINES - 16].astype(BF16)
            stage[lane, (h + 1) * LINES - 16 : (h + 1) * LINES, :] = jnp.where(
                one_row == 15, tail, kept[LINES - 16 :]
            ).astype(BF16)
        for j in range(2):
            for c in range(edge_lines):
                end = min(column_width, 128 * (c + 1))
                line = 2 * heads + edge_lines * j + c
                extra[line : line + 1, : end - 128 * c] = edges[2 * r + j : 2 * r + j + 1, 128 * c : end]
        mark = (one_row == EXTRA - 1) & (one_line == 127)
        stage[lane, body : body + EXTRA, :] = jnp.where(mark, 1.0, extra[...]).astype(BF16)
    sends = [
        pltpu.make_async_copy(stage.at[pl.ds(pair_cap * i, pair_cap)], pieces[i], out_sem.at[i])
        for i in range(count)
    ]
    for send in sends:
        send.start()
    for send in sends:
        send.wait()


def attend_kernel(
    heads, core_bit,
    q_ref, k_ref, v_ref, start_ref, norm_ref, wo_ref, pick_ref, bias_ref, plain_pick_ref, plain_bias_ref, mask_ref,
    keep_ref, send_ref,
    attended, part,
):
    requests = start_ref.shape[0]
    rows_all = q_ref.shape[0]
    steps = rows_all // requests
    row_ids = lax.broadcasted_iota(jnp.int32, (rows_all, rows_all), 0)
    column_ids = lax.broadcasted_iota(jnp.int32, (rows_all, rows_all), 1)
    allowed = (row_ids // steps == column_ids // steps) & (row_ids >= column_ids)
    lane_ids = lax.broadcasted_iota(jnp.int32, (steps, 128), 1)
    for h in range(heads):
        query = q_ref[:, FD * h : FD * (h + 1)]
        key = k_ref[:, FD * h : FD * (h + 1)]
        value = v_ref[:, DV * h : DV * (h + 1)]
        phi = expand(query, pick_ref, bias_ref).astype(BF16)
        plain = expand(query, plain_pick_ref, plain_bias_ref)
        inner = dot_nt(query, key) * 0.25
        scores = jnp.where(allowed, 1.0 + inner + 0.5 * inner * inner, 0.0)
        below = jnp.sum(scores, axis=-1, keepdims=True)
        within = dot_nn(scores.astype(BF16), value)
        for r in range(requests):
            rows = slice(steps * r, steps * (r + 1))
            spread_query = spread(phi[rows], mask_ref)[:, :LINES]
            lined = dot_nn(spread_query, start_ref[r, h])
            total = jnp.zeros((steps, 128), F32)
            for j in range(PHASES + 1):
                block = jnp.zeros((steps, 128), F32)
                if j < PHASES:
                    at = steps * (2 * j)
                    block = jnp.where(lane_ids < DV - 16 * j, lined[at : at + steps], 0.0)
                if j > 0:
                    at = steps * (2 * (j - 1) + 1)
                    block = jnp.where(lane_ids >= DV - 16 * (j - 1), lined[at : at + steps], block)
                total = total + (pltpu.roll(block, 16 * j, 1) if 0 < j < 8 else block)
            beneath = below[rows] + jnp.sum(plain[rows, :F] * norm_ref[h, r : r + 1, :], axis=-1, keepdims=True)
            attended[h, rows, :] = ((total[:, :DV] + within[rows]) / beneath).astype(BF16)
    out = dot_nn(attended[0], wo_ref[0:DV, :])
    for h in range(1, heads):
        out = out + dot_nn(attended[h], wo_ref[DV * h : DV * (h + 1), :])
    part[...] = out.astype(BF16)
    half = rows_all // 2
    mine = lax.rem(lax.axis_index("tp"), 2)
    keep_ref[...] = part[pl.ds(pl.multiple_of(mine * half, half), half), :]
    send_ref[...] = part[pl.ds(pl.multiple_of((1 - mine) * half, half), half), :]


def joined(own_ref, other_ref, scratch):
    half = own_ref.shape[0]
    mine = lax.rem(lax.axis_index("tp"), 2)
    scratch[pl.ds(pl.multiple_of(mine * half, half), half), :] = own_ref[...]
    scratch[pl.ds(pl.multiple_of((1 - mine) * half, half), half), :] = other_ref[...]


def mlp_kernel(
    tokens_ref, own_ref, other_ref, gain_ref, wg_ref, wu_ref, wd_ref,
    residual_ref, keep_ref, send_ref,
    part,
):
    joined(own_ref, other_ref, part)
    residual = tokens_ref[...].astype(F32) + part[...].astype(F32)
    residual_ref[...] = residual
    mean = jnp.mean(residual * residual, axis=-1, keepdims=True)
    second = (residual * lax.rsqrt(mean + EPSILON) * gain_ref[...]).astype(BF16)
    gate = dot_nn(second, wg_ref[...])
    up = dot_nn(second, wu_ref[...])
    hidden = (gate / (1.0 + jnp.exp(-gate)) * up).astype(BF16)
    part[...] = dot_nn(hidden, wd_ref[...]).astype(BF16)
    half = own_ref.shape[0]
    mine = lax.rem(lax.axis_index("tp"), 2)
    keep_ref[...] = part[pl.ds(pl.multiple_of(mine * half, half), half), :]
    send_ref[...] = part[pl.ds(pl.multiple_of((1 - mine) * half, half), half), :]


def close_kernel(residual_ref, own_ref, other_ref, out_ref, part):
    joined(own_ref, other_ref, part)
    out_ref[...] = (residual_ref[...] + part[...].astype(F32)).astype(BF16)


def settle_kernel(heads, shape, pair_cap, plan, *rest):
    nz, ny = shape
    count = nz * ny
    lanes = count * pair_cap
    inputs = rest[: len(plan)]
    state_ref, norm_ref, edge_ref, stage, flat, shifted, table, in_sem, out_sem = rest[len(plan) :]
    body = heads * LINES
    here = lax.axis_index("req")
    row_here, column_here = here // ny, here % ny
    loads = []
    for i, parts in enumerate(plan):
        for place, (dz, dy, first, size) in enumerate(parts):
            source = lax.rem(row_here - dz + nz, nz) * ny + lax.rem(column_here - dy + ny, ny)
            at = sum(p[3] for p in parts[:place])
            loads.append(
                pltpu.make_async_copy(
                    inputs[i].at[pl.ds(at, size)],
                    stage.at[pl.ds(source * pair_cap + first, size)],
                    in_sem.at[len(loads)],
                )
            )
    for load in loads:
        load.start()
    norm_ref[...] = jnp.zeros(norm_ref.shape, F32)
    edge_ref[...] = jnp.zeros(edge_ref.shape, BF16)
    for load in loads:
        load.wait()
    one_row = lax.broadcasted_iota(jnp.int32, (EXTRA, 128), 0)
    one_line = lax.broadcasted_iota(jnp.int32, (EXTRA, 128), 1)
    mark = (one_row == EXTRA - 1) & (one_line == 127)
    filled = jnp.int32(0)
    for lane in range(lanes):
        block = jnp.where(mark, stage[lane, body : body + EXTRA, :].astype(F32), 0.0)
        live = jnp.sum(block).astype(jnp.int32)
        table[filled] = lane
        filled = filled + live

    total = state_ref.shape[0]
    width = edge_ref.shape[2]
    edge_lines = -(-width // 128)
    lane_ids = lax.broadcasted_iota(jnp.int32, (LINES, 128), 1)
    head_ids = lax.broadcasted_iota(jnp.int32, (8, 128), 1)
    head_rows = lax.broadcasted_iota(jnp.int32, (8, 128), 0)
    stores = []
    done = 0
    for s in range(CAP):
        first, shift = line_of(s)
        last = -(-((s + 1) * SPAN) // 128)
        span = last - first

        @pl.when(s < filled)
        def _():
            lane = table[s]
            extra = stage[lane, body : body + EXTRA, :].astype(F32)
            pairs = [[], []]
            for j in range(2):
                for c in range(edge_lines):
                    end = min(width, 128 * (c + 1))
                    line = 2 * heads + edge_lines * j + c
                    pairs[j].append(extra[line : line + 1, : end - 128 * c])
            edge_ref[s] = jnp.concatenate(
                [jnp.concatenate(pairs[j], axis=1) for j in range(2)], axis=0
            ).astype(BF16)
            for h in range(heads):
                rows = stage[lane, h * LINES : (h + 1) * LINES, :].astype(F32)
                norm_ref[h, s : s + 1, :] = jnp.concatenate(
                    [
                        extra[2 * h : 2 * h + 1, :],
                        extra[2 * h + 1 : 2 * h + 2, :],
                        rows[LINES - 1 : LINES, : F - 256],
                    ],
                    axis=1,
                )
                if shift:
                    shifted[h, 8 : 8 + LINES, :] = rows
                    before = shifted[h, 7 : 7 + LINES, :]
                    rows = pltpu.roll(jnp.where(lane_ids < 128 - shift, rows, before), shift, 1)
                    old = flat[h, first : first + 1, :]
                    flat[h, first + 1 : last, :] = rows[1:span]
                    flat[h, first : first + 1, :] = jnp.where(head_ids[:1] < shift, old, rows[:1])
                else:
                    flat[h, first:last, :] = rows[:span]

        @pl.when(s >= filled)
        def _():
            for h in range(heads):
                if shift:
                    old = flat[h, first : first + 1, :]
                    flat[h, first + 1 : last, :] = jnp.zeros((span - 1, 128), F32)
                    flat[h, first : first + 1, :] = jnp.where(head_ids[:1] < shift, old, 0.0)
                else:
                    flat[h, first:last, :] = jnp.zeros((span, 128), F32)

        until = total if s == CAP - 1 else ((s + 1) * SPAN // 128) // 8 * 8
        for h in range(heads):
            store = pltpu.make_async_copy(
                flat.at[h, pl.ds(done, until - done)],
                state_ref.at[pl.ds(done, until - done), h],
                out_sem.at[s, h],
            )
            store.start()
            stores.append(store)
        done = until
    for store in stores:
        store.wait()


def shards(
    tokens, conv_edge, state_start, norm_start, accepted, owner, attn_gain, conv_weight,
    w_query, w_key, w_value, w_out, mlp_gain, w_gate, w_up, w_down,
):
    requests, steps, width = tokens.shape
    count = lax.axis_size("req")
    tp_size = lax.axis_size("tp")
    nz, ny = shape = grid_of(count)
    pair_cap = (CAP + count - 1) // count
    heads = w_query.shape[1] // FD
    rows_all = requests * steps
    lines = state_start.shape[1] // 128
    payload = heads * LINES + EXTRA
    column_width = width // tp_size
    line_pick, line_bias, plain_pick, plain_bias, phase_mask, turn = (jnp.asarray(t) for t in tables())

    vmem = pl.BlockSpec(memory_space=pltpu.VMEM)
    smem = pl.BlockSpec(memory_space=pltpu.SMEM)
    anywhere = pl.BlockSpec(memory_space=pl.ANY)
    limit = pltpu.CompilerParams(vmem_limit_bytes=48 * 2**20)

    flat_tokens = tokens.reshape(rows_all, width)
    lined_state = jnp.swapaxes(state_start.reshape(heads, lines, 128), 0, 1)
    piece_shape = jax.ShapeDtypeStruct((pair_cap, payload, 128), BF16)
    outs = pl.pallas_call(
        functools.partial(pack_kernel, heads, shape, pair_cap, tp_size),
        out_shape=[piece_shape] * count
        + [
            jax.ShapeDtypeStruct((rows_all, heads * FD), BF16),
            jax.ShapeDtypeStruct((rows_all, heads * FD), BF16),
            jax.ShapeDtypeStruct((rows_all, heads * DV), BF16),
            jax.ShapeDtypeStruct((requests, heads, LINES, 128), BF16),
        ],
        in_specs=[smem, smem, anywhere] + [vmem] * 14,
        out_specs=[anywhere] * count + [vmem] * 4,
        scratch_shapes=[
            pltpu.VMEM((heads, (lines + 1) // 8 * 8 + 8, 128), F32),
            pltpu.VMEM((requests * 24, width), F32),
            pltpu.VMEM((rows_all, width), BF16),
            pltpu.VMEM((heads, rows_all, 2 * WIDE), F32),
            pltpu.VMEM((heads, rows_all, 384), F32),
            pltpu.VMEM((heads, rows_all, PHASES * 128), BF16),
            pltpu.VMEM((2 * requests, -(-column_width // 128) * 128), F32),
            pltpu.VMEM((EXTRA, 128), F32),
            pltpu.VMEM((count * pair_cap, payload, 128), BF16),
            pltpu.SemaphoreType.DMA((heads,)),
            pltpu.SemaphoreType.DMA((count,)),
        ],
        compiler_params=limit,
        name="pack",
    )(
        owner, accepted, lined_state, flat_tokens, conv_edge, norm_start, attn_gain[None, :], conv_weight,
        w_query.T, w_key.T, w_value, line_pick, line_bias, plain_pick, plain_bias, phase_mask, turn,
    )
    pieces, (queries, keys, values, start_rows) = outs[:count], outs[count:]

    def moved(x, dz, dy):
        route = [
            (z * ny + y, (z + dz) % nz * ny + (y + dy) % ny) for z in range(nz) for y in range(ny)
        ]
        return lax.ppermute(x, "req", route)

    arrived, plan = [pieces[0]], [((0, 0, 0, pair_cap),)]
    for dz in range(nz):
        for dy in range(ny):
            if dz or dy:
                arrived.append(moved(pieces[dz * ny + dy], dz, dy))
                plan.append(((dz, dy, 0, pair_cap),))

    half_shape = jax.ShapeDtypeStruct((rows_all // 2, width), BF16)

    def summed(keep, send):
        swap = [(i, i ^ 1) for i in range(tp_size)]
        total = keep.astype(F32) + lax.ppermute(send, "tp", swap).astype(F32)
        step = 2
        while step < tp_size:
            rounded = total.astype(BF16)
            across = lax.ppermute(rounded, "tp", [(i, i ^ step) for i in range(tp_size)])
            total = rounded.astype(F32) + across.astype(F32)
            step *= 2
        rounded = total.astype(BF16)
        return rounded, lax.ppermute(rounded, "tp", swap)

    keep, send = pl.pallas_call(
        functools.partial(attend_kernel, heads, 0),
        out_shape=[half_shape] * 2,
        in_specs=[vmem] * 11,
        out_specs=[vmem] * 2,
        scratch_shapes=[
            pltpu.VMEM((heads, rows_all, DV), BF16),
            pltpu.VMEM((rows_all, width), BF16),
        ],
        compiler_params=limit,
        name="attend",
    )(
        queries, keys, values, start_rows, norm_start, w_out,
        line_pick, line_bias, plain_pick, plain_bias, phase_mask,
    )
    own, other = summed(keep, send)
    residual, keep, send = pl.pallas_call(
        mlp_kernel,
        out_shape=[jax.ShapeDtypeStruct((rows_all, width), F32)] + [half_shape] * 2,
        in_specs=[vmem] * 7,
        out_specs=[vmem] * 3,
        scratch_shapes=[pltpu.VMEM((rows_all, width), BF16)],
        compiler_params=limit,
        name="mlp",
    )(flat_tokens, own, other, mlp_gain[None, :], w_gate, w_up, w_down)
    own, other = summed(keep, send)
    hidden_out = pl.pallas_call(
        close_kernel,
        out_shape=jax.ShapeDtypeStruct((rows_all, width), BF16),
        in_specs=[vmem] * 3,
        out_specs=vmem,
        scratch_shapes=[pltpu.VMEM((rows_all, width), BF16)],
        compiler_params=limit,
        name="close",
    )(residual, own, other)

    out_lines = CAP * SPAN // 128
    kept_state, kept_norm, kept_edge = pl.pallas_call(
        functools.partial(settle_kernel, heads, shape, pair_cap, tuple(plan)),
        out_shape=[
            jax.ShapeDtypeStruct((out_lines, heads, 128), F32),
            jax.ShapeDtypeStruct((heads, CAP, F), F32),
            jax.ShapeDtypeStruct((CAP, 2, column_width), BF16),
        ],
        in_specs=[anywhere] * len(arrived),
        out_specs=[anywhere, vmem, vmem],
        scratch_shapes=[
            pltpu.VMEM((count * pair_cap, payload, 128), BF16),
            pltpu.VMEM((heads, out_lines, 128), F32),
            pltpu.VMEM((heads, LINES + 16, 128), F32),
            pltpu.SMEM((count * pair_cap + 1,), jnp.int32),
            pltpu.SemaphoreType.DMA((sum(len(p) for p in plan),)),
            pltpu.SemaphoreType.DMA((CAP, heads)),
        ],
        compiler_params=limit,
        name="settle",
    )(*arrived)
    return (
        hidden_out.reshape(requests, steps, width),
        jnp.swapaxes(kept_state, 0, 1).reshape(heads, out_lines * 128),
        kept_norm,
        kept_edge,
    )


def solution(mesh):
    placed = (
        P("req", None, None),
        P("req", None, None),
        P("tp", "req"),
        P("tp", "req", None),
        P("req"),
        P("req"),
        P(),
        P(),
        P(None, "tp"),
        P(None, "tp"),
        P("tp", None),
        P("tp", None),
        P(),
        P(None, "tp"),
        P(None, "tp"),
        P("tp", None),
    )
    return jax.shard_map(
        shards,
        mesh=mesh,
        in_specs=placed,
        out_specs=(
            P("req", None, None),
            P("tp", "req"),
            P("tp", "req", None),
            P("req", None, "tp"),
        ),
        check_vma=False,
    )
```

time: 605 us -> 143 us (0.24); the launches traced: 594 us -> 142 us
  other arithmetic: 145 us -> 0.22 us
  local copies, waits for them, and re-layouts: 140 us -> 13.4 us
  waiting for transfers between devices: 170 us -> 86.1 us
  matrix products: 79.7 us -> 0 us
  Pallas kernels: 0 us -> 25.7 us
  between operations: 15.5 us -> 0.83 us
  loops' own time: 11.2 us -> 0 us
  blocking collectives: 10.5 us -> 0 us
  starting transfers between devices: 23.2 us -> 15.4 us
    select_n x42 -> x0, other arithmetic: 107 us -> none  [the longest x16 106 us: advance(): held_state = jnp.where(landed[None, :, None, None], state_sum, held_state)]
    all_to_all x4 -> x0, waiting for transfers between devices: 104 us -> none  [the longest x1 104 us: shards(): lax.all_to_all(packed_lanes(chosen_state), 'req', split_axis=1, concat_ax...]
    ppermute x0 -> x13, waiting for transfers between devices: none -> 86.1 us  [the longest x7 77.1 us: moved(): return lax.ppermute(x, 'req', route)]
    dot_general x22 -> x0, matrix products: 79.7 us -> none  [the longest x16 67.3 us: advance(): jnp.einsum('rhf,hrfd->rhd', query_step, state_sum, precision=HIGHEST)]
    psum x2 -> x0, waiting for transfers between devices: 66.1 us -> none  [the longest x1 35.6 us: shards(): lax.psum(attn_part, 'tp')]
    scatter x6 -> x0, local copies, waits for them, and re-layouts: 31 us -> none  [the longest x4 29.6 us: settle_lanes(): return jnp.zeros((lane_block.shape[0], CAP) + lane_block.shape[2:], lane_...]
    pallas_call x0 -> x5, Pallas kernels: none -> 25.7 us  [the longest x1 12 us: shards(): pl.pallas_call(functools.partial(pack_kernel, heads, shape, pair_cap, tp_...]
    reshape x5 -> x0, local copies, waits for them, and re-layouts: 23.4 us -> none  [the longest x1 14.6 us: shards(): settle_lanes(arrived_state, arrived_slot).reshape(local_heads, CAP * F * DV)]
  transfers between devices with their start and end apart: 6 -> 13, of which waited for: 3 -> 8; matrix products, arithmetic and copies ran while one was open for 52% -> 0% of each run, Pallas kernels for 0% -> 5%
where the time goes in v1:
time: 143 us; the launch traced here: 142 us
  waiting for transfers between devices  86.1 us (60%)
  Pallas kernels  25.7 us (18%)
  starting transfers between devices  15.4 us (11%)
  local copies, waits for them, and re-layouts  13.4 us (9%)
    ppermute x7, waiting for transfers between devices, moved(): return lax.ppermute(x, 'req', route)  77.1 us
    unnamed x52, local copies, waits for them, and re-layouts  12.7 us
    pallas_call x1, Pallas kernels, shards(): pl.pallas_call(functools.partial(pack_kernel, heads, shape, pair_cap, tp_...  12 us
    ppermute x7, starting transfers between devices, moved(): return lax.ppermute(x, 'req', route)  12 us
    pallas_call x1, Pallas kernels, shards(): pl.pallas_call(functools.partial(settle_kernel, heads, shape, pair_cap, t...  7.21 us
    ppermute x2, waiting for transfers between devices, summed(): lax.ppermute(rounded, 'tp', [(i, i ^ step) for i in range(tp_size)])  6.16 us
    ppermute x2, starting transfers between devices, summed(): lax.ppermute(rounded, 'tp', [(i, i ^ step) for i in range(tp_size)])  3.11 us
  transfers between devices with their start and end apart: 13, of which 8 were waited for; matrix products, arithmetic and copies ran while one was open for 0% of the time, Pallas kernels for 5%

profile of v1, /device:TPU:8, one launch (start us, length us, event | category | flops | bytes accessed | tf_op | source)
XLA Modules:
  0.0 141.7 jit_solution(2650585273808715346)
XLA Ops:
  0.6 0.7 broadcast_in_dim.6.gain_ref
  1.3 1.0 copy-done.1
  2.4 0.9 copy-done.6
  3.3 0.9 copy-done.7
  4.2 0.9 copy-done.8
  5.2 0.8 copy-done.9
  6.0 0.8 copy-done.11
  6.7 0.7 copy-done.13
  7.5 0.7 copy-done.15
  8.2 0.8 copy-done.17
  9.0 0.7 copy-done.18
  9.7 0.7 copy-done.20
  10.4 0.7 copy-done.21
  11.1 0.7 copy-done.23
  11.8 0.7 copy-done.24
  12.5 0.0 copy-start.16
  12.5 0.0 copy-start.19
  12.5 0.0 copy-start.22
  12.5 12.0 %pack.1 = (bf16[2,976,128]{2,1,0:T(8,128)(2,1)S(1)}, bf16[2,976,128]{2,1,0:T(8,128)(2,1)S(1)}, bf16[2,976,128]{2,1,0:T(8,128)(2,1)S(1)}, bf16[2,976,128]{2,1,0:T...) custom-call(s32[8]{0:T(128)S(1)} %copy-done.23, ...), custom_call_target="tpu_custom_call" | custom-call | tf_op jit(solution)/shard_map/pack/pallas_call | solution.py:456
  24.6 1.5 %copy-done = bf16[8,4,240,128]{3,2,1,0:T(8,128)(2,1)S(1)} copy-done((bf16[8,4,240,128]{3,2,1,0:T(8,128)(2,1)S(1)}, bf16[8,4,240,128]{3,2,1,0:T(8,128)(2,1)}, u32[]{:S(2)}) %copy-start) | copy-done | bytes 1966104
  26.2 2.6 %attend.1 = (bf16[64,1792]{1,0:T(8,128)(2,1)S(1)}, bf16[64,1792]{1,0:T(8,128)(2,1)S(1)}) custom-call(bf16[128,64]{1,0:T(8,128)(2,1)S(1)} %get-tuple-element.24.q_ref, bf16[128,64]{1,0:T(8,128)(2,1)S(1)} %get-tuple-element.25.k_ref, bf16[128,448]{1,0:T(8,128)(2,1)S(1)} %get-tuple-element.26.v_ref, bf16[8,4,240,128]{3,2,1,0:T(8,128)(2,1)S(1)} %copy-done, ...), custom_call_target="tpu_custom_call" | custom-call | tf_op jit(solution)/shard_map/attend/pallas_call | solution.py:515
  28.8 0.1 collective-permute-start
  28.9 1.5 %collective-permute-done = bf16[64,1792]{1,0:T(8,128)(2,1)S(1)} collective-permute-done((bf16[64,1792]{1,0:T(8,128)(2,1)S(1)}, bf16[64,1792]{1,0:T(8,128)(2,1)S(1)}, u32[]{:S(2)}, u32[]{:S(2)}) %collective-permute-start) | collective-permute-done | bytes 229408 | tf_op jit(solution)/shard_map/ppermute | solution.py:505
  30.4 0.1 add_convert_fusion.3
  30.4 1.6 %collective-permute-start.1 = (bf16[64,1792]{1,0:T(8,128)(2,1)S(1)}, bf16[64,1792]{1,0:T(8,128)(2,1)S(1)}, u32[]{:S(2)}, u32[]{:S(2)}) collective-permute-start(bf16[64,1792]{1,0:T(8,128)(2,1)S(1)} %add_convert_fusion.3), channel_id=1, source_target_pairs={{0,2},{1,3},{2,0},{3,1},{4,6},{5,7},{6,4},{7,5},{8,10},{9,11},{10,... | collective-permute-start | bytes 688136 | tf_op jit(solution)/shard_map/ppermute | solution.py:509
  32.0 6.2 %collective-permute-done.1 = bf16[64,1792]{1,0:T(8,128)(2,1)S(1)} collective-permute-done((bf16[64,1792]{1,0:T(8,128)(2,1)S(1)}, bf16[64,1792]{1,0:T(8,128)(2,1)S(1)}, u32[]{:S(2)}, u32[]{:S(2)}) %collective-permute-start.1) | collective-permute-done | bytes 229408 | tf_op jit(solution)/shard_map/ppermute | solution.py:509
  38.1 0.1 add_convert_fusion.2.own_ref
  38.2 0.1 collective-permute-start.2
  38.3 1.5 %collective-permute-done.2.other_ref = bf16[64,1792]{1,0:T(8,128)(2,1)S(1)} collective-permute-done((bf16[64,1792]{1,0:T(8,128)(2,1)S(1)}, bf16[64,1792]{1,0:T(8,128)(2,1)S(1)}, u32[]{:S(2)}, u32[]{:S(2)}) %collective-permute-start.2) | collective-permute-done | bytes 229408 | tf_op jit(solution)/shard_map/ppermute | solution.py:513
  39.8 2.8 %mlp.1 = (f32[128,1792]{1,0:T(8,128)S(1)}, bf16[64,1792]{1,0:T(8,128)(2,1)S(1)}, bf16[64,1792]{1,0:T(8,128)(2,1)S(1)}) custom-call(bf16[128,1792]{1,0:T(8,128)(2,1)S(1)} %bitcast.11, bf16[64,1792]{1,0:T(8,128)(2,1)S(1)} %add_convert_fusion.2.own_ref, bf16[64,1792]{1,0:T(8,128)(2,1)S(1)} %collective-permute-done.2.other_ref, ...), custom_call_target="tpu_custom_call" | custom-call | tf_op jit(solution)/shard_map/mlp/pallas_call | solution.py:531
  42.6 0.2 collective-permute-start.3
  42.8 1.5 %collective-permute-start.6 = (bf16[2,976,128]{2,1,0:T(8,128)(2,1)S(1)}, bf16[2,976,128]{2,1,0:T(8,128)(2,1)S(1)}, u32[]{:S(2)}, u32[]{:S(2)}) collective-permute-start(bf16[2,976,128]{2,1,0:T(8,128)(2,1)S(1)} %get-tuple-element.34), channel_id=1, source_target_pairs={{0,4},{4,0},{8,12},{12,8},{16,20},{20,16},{24,28},{28,24},{1,5},{5... | collective-permute-start | bytes 1499144 | tf_op jit(solution)/shard_map/ppermute | solution.py:492
  44.3 1.6 %collective-permute-start.7 = (bf16[2,976,128]{2,1,0:T(8,128)(2,1)S(1)}, bf16[2,976,128]{2,1,0:T(8,128)(2,1)S(1)}, u32[]{:S(2)}, u32[]{:S(2)}) collective-permute-start(bf16[2,976,128]{2,1,0:T(8,128)(2,1)S(1)} %get-tuple-element.35), channel_id=1, source_target_pairs={{0,8},{4,12},{8,16},{12,20},{16,24},{20,28},{24,0},{28,4},{1,9},{5... | collective-permute-start | bytes 1499144 | tf_op jit(solution)/shard_map/ppermute | solution.py:492
  45.9 0.1 add_convert_fusion.1
  45.9 1.6 %collective-permute-start.4 = (bf16[64,1792]{1,0:T(8,128)(2,1)S(1)}, bf16[64,1792]{1,0:T(8,128)(2,1)S(1)}, u32[]{:S(2)}, u32[]{:S(2)}) collective-permute-start(bf16[64,1792]{1,0:T(8,128)(2,1)S(1)} %add_convert_fusion.1), channel_id=1, source_target_pairs={{0,2},{1,3},{2,0},{3,1},{4,6},{5,7},{6,4},{7,5},{8,10},{9,11},{10,... | collective-permute-start | bytes 688136 | tf_op jit(solution)/shard_map/ppermute | solution.py:509
  47.5 1.5 %collective-permute-start.8 = (bf16[2,976,128]{2,1,0:T(8,128)(2,1)S(1)}, bf16[2,976,128]{2,1,0:T(8,128)(2,1)S(1)}, u32[]{:S(2)}, u32[]{:S(2)}) collective-permute-start(bf16[2,976,128]{2,1,0:T(8,128)(2,1)S(1)} %get-tuple-element.36), channel_id=1, source_target_pairs={{0,12},{4,8},{8,20},{12,16},{16,28},{20,24},{24,4},{28,0},{1,13},{... | collective-permute-start | bytes 1499144 | tf_op jit(solution)/shard_map/ppermute | solution.py:492
  49.0 1.2 collective-permute-start.9
  50.2 6.2 %collective-permute-done.6.rest_1_ = bf16[2,976,128]{2,1,0:T(8,128)(2,1)S(1)} collective-permute-done((bf16[2,976,128]{2,1,0:T(8,128)(2,1)S(1)}, bf16[2,976,128]{2,1,0:T(8,128)(2,1)S(1)}, u32[]{:S(2)}, u32[]{:S(2)}) %collective-permute-start.6) | collective-permute-done | bytes 499744 | tf_op jit(solution)/shard_map/ppermute | solution.py:492
  56.4 3.5 %collective-permute-start.10 = (bf16[2,976,128]{2,1,0:T(8,128)(2,1)S(1)}, bf16[2,976,128]{2,1,0:T(8,128)(2,1)S(1)}, u32[]{:S(2)}, u32[]{:S(2)}) collective-permute-start(bf16[2,976,128]{2,1,0:T(8,128)(2,1)S(1)} %get-tuple-element.38), channel_id=1, source_target_pairs={{0,20},{4,16},{8,28},{12,24},{16,4},{20,0},{24,12},{28,8},{1,21},{... | collective-permute-start | bytes 1499144 | tf_op jit(solution)/shard_map/ppermute | solution.py:492
  60.0 0.9 collective-permute-start.11
  60.9 1.7 %collective-permute-start.12 = (bf16[2,976,128]{2,1,0:T(8,128)(2,1)S(1)}, bf16[2,976,128]{2,1,0:T(8,128)(2,1)S(1)}, u32[]{:S(2)}, u32[]{:S(2)}) collective-permute-start(bf16[2,976,128]{2,1,0:T(8,128)(2,1)S(1)} %get-tuple-element.40), channel_id=1, source_target_pairs={{0,28},{4,24},{8,4},{12,0},{16,12},{20,8},{24,20},{28,16},{1,29},{... | collective-permute-start | bytes 1499144 | tf_op jit(solution)/shard_map/ppermute | solution.py:492
  62.5 0.1 add_convert_fusion.own_ref
  62.6 48.6 %collective-permute-done.8.rest_3_ = bf16[2,976,128]{2,1,0:T(8,128)(2,1)S(1)} collective-permute-done((bf16[2,976,128]{2,1,0:T(8,128)(2,1)S(1)}, bf16[2,976,128]{2,1,0:T(8,128)(2,1)S(1)}, u32[]{:S(2)}, u32[]{:S(2)}) %collective-permute-start.8) | collective-permute-done | bytes 499744 | tf_op jit(solution)/shard_map/ppermute | solution.py:492
  111.2 10.7 %collective-permute-done.9.rest_4_ = bf16[2,976,128]{2,1,0:T(8,128)(2,1)S(1)} collective-permute-done((bf16[2,976,128]{2,1,0:T(8,128)(2,1)S(1)}, bf16[2,976,128]{2,1,0:T(8,128)(2,1)S(1)}, u32[]{:S(2)}, u32[]{:S(2)}) %collective-permute-start.9) | collective-permute-done | bytes 499744 | tf_op jit(solution)/shard_map/ppermute | solution.py:492
  121.9 9.8 %collective-permute-done.10.rest_5_ = bf16[2,976,128]{2,1,0:T(8,128)(2,1)S(1)} collective-permute-done((bf16[2,976,128]{2,1,0:T(8,128)(2,1)S(1)}, bf16[2,976,128]{2,1,0:T(8,128)(2,1)S(1)}, u32[]{:S(2)}, u32[]{:S(2)}) %collective-permute-start.10) | collective-permute-done | bytes 499744 | tf_op jit(solution)/shard_map/ppermute | solution.py:492
  131.7 1.7 %collective-permute-done.12.rest_7_ = bf16[2,976,128]{2,1,0:T(8,128)(2,1)S(1)} collective-permute-done((bf16[2,976,128]{2,1,0:T(8,128)(2,1)S(1)}, bf16[2,976,128]{2,1,0:T(8,128)(2,1)S(1)}, u32[]{:S(2)}, u32[]{:S(2)}) %collective-permute-start.12) | collective-permute-done | bytes 499744 | tf_op jit(solution)/shard_map/ppermute | solution.py:492
  133.5 7.2 %settle.1 = (f32[3822,4,128]{2,1,0:T(4,128)}, f32[4,16,273]{2,1,0:T(8,128)}, bf16[16,2,448]{2,1,0:T(2,128)(2,1)}) custom-call(bf16[2,976,128]{2,1,0:T(8,128)(2,1)S(1)} %get-tuple-element.33.rest_0_, bf16[2,976,128]{2,1,0:T(8,128)(2,1)S(1)} %collective-permute-done.6.rest_1_, bf16[2,976,128]{2,1,0:T(8,128)(2,1)S(1)} %collective-permute-done.7.rest_2_, ...), custom_call_target="tpu_custom_call" | custom-call | tf_op jit(solution)/shard_map/settle/pallas_call | solution.py:552
  140.7 1.0 close.1
  (41 shorter events, 0.1 us)
Async XLA Ops:
  1.3 1.0 copy-start.1
  2.4 0.9 copy-start.6
  3.3 0.9 copy-start.7
  4.2 0.9 copy-start.8
  5.2 0.8 copy-start.9
  6.0 0.8 copy-start.11
  6.7 0.7 copy-start.13
  7.5 0.7 copy-start.15
  8.2 0.8 copy-start.17
  9.0 0.7 copy-start.18
  9.7 0.7 copy-start.20
  10.4 0.7 copy-start.21
  11.1 0.7 copy-start.23
  11.8 0.7 copy-start.24
  12.4 12.1 %copy-start.5 = (bf16[448,1792]{1,0:T(8,128)(2,1)S(1)}, bf16[448,1792]{1,0:T(8,128)(2,1)}, u32[]{:S(2)}) copy-start(bf16[448,1792]{1,0:T(8,128)(2,1)} %wo_ref.1) | copy-start | bytes 4816900
  12.4 12.1 %copy-start.10 = (f32[4,8,273]{2,1,0:T(8,128)S(1)}, f32[4,8,273]{2,1,0:T(8,128)}, u32[]{:S(2)}) copy-start(f32[4,8,273]{2,1,0:T(8,128)} %norm_ref.3) | copy-start | bytes 104836
  12.5 12.1 %copy-start.12 = (bf16[16,1024]{1,0:T(8,128)(2,1)S(1)}, bf16[16,1024]{1,0:T(8,128)(2,1)}, u32[]{:S(2)}) copy-start(bf16[16,1024]{1,0:T(8,128)(2,1)} %constant.12.clone.pick_ref) | copy-start | bytes 98308
  12.5 12.1 %copy-start.14 = (bf16[16,768]{1,0:T(8,128)(2,1)S(1)}, bf16[16,768]{1,0:T(8,128)(2,1)}, u32[]{:S(2)}) copy-start(bf16[16,768]{1,0:T(8,128)(2,1)} %constant.14.clone.plain_pick_ref) | copy-start | bytes 73732
  12.5 12.1 %copy-start.16 = (f32[8,512]{1,0:T(8,128)S(1)}, f32[8,512]{1,0:T(8,128)}, u32[]{:S(2)}) copy-start(f32[8,512]{1,0:T(8,128)} %constant.13.clone.bias_ref) | copy-start | bytes 49156
  12.5 12.1 %copy-start.19 = (f32[8,384]{1,0:T(8,128)S(1)}, f32[8,384]{1,0:T(8,128)}, u32[]{:S(2)}) copy-start(f32[8,384]{1,0:T(8,128)} %constant.15.clone.plain_bias_ref) | copy-start | bytes 36868
  12.5 12.1 %copy-start.22 = (bf16[8,256]{1,0:T(8,128)(2,1)S(1)}, bf16[8,256]{1,0:T(8,128)(2,1)}, u32[]{:S(2)}) copy-start(bf16[8,256]{1,0:T(8,128)(2,1)} %constant.16.clone.mask_ref) | copy-start | bytes 12292
  24.6 1.5 %copy-start = (bf16[8,4,240,128]{3,2,1,0:T(8,128)(2,1)S(1)}, bf16[8,4,240,128]{3,2,1,0:T(8,128)(2,1)}, u32[]{:S(2)}) copy-start(bf16[8,4,240,128]{3,2,1,0:T(8,128)(2,1)} %get-tuple-element.27.start_ref) | copy-start | bytes 5898244
  26.2 12.1 %copy-start.25 = (f32[1792]{0:T(1024)S(1)}, f32[1792]{0:T(1024)}, u32[]{:S(2)}) copy-start(f32[1792]{0:T(1024)} %param.34) | copy-start | bytes 21508
  26.2 13.6 %copy-start.2 = (bf16[8,16,1792]{2,1,0:T(8,128)(2,1)S(1)}, bf16[8,16,1792]{2,1,0:T(8,128)(2,1)}, u32[]{:S(2)}) copy-start(bf16[8,16,1792]{2,1,0:T(8,128)(2,1)} %param.22) | copy-start | bytes 1376260
  26.2 13.6 %copy-start.3 = (bf16[1792,512]{1,0:T(8,128)(2,1)S(1)}, bf16[1792,512]{1,0:T(8,128)(2,1)}, u32[]{:S(2)}) copy-start(bf16[1792,512]{1,0:T(8,128)(2,1)} %wg_ref.1) | copy-start | bytes 5505028
  26.2 13.6 %copy-start.4 = (bf16[1792,512]{1,0:T(8,128)(2,1)S(1)}, bf16[1792,512]{1,0:T(8,128)(2,1)}, u32[]{:S(2)}) copy-start(bf16[1792,512]{1,0:T(8,128)(2,1)} %wu_ref.1) | copy-start | bytes 5505028
  28.8 1.6 %collective-permute-start = (bf16[64,1792]{1,0:T(8,128)(2,1)S(1)}, bf16[64,1792]{1,0:T(8,128)(2,1)S(1)}, u32[]{:S(2)}, u32[]{:S(2)}) collective-permute-start(bf16[64,1792]{1,0:T(8,128)(2,1)S(1)} %get-tuple-element.29), channel_id=1, source_target_pairs={{0,1},{1,0},{2,3},{3,2},{4,5},{5,4},{6,7},{7,6},{8,9},{9,8},{10,11... | collective-permute-start | bytes 688136 | tf_op jit(solution)/shard_map/ppermute | solution.py:505
  30.4 7.7 %collective-permute-start.1 = (bf16[64,1792]{1,0:T(8,128)(2,1)S(1)}, bf16[64,1792]{1,0:T(8,128)(2,1)S(1)}, u32[]{:S(2)}, u32[]{:S(2)}) collective-permute-start(bf16[64,1792]{1,0:T(8,128)(2,1)S(1)} %add_convert_fusion.3), channel_id=1, source_target_pairs={{0,2},{1,3},{2,0},{3,1},{4,6},{5,7},{6,4},{7,5},{8,10},{9,11},{10,... | collective-permute-start | bytes 688136 | tf_op jit(solution)/shard_map/ppermute | solution.py:509
  38.2 1.6 %collective-permute-start.2 = (bf16[64,1792]{1,0:T(8,128)(2,1)S(1)}, bf16[64,1792]{1,0:T(8,128)(2,1)S(1)}, u32[]{:S(2)}, u32[]{:S(2)}) collective-permute-start(bf16[64,1792]{1,0:T(8,128)(2,1)S(1)} %add_convert_fusion.2.own_ref), channel_id=1, source_target_pairs={{0,1},{1,0},{2,3},{3,2},{4,5},{5,4},{6,7},{7,6},{8,9},{9,8},{10,11... | collective-permute-start | bytes 688136 | tf_op jit(solution)/shard_map/ppermute | solution.py:513
  42.6 3.3 %collective-permute-start.3 = (bf16[64,1792]{1,0:T(8,128)(2,1)S(1)}, bf16[64,1792]{1,0:T(8,128)(2,1)S(1)}, u32[]{:S(2)}, u32[]{:S(2)}) collective-permute-start(bf16[64,1792]{1,0:T(8,128)(2,1)S(1)} %get-tuple-element.32), channel_id=1, source_target_pairs={{0,1},{1,0},{2,3},{3,2},{4,5},{5,4},{6,7},{7,6},{8,9},{9,8},{10,11... | collective-permute-start | bytes 688136 | tf_op jit(solution)/shard_map/ppermute | solution.py:505
  42.8 13.7 %collective-permute-start.6 = (bf16[2,976,128]{2,1,0:T(8,128)(2,1)S(1)}, bf16[2,976,128]{2,1,0:T(8,128)(2,1)S(1)}, u32[]{:S(2)}, u32[]{:S(2)}) collective-permute-start(bf16[2,976,128]{2,1,0:T(8,128)(2,1)S(1)} %get-tuple-element.34), channel_id=1, source_target_pairs={{0,4},{4,0},{8,12},{12,8},{16,20},{20,16},{24,28},{28,24},{1,5},{5... | collective-permute-start | bytes 1499144 | tf_op jit(solution)/shard_map/ppermute | solution.py:492
  44.3 15.7 %collective-permute-start.7 = (bf16[2,976,128]{2,1,0:T(8,128)(2,1)S(1)}, bf16[2,976,128]{2,1,0:T(8,128)(2,1)S(1)}, u32[]{:S(2)}, u32[]{:S(2)}) collective-permute-start(bf16[2,976,128]{2,1,0:T(8,128)(2,1)S(1)} %get-tuple-element.35), channel_id=1, source_target_pairs={{0,8},{4,12},{8,16},{12,20},{16,24},{20,28},{24,0},{28,4},{1,9},{5... | collective-permute-start | bytes 1499144 | tf_op jit(solution)/shard_map/ppermute | solution.py:492
  45.9 14.9 %collective-permute-start.4 = (bf16[64,1792]{1,0:T(8,128)(2,1)S(1)}, bf16[64,1792]{1,0:T(8,128)(2,1)S(1)}, u32[]{:S(2)}, u32[]{:S(2)}) collective-permute-start(bf16[64,1792]{1,0:T(8,128)(2,1)S(1)} %add_convert_fusion.1), channel_id=1, source_target_pairs={{0,2},{1,3},{2,0},{3,1},{4,6},{5,7},{6,4},{7,5},{8,10},{9,11},{10,... | collective-permute-start | bytes 688136 | tf_op jit(solution)/shard_map/ppermute | solution.py:509
  47.5 63.7 %collective-permute-start.8 = (bf16[2,976,128]{2,1,0:T(8,128)(2,1)S(1)}, bf16[2,976,128]{2,1,0:T(8,128)(2,1)S(1)}, u32[]{:S(2)}, u32[]{:S(2)}) collective-permute-start(bf16[2,976,128]{2,1,0:T(8,128)(2,1)S(1)} %get-tuple-element.36), channel_id=1, source_target_pairs={{0,12},{4,8},{8,20},{12,16},{16,28},{20,24},{24,4},{28,0},{1,13},{... | collective-permute-start | bytes 1499144 | tf_op jit(solution)/shard_map/ppermute | solution.py:492
  49.0 72.9 %collective-permute-start.9 = (bf16[2,976,128]{2,1,0:T(8,128)(2,1)S(1)}, bf16[2,976,128]{2,1,0:T(8,128)(2,1)S(1)}, u32[]{:S(2)}, u32[]{:S(2)}) collective-permute-start(bf16[2,976,128]{2,1,0:T(8,128)(2,1)S(1)} %get-tuple-element.37), channel_id=1, source_target_pairs={{0,16},{4,20},{8,24},{12,28},{16,0},{20,4},{24,8},{28,12},{1,17},{... | collective-permute-start | bytes 1499144 | tf_op jit(solution)/shard_map/ppermute | solution.py:492
  56.4 75.3 %collective-permute-start.10 = (bf16[2,976,128]{2,1,0:T(8,128)(2,1)S(1)}, bf16[2,976,128]{2,1,0:T(8,128)(2,1)S(1)}, u32[]{:S(2)}, u32[]{:S(2)}) collective-permute-start(bf16[2,976,128]{2,1,0:T(8,128)(2,1)S(1)} %get-tuple-element.38), channel_id=1, source_target_pairs={{0,20},{4,16},{8,28},{12,24},{16,4},{20,0},{24,12},{28,8},{1,21},{... | collective-permute-start | bytes 1499144 | tf_op jit(solution)/shard_map/ppermute | solution.py:492
  60.0 71.8 %collective-permute-start.11 = (bf16[2,976,128]{2,1,0:T(8,128)(2,1)S(1)}, bf16[2,976,128]{2,1,0:T(8,128)(2,1)S(1)}, u32[]{:S(2)}, u32[]{:S(2)}) collective-permute-start(bf16[2,976,128]{2,1,0:T(8,128)(2,1)S(1)} %get-tuple-element.39), channel_id=1, source_target_pairs={{0,24},{4,28},{8,0},{12,4},{16,8},{20,12},{24,16},{28,20},{1,25},{... | collective-permute-start | bytes 1499144 | tf_op jit(solution)/shard_map/ppermute | solution.py:492
  60.9 72.6 %collective-permute-start.12 = (bf16[2,976,128]{2,1,0:T(8,128)(2,1)S(1)}, bf16[2,976,128]{2,1,0:T(8,128)(2,1)S(1)}, u32[]{:S(2)}, u32[]{:S(2)}) collective-permute-start(bf16[2,976,128]{2,1,0:T(8,128)(2,1)S(1)} %get-tuple-element.40), channel_id=1, source_target_pairs={{0,28},{4,24},{8,4},{12,0},{16,12},{20,8},{24,20},{28,16},{1,29},{... | collective-permute-start | bytes 1499144 | tf_op jit(solution)/shard_map/ppermute | solution.py:492
  111.2 29.5 %collective-permute-start.5 = (bf16[64,1792]{1,0:T(8,128)(2,1)S(1)}, bf16[64,1792]{1,0:T(8,128)(2,1)S(1)}, u32[]{:S(2)}, u32[]{:S(2)}) collective-permute-start(bf16[64,1792]{1,0:T(8,128)(2,1)S(1)} %add_convert_fusion.own_ref), channel_id=1, source_target_pairs={{0,1},{1,0},{2,3},{3,2},{4,5},{5,4},{6,7},{7,6},{8,9},{9,8},{10,11... | collective-permute-start | bytes 688136 | tf_op jit(solution)/shard_map/ppermute | solution.py:513

commit v2 on v1

v2 whole, which is shorter than its diff:
```python
import functools
import math

import jax
import jax.numpy as jnp
import numpy as np
from jax import lax
from jax.experimental import pallas as pl
from jax.experimental.pallas import tpu as pltpu
from jax.sharding import PartitionSpec as P

FD = 16
DV = 112
F = 273
CAP = 16
EPSILON = 1e-05

SPAN = F * DV
LINES = 240
WIDE = 256
PHASES = 7
EXTRA = 16
BF16 = jnp.bfloat16
F32 = jnp.float32


def line_of(index):
    return (index * SPAN) // 128, (index * SPAN) % 128


@functools.lru_cache(None)
def tables():
    scale_two = 0.25 * math.sqrt(0.5)

    def feature(column, f, left, right, bias):
        if f == 0:
            bias[0, column] = bias[1, column] = bias[2, column] = 1.0
        elif f <= FD:
            left[f - 1, column] = 1.0
            bias[1, column] = 1.0
            bias[2, column] = 0.5
        elif f < F:
            left[(f - 1 - FD) // FD, column] = 1.0
            right[(f - 1 - FD) % FD, column] = 1.0
            bias[2, column] = scale_two

    def build(width, places):
        left, right = np.zeros((FD, width)), np.zeros((FD, width))
        bias = np.zeros((8, width), np.float32)
        for column, f in places:
            feature(column, f, left, right, bias)
        return np.concatenate([left, right], 1).astype(BF16), bias

    lined = [
        (part * WIDE + m, 8 * (m // PHASES) + m % PHASES + part)
        for part in range(2)
        for m in range(LINES)
    ]
    line_pick, line_bias = build(2 * WIDE, lined)
    plain_pick, plain_bias = build(384, [(f, f) for f in range(F)])
    phase_mask = np.zeros((8, WIDE))
    for k in range(PHASES):
        phase_mask[k, k::PHASES] = 1.0
    turn = np.zeros((DV, PHASES * 128))
    for k in range(PHASES):
        for lane in range(128):
            turn[(16 * k + lane) % DV, 128 * k + lane] = 1.0
    table = np.zeros((DV + FD, 1792))
    table[:DV, : PHASES * 128] = turn
    table[:8, PHASES * 128 : PHASES * 128 + WIDE] = phase_mask
    table[DV:] = np.concatenate([line_pick, plain_pick], 1)
    return table.astype(BF16), np.concatenate([line_bias, plain_bias], 1)


def dot_nt(a, b):
    return lax.dot_general(a, b, (((1,), (1,)), ((), ())), preferred_element_type=F32)


def dot_tn(a, b):
    return lax.dot_general(a, b, (((0,), (0,)), ((), ())), preferred_element_type=F32)


def dot_nn(a, b):
    return jnp.dot(a, b, preferred_element_type=F32)


def expand(x, table_ref, bias_ref, start, width):
    both = dot_nn(x, table_ref[DV:, 2 * start : 2 * (start + width)])
    bias = bias_ref[:, start : start + width]
    left = both[:, :width] + bias[0:1, :]
    right = both[:, width:] + bias[1:2, :]
    return left * right * bias[2:3, :]


def lined_phi(x, table_ref, bias_ref):
    return expand(x, table_ref, bias_ref, 0, 2 * WIDE)


def plain_phi(x, table_ref, bias_ref):
    return expand(x, table_ref, bias_ref, 2 * WIDE, 384)


def spread(phi, table_ref):
    pieces = []
    for k in range(PHASES):
        chosen = table_ref[k : k + 1, PHASES * 128 : PHASES * 128 + WIDE]
        for part in range(2):
            pieces.append(phi[:, part * WIDE : (part + 1) * WIDE] * chosen)
    return jnp.concatenate(pieces, axis=0)


def pack_kernel(
    heads, count, pair_cap, tp_size, loaded, made,
    state_ref, *rest,
):
    fetched, rest = rest[:loaded], rest[loaded:]
    pieces, rest = rest[:made], rest[made:]
    (q_ref, k_ref, v_ref, start_ref), rest = rest[:4], rest[4:]
    held, rest = rest[:loaded], rest[loaded:]
    flat, padded, mixed, phi, plain, turned, edges, extra, stage, begun, none, state_sem, load_sem, none_sem, out_sem, begun_sem = rest
    fetches = [pltpu.make_async_copy(fetched[i], held[i], load_sem.at[i]) for i in range(loaded)]
    for fetch in fetches:
        fetch.start()
    lines = state_ref.shape[0]
    loads = [
        pltpu.make_async_copy(state_ref.at[:, h], flat.at[h, pl.ds(0, lines)], state_sem.at[h])
        for h in range(heads)
    ]
    for load in loads:
        load.start()
    (
        owner_ref, accepted_ref, tokens_ref, edge_ref, gain_ref, conv_ref,
        wq_ref, wk_ref, wv_ref, table_ref, bias_ref, norm_ref,
    ) = held
    requests = owner_ref.shape[0]
    steps = tokens_ref.shape[0] // requests
    body = heads * LINES
    empty = [piece.at[i, pl.ds(body, EXTRA)] for piece in pieces for i in range(piece.shape[0])]
    blanks = [pltpu.make_async_copy(none, place, none_sem.at[i]) for i, place in enumerate(empty)]
    for fetch in fetches[:6]:
        fetch.wait()
    ranks, seconds, second = [], [], jnp.int32(0)
    for r in range(requests):
        rank = jnp.int32(0)
        for earlier in range(r):
            rank = rank + (owner_ref[earlier] == owner_ref[r]).astype(jnp.int32)
        ranks.append(rank)
        seconds.append((rank == 1) & (second == 0))
        second = second + (rank == 1).astype(jnp.int32)
    one_line = lax.broadcasted_iota(jnp.int32, (EXTRA, 128), 1)
    one_row = lax.broadcasted_iota(jnp.int32, (EXTRA, 128), 0)
    last = one_row == EXTRA - 1
    count_mark = jnp.where(last & (one_line == 126), second.astype(F32), 0.0)
    none[...] = count_mark.astype(BF16)
    for blank in blanks:
        blank.start()

    tp_here = lax.axis_index("tp")
    gain = gain_ref[...].reshape(1, gain_ref.shape[0])
    for r in range(requests):
        base = 24 * r
        wide = tokens_ref[steps * r : steps * (r + 1), :].astype(F32)
        mean = jnp.mean(wide * wide, axis=-1, keepdims=True)
        normed = (wide * lax.rsqrt(mean + EPSILON) * gain).astype(BF16).astype(F32)
        padded[base + 8 : base + 8 + steps, :] = normed
        padded[base : base + 8, :] = jnp.zeros((8, wide.shape[1]), F32)
        padded[base + 6 : base + 8, :] = edge_ref[r].astype(F32)
        convolved = conv_ref[2:3, :] * normed
        for tap in range(2):
            convolved = convolved + conv_ref[tap : tap + 1, :] * padded[base + 6 + tap : base + 6 + tap + steps, :]
        blend = normed + convolved / (1.0 + jnp.exp(-normed))
        mixed[steps * r : steps * (r + 1), :] = blend.astype(BF16)

    for fetch in fetches[6:]:
        fetch.wait()
    queries = dot_nt(mixed[...], wq_ref[...]).astype(BF16)
    keys = dot_nt(mixed[...], wk_ref[...]).astype(BF16)
    values = dot_nt(mixed[...], wv_ref[...]).astype(BF16)
    q_ref[...] = queries
    k_ref[...] = keys
    v_ref[...] = values

    for h in range(heads):
        key = keys[:, FD * h : FD * (h + 1)]
        phi[h] = lined_phi(key, table_ref, bias_ref)
        plain[h] = plain_phi(key, table_ref, bias_ref)
        turned[h] = dot_nn(values[:, DV * h : DV * (h + 1)], table_ref[:DV, : PHASES * 128]).astype(BF16)

    column_width = tokens_ref.shape[1] // tp_size
    edge_rows = lax.broadcasted_iota(jnp.int32, (2 * requests, 24 * requests), 0)
    edge_columns = lax.broadcasted_iota(jnp.int32, (2 * requests, 24 * requests), 1)
    wanted = jnp.zeros(edge_rows.shape, jnp.int32)
    for r in range(requests):
        wanted = jnp.where(edge_rows // 2 == r, 24 * r + 6 + accepted_ref[r] + edge_rows % 2, wanted)
    choose = (edge_columns == wanted).astype(F32).astype(BF16)
    for i in range(tp_size):
        @pl.when(tp_here == i)
        def _():
            window = padded[:, column_width * i : column_width * (i + 1)].astype(BF16)
            edges[:, :column_width] = dot_nn(choose, window)

    lane_ids = lax.broadcasted_iota(jnp.int32, (LINES, 128), 1)
    step_ids = lax.broadcasted_iota(jnp.int32, (steps, 1), 0)
    edge_lines = -(-column_width // 128)
    for load in loads:
        load.wait()
    for blank in blanks:
        blank.wait()
    sends, keeps = [], []
    for r in range(requests):
        owner = owner_ref[r]
        taken = (step_ids < accepted_ref[r]).astype(F32)
        first, shift = line_of(r)
        extra[...] = jnp.zeros((EXTRA, 128), F32)
        for h in range(heads):
            rows = slice(steps * r, steps * (r + 1))
            spread_keys = spread((phi[h, rows, :] * taken).astype(BF16), table_ref)
            value_rows = turned[h, rows, :]
            parts = []
            for k in range(PHASES):
                block = value_rows[:, 128 * k : 128 * (k + 1)]
                early = one_line < DV - 16 * k
                zero = jnp.zeros((steps, 128), BF16)
                parts.append(jnp.where(early, block, zero))
                parts.append(jnp.where(early, zero, block))
            added = dot_tn(spread_keys, jnp.concatenate(parts, axis=0))[:LINES]
            start = flat[h, first : first + LINES, :]
            if shift:
                following = flat[h, first + 1 : first + 1 + LINES, :]
                start = pltpu.roll(jnp.where(lane_ids >= shift, start, following), 128 - shift, 1)
            begun[r, h] = start.astype(BF16)
            kept = start + added
            sums = jnp.sum(plain[h, rows, :] * taken, axis=0, keepdims=True)[:, :F] + norm_ref[h, r : r + 1, :]
            extra[2 * h : 2 * h + 1, :] = sums[:, :128]
            extra[2 * h + 1 : 2 * h + 2, :] = sums[:, 128:256]
            tail = jnp.concatenate([sums[:, 256:], jnp.zeros((1, 128 - (F - 256)), F32)], axis=1)
            stage[r, h * LINES : (h + 1) * LINES - 16, :] = kept[: LINES - 16].astype(BF16)
            stage[r, (h + 1) * LINES - 16 : (h + 1) * LINES, :] = jnp.where(
                one_row == 15, tail, kept[LINES - 16 :]
            ).astype(BF16)
        for j in range(2):
            for c in range(edge_lines):
                end = min(column_width, 128 * (c + 1))
                line = 2 * heads + edge_lines * j + c
                extra[line : line + 1, : end - 128 * c] = edges[2 * r + j : 2 * r + j + 1, 128 * c : end]
        marked = jnp.where(last & (one_line == 127), (owner + 1).astype(F32), extra[...] + count_mark)
        stage[r, body : body + EXTRA, :] = marked.astype(BF16)
        keep = pltpu.make_async_copy(begun.at[r], start_ref.at[r], begun_sem.at[r])
        keep.start()
        keeps.append(keep)
        if pair_cap == 1:
            routes = [(ranks[r] == 0, pieces[0].at[owner])]
        else:
            far = owner ^ lax.axis_index("req")
            routes = [((ranks[r] == 0) & (far == k), pieces[k].at[0]) for k in range(count)]
            routes += [(seconds[r], pieces[k].at[1]) for k in range(5)]
            routes += [(ranks[r] == 1, pieces[count].at[owner])]
        for i, (chosen, place) in enumerate(routes):
            send = pltpu.make_async_copy(stage.at[r], place, out_sem.at[r, i])
            sends.append((chosen, send))

            @pl.when(chosen)
            def _():
                send.start()
    for chosen, send in sends:
        @pl.when(chosen)
        def _():
            send.wait()
    for keep in keeps:
        keep.wait()


def attend_kernel(
    heads,
    q_ref, k_ref, v_ref, start_ref, norm_ref, wo_ref, table_ref, bias_ref,
    part_ref,
    attended,
):
    requests = start_ref.shape[0]
    rows_all = q_ref.shape[0]
    steps = rows_all // requests
    row_ids = lax.broadcasted_iota(jnp.int32, (rows_all, rows_all), 0)
    column_ids = lax.broadcasted_iota(jnp.int32, (rows_all, rows_all), 1)
    allowed = (row_ids // steps == column_ids // steps) & (row_ids >= column_ids)
    lane_ids = lax.broadcasted_iota(jnp.int32, (steps, 128), 1)
    for h in range(heads):
        query = q_ref[:, FD * h : FD * (h + 1)]
        key = k_ref[:, FD * h : FD * (h + 1)]
        value = v_ref[:, DV * h : DV * (h + 1)]
        phi = lined_phi(query, table_ref, bias_ref).astype(BF16)
        plain = plain_phi(query, table_ref, bias_ref)
        inner = dot_nt(query, key) * 0.25
        scores = jnp.where(allowed, 1.0 + inner + 0.5 * inner * inner, 0.0)
        below = jnp.sum(scores, axis=-1, keepdims=True)
        within = dot_nn(scores.astype(BF16), value)
        for r in range(requests):
            rows = slice(steps * r, steps * (r + 1))
            spread_query = spread(phi[rows], table_ref)[:, :LINES]
            lined = dot_nn(spread_query, start_ref[r, h])
            total = jnp.zeros((steps, 128), F32)
            for j in range(PHASES + 1):
                block = jnp.zeros((steps, 128), F32)
                if j < PHASES:
                    at = steps * (2 * j)
                    block = jnp.where(lane_ids < DV - 16 * j, lined[at : at + steps], 0.0)
                if j > 0:
                    at = steps * (2 * (j - 1) + 1)
                    block = jnp.where(lane_ids >= DV - 16 * (j - 1), lined[at : at + steps], block)
                total = total + (pltpu.roll(block, 16 * j, 1) if 0 < j < 8 else block)
            beneath = below[rows] + jnp.sum(plain[rows, :F] * norm_ref[h, r : r + 1, :], axis=-1, keepdims=True)
            attended[h, rows, :] = ((total[:, :DV] + within[rows]) / beneath).astype(BF16)
    out = dot_nn(attended[0], wo_ref[0:DV, :])
    for h in range(1, heads):
        out = out + dot_nn(attended[h], wo_ref[DV * h : DV * (h + 1), :])
    part_ref[...] = out.astype(BF16)


def mlp_kernel(tokens_ref, sum_ref, gain_ref, wg_ref, wu_ref, wd_ref, residual_ref, part_ref):
    residual = tokens_ref[...].astype(F32) + sum_ref[...].astype(F32)
    residual_ref[...] = residual
    mean = jnp.mean(residual * residual, axis=-1, keepdims=True)
    gain = gain_ref[...].reshape(1, gain_ref.shape[0])
    second = (residual * lax.rsqrt(mean + EPSILON) * gain).astype(BF16)
    gate = dot_nn(second, wg_ref[...])
    up = dot_nn(second, wu_ref[...])
    hidden = (gate / (1.0 + jnp.exp(-gate)) * up).astype(BF16)
    part_ref[...] = dot_nn(hidden, wd_ref[...]).astype(BF16)


def close_kernel(residual_ref, sum_ref, *rest):
    marks, (out_ref, several_ref, lines, sems) = rest[:-4], rest[-4:]
    reads = [
        pltpu.make_async_copy(mark.at[0, pl.ds(mark.shape[1] - EXTRA, EXTRA)], lines.at[i], sems.at[i])
        for i, mark in enumerate(marks)
    ]
    for read in reads:
        read.start()
    out_ref[...] = (residual_ref[...] + sum_ref[...].astype(F32)).astype(BF16)
    for read in reads:
        read.wait()
    several_ref[0] = jnp.int32(0)
    if marks:
        row = lax.broadcasted_iota(jnp.int32, (EXTRA, 128), 0)
        lane = lax.broadcasted_iota(jnp.int32, (EXTRA, 128), 1)
        most = functools.reduce(jnp.maximum, [lines[i].astype(F32) for i in range(len(marks))])
        most = jnp.max(jnp.where((row == EXTRA - 1) & (lane == 126), most, 0.0))
        several_ref[0] = (most > 1.0).astype(jnp.int32)


def settle_kernel(heads, count, pair_cap, direct, arrivals, *rest):
    lanes = count * pair_cap
    body = heads * LINES
    here = lax.axis_index("req")
    inputs, rest = rest[:arrivals], rest[arrivals:]
    state_ref, norm_ref, edge_ref, stage, flat, shifted, table, in_sem, out_sem = rest
    loads = []

    def load(place, lane):
        loads.append(pltpu.make_async_copy(place, stage.at[lane], in_sem.at[len(loads)]))

    for i in range(count):
        if pair_cap == 1:
            load(inputs[0].at[i], i)
        else:
            source = here ^ i
            load(inputs[i].at[0], 2 * source)
            if direct:
                load(inputs[i].at[1] if i < 5 else inputs[count + i - 5].at[0], 2 * source + 1)
            else:
                load(inputs[count].at[i], 2 * i + 1)
    for copy in loads:
        copy.start()
    norm_ref[...] = jnp.zeros(norm_ref.shape, F32)
    edge_ref[...] = jnp.zeros(edge_ref.shape, BF16)
    for copy in loads:
        copy.wait()
    one_row = lax.broadcasted_iota(jnp.int32, (EXTRA, 128), 0)
    one_line = lax.broadcasted_iota(jnp.int32, (EXTRA, 128), 1)
    mark = (one_row == EXTRA - 1) & (one_line == 127)
    filled = jnp.int32(0)
    for lane in range(lanes):
        block = jnp.where(mark, stage[lane, body : body + EXTRA, :].astype(F32), 0.0)
        live = jnp.sum(block).astype(jnp.int32) == here + 1
        table[filled] = lane
        filled = filled + live.astype(jnp.int32)

    total = state_ref.shape[0]
    width = edge_ref.shape[2]
    edge_lines = -(-width // 128)
    lane_ids = lax.broadcasted_iota(jnp.int32, (LINES, 128), 1)
    head_ids = lax.broadcasted_iota(jnp.int32, (8, 128), 1)
    head_rows = lax.broadcasted_iota(jnp.int32, (8, 128), 0)
    stores = []
    done = 0
    for s in range(CAP):
        first, shift = line_of(s)
        last = -(-((s + 1) * SPAN) // 128)
        span = last - first

        @pl.when(s < filled)
        def _():
            lane = table[s]
            extra = stage[lane, body : body + EXTRA, :].astype(F32)
            pairs = [[], []]
            for j in range(2):
                for c in range(edge_lines):
                    end = min(width, 128 * (c + 1))
                    line = 2 * heads + edge_lines * j + c
                    pairs[j].append(extra[line : line + 1, : end - 128 * c])
            edge_ref[s] = jnp.concatenate(
                [jnp.concatenate(pairs[j], axis=1) for j in range(2)], axis=0
            ).astype(BF16)
            for h in range(heads):
                rows = stage[lane, h * LINES : (h + 1) * LINES, :].astype(F32)
                norm_ref[h, s : s + 1, :] = jnp.concatenate(
                    [
                        extra[2 * h : 2 * h + 1, :],
                        extra[2 * h + 1 : 2 * h + 2, :],
                        rows[LINES - 1 : LINES, : F - 256],
                    ],
                    axis=1,
                )
                if shift:
                    shifted[h, 8 : 8 + LINES, :] = rows
                    before = shifted[h, 7 : 7 + LINES, :]
                    rows = pltpu.roll(jnp.where(lane_ids < 128 - shift, rows, before), shift, 1)
                    old = flat[h, first : first + 1, :]
                    flat[h, first + 1 : last, :] = rows[1:span]
                    flat[h, first : first + 1, :] = jnp.where(head_ids[:1] < shift, old, rows[:1])
                else:
                    flat[h, first:last, :] = rows[:span]

        @pl.when(s >= filled)
        def _():
            for h in range(heads):
                if shift:
                    old = flat[h, first : first + 1, :]
                    flat[h, first + 1 : last, :] = jnp.zeros((span - 1, 128), F32)
                    flat[h, first : first + 1, :] = jnp.where(head_ids[:1] < shift, old, 0.0)
                else:
                    flat[h, first:last, :] = jnp.zeros((span, 128), F32)

        until = total if s == CAP - 1 else ((s + 1) * SPAN // 128) // 8 * 8
        for h in range(heads):
            store = pltpu.make_async_copy(
                flat.at[h, pl.ds(done, until - done)],
                state_ref.at[pl.ds(done, until - done), h],
                out_sem.at[s, h],
            )
            store.start()
            stores.append(store)
        done = until
    for store in stores:
        store.wait()


def shards(
    tokens, conv_edge, state_start, norm_start, accepted, owner, attn_gain, conv_weight,
    w_query, w_key, w_value, w_out, mlp_gain, w_gate, w_up, w_down,
):
    requests, steps, width = tokens.shape
    count = lax.axis_size("req")
    tp_size = lax.axis_size("tp")
    pair_cap = (CAP + count - 1) // count
    heads = w_query.shape[1] // FD
    rows_all = requests * steps
    lines = state_start.shape[1] // 128
    payload = heads * LINES + EXTRA
    column_width = width // tp_size
    table, bias = (jnp.asarray(t) for t in tables())

    vmem = pl.BlockSpec(memory_space=pltpu.VMEM)
    smem = pl.BlockSpec(memory_space=pltpu.SMEM)
    hbm = pl.BlockSpec(memory_space=pltpu.HBM)
    anywhere = pl.BlockSpec(memory_space=pl.ANY)
    limit = functools.partial(pltpu.CompilerParams, vmem_limit_bytes=40 * 2**20)

    def cost(us):
        return pl.CostEstimate(flops=0, transcendentals=0, bytes_accessed=int(us * 3.6e2))

    flat_tokens = tokens.reshape(rows_all, width)
    lined_state = jnp.swapaxes(state_start.reshape(heads, lines, 128), 0, 1)
    held = [count] if pair_cap == 1 else [2] * 5 + [1] * 3 + [count]
    piece_shapes = [jax.ShapeDtypeStruct((size, payload, 128), BF16) for size in held]
    fetched = [
        owner, accepted, flat_tokens, conv_edge, attn_gain, conv_weight,
        w_query.T, w_key.T, w_value, table, bias, norm_start,
    ]
    outs = pl.pallas_call(
        functools.partial(pack_kernel, heads, count, pair_cap, tp_size, len(fetched), len(held)),
        out_shape=piece_shapes
        + [
            jax.ShapeDtypeStruct((rows_all, heads * FD), BF16),
            jax.ShapeDtypeStruct((rows_all, heads * FD), BF16),
            jax.ShapeDtypeStruct((rows_all, heads * DV), BF16),
            jax.ShapeDtypeStruct((requests, heads, LINES, 128), BF16),
        ],
        in_specs=[hbm] * (1 + len(fetched)),
        out_specs=[anywhere] * len(held) + [vmem] * 3 + [anywhere],
        scratch_shapes=[pltpu.SMEM(x.shape, x.dtype) for x in fetched[:2]]
        + [pltpu.VMEM(x.shape, x.dtype) for x in fetched[2:]]
        + [
            pltpu.VMEM((heads, (lines + 1) // 8 * 8 + 8, 128), F32),
            pltpu.VMEM((requests * 24, width), F32),
            pltpu.VMEM((rows_all, width), BF16),
            pltpu.VMEM((heads, rows_all, 2 * WIDE), F32),
            pltpu.VMEM((heads, rows_all, 384), F32),
            pltpu.VMEM((heads, rows_all, PHASES * 128), BF16),
            pltpu.VMEM((2 * requests, -(-column_width // 128) * 128), F32),
            pltpu.VMEM((EXTRA, 128), F32),
            pltpu.VMEM((requests, payload, 128), BF16),
            pltpu.VMEM((requests, heads, LINES, 128), BF16),
            pltpu.VMEM((EXTRA, 128), BF16),
            pltpu.SemaphoreType.DMA((heads,)),
            pltpu.SemaphoreType.DMA((len(fetched),)),
            pltpu.SemaphoreType.DMA((sum(held),)),
            pltpu.SemaphoreType.DMA((requests, count + 6)),
            pltpu.SemaphoreType.DMA((requests,)),
        ],
        compiler_params=limit(vmem_limit_bytes=60 * 2**20),
        cost_estimate=cost(8),
        name="pack",
    )(lined_state, *fetched)
    pieces, (queries, keys, values, start_rows) = list(outs[: len(held)]), outs[len(held) :]

    def swapped(x, far):
        return lax.ppermute(x, "req", [(i, i ^ far) for i in range(count)])

    arrived = {}

    def wave(now, fars, waits, later):
        for far in fars:
            arrived[far] = swapped(pieces[far], far)
        now, done, held_back = lax.optimization_barrier(
            (now, [arrived[far] for far in waits], [pieces[far] for far in later])
        )
        for far, x in zip(waits, done):
            arrived[far] = x
        for far, x in zip(later, held_back):
            pieces[far] = x
        return now

    cores = [[i, i + 1] for i in range(0, tp_size, 2)]
    chips = [list(range(core, tp_size, 2)) for core in range(2)]

    def summed(part, meet=lambda x: x):
        half = rows_all // 2
        both = lax.all_gather(part, "tp", axis=0, axis_index_groups=cores)
        mine = lax.dynamic_slice_in_dim(both, lax.axis_index("tp") % 2 * half, half, 1)
        mine = meet(jnp.sum(mine.astype(F32), axis=0).astype(BF16))
        mine = lax.all_gather(mine, "tp", axis=0, axis_index_groups=chips)
        mine = jnp.sum(mine.astype(F32), axis=0).astype(BF16)
        return lax.all_gather(mine, "tp", axis=0, tiled=True, axis_index_groups=cores)

    part = pl.pallas_call(
        functools.partial(attend_kernel, heads),
        out_shape=jax.ShapeDtypeStruct((rows_all, width), BF16),
        in_specs=[vmem] * 8,
        out_specs=vmem,
        scratch_shapes=[pltpu.VMEM((heads, rows_all, DV), BF16)],
        compiler_params=limit(),
        cost_estimate=cost(3),
        name="attend",
    )(
        queries, keys, values, start_rows, norm_start, w_out, table, bias,
    )
    total = summed(part)
    residual, part = pl.pallas_call(
        mlp_kernel,
        out_shape=[jax.ShapeDtypeStruct((rows_all, width), F32), jax.ShapeDtypeStruct((rows_all, width), BF16)],
        in_specs=[vmem] * 6,
        out_specs=[vmem] * 2,
        compiler_params=limit(),
        cost_estimate=cost(3),
        name="mlp",
    )(flat_tokens, total, mlp_gain, w_gate, w_up, w_down)
    forward = {}

    def half_way(x):
        if pair_cap > 1:
            x = wave(x, (4, 5, 2, 1, 3), (4, 5, 2, 1, 3), (6, 7))
            passed = arrived[4][1:2]
            forward.update({far: swapped(passed, far) for far in (1, 2, 3)})
        return x

    total = summed(part, half_way)
    if pair_cap > 1:
        total, forward = wave((total, forward), (6, 7), (6, 7), ())
    firsts, items = [], []
    if pair_cap > 1:
        arrived[0] = pieces[0]
        firsts = [arrived[far] for far in range(count)]
        items = [forward[far] for far in (1, 2, 3)]
    hidden_out, several = pl.pallas_call(
        close_kernel,
        out_shape=[jax.ShapeDtypeStruct((rows_all, width), BF16), jax.ShapeDtypeStruct((1,), jnp.int32)],
        in_specs=[vmem] * 2 + [anywhere] * len(firsts),
        out_specs=[vmem, smem],
        scratch_shapes=[pltpu.VMEM((count, EXTRA, 128), BF16), pltpu.SemaphoreType.DMA((count,))],
        compiler_params=limit(),
        cost_estimate=cost(1),
        name="close",
    )(residual, total, *firsts)

    out_lines = CAP * SPAN // 128

    def settled(direct, *inputs):
        return pl.pallas_call(
            functools.partial(settle_kernel, heads, count, pair_cap, direct, len(inputs)),
            out_shape=[
                jax.ShapeDtypeStruct((out_lines, heads, 128), F32),
                jax.ShapeDtypeStruct((heads, CAP, F), F32),
                jax.ShapeDtypeStruct((CAP, 2, column_width), BF16),
            ],
            in_specs=[anywhere] * len(inputs),
            out_specs=[anywhere, vmem, vmem],
            scratch_shapes=[
                pltpu.VMEM((count * pair_cap, payload, 128), BF16),
                pltpu.VMEM((heads, out_lines, 128), F32),
                pltpu.VMEM((heads, LINES + 16, 128), F32),
                pltpu.SMEM((count * pair_cap + 1,), jnp.int32),
                pltpu.SemaphoreType.DMA((count * pair_cap,)),
                pltpu.SemaphoreType.DMA((CAP, heads)),
            ],
            compiler_params=limit(),
            cost_estimate=cost(7),
            name="settle" if direct else "settle_general",
        )(*inputs)

    def exchanged(x):
        return lax.all_to_all(x, "req", 0, 0, tiled=True)

    if pair_cap > 1:
        kept_state, kept_norm, kept_edge = lax.cond(
            several[0] > 0,
            lambda firsts, items, spare: settled(False, *firsts, exchanged(spare)),
            lambda firsts, items, spare: settled(True, *firsts, *items),
            firsts, items, pieces[count],
        )
    else:
        kept_state, kept_norm, kept_edge = settled(True, exchanged(pieces[0]))
    return (
        hidden_out.reshape(requests, steps, width),
        jnp.swapaxes(kept_state, 0, 1).reshape(heads, out_lines * 128),
        kept_norm,
        kept_edge,
    )


def solution(mesh):
    placed = (
        P("req", None, None),
        P("req", None, None),
        P("tp", "req"),
        P("tp", "req", None),
        P("req"),
        P("req"),
        P(),
        P(),
        P(None, "tp"),
        P(None, "tp"),
        P("tp", None),
        P("tp", None),
        P(),
        P(None, "tp"),
        P(None, "tp"),
        P("tp", None),
    )
    return jax.shard_map(
        shards,
        mesh=mesh,
        in_specs=placed,
        out_specs=(
            P("req", None, None),
            P("tp", "req"),
            P("tp", "req", None),
            P("req", None, "tp"),
        ),
        check_vma=False,
    )
```

time: 143 us -> 93.5 us (0.65)
  waiting for transfers between devices: 86.1 us -> 19.7 us
  blocking collectives: 0 us -> 24.5 us
  local copies, waits for them, and re-layouts: 13.4 us -> 8.65 us
  Pallas kernels: 25.7 us -> 22.8 us
    ppermute x13 -> x10, waiting for transfers between devices: 86.1 us -> 19.7 us  [swapped(): return lax.ppermute(x, 'req', [(i, i ^ far) for i in range(count)])]
    all_gather x0 -> x6, blocking collectives: none -> 24.5 us  [the longest x2 15 us: summed(): mine = lax.all_gather(mine, 'tp', axis=0, axis_index_groups=chips)]
    unnamed x52 -> x28, local copies, waits for them, and re-layouts: 12.7 us -> 7 us
    slice x0 -> x1, local copies, waits for them, and re-layouts: none -> 1.66 us  [half_way(): passed = arrived[4][1:2]]
    pallas_call x1, Pallas kernels: 2.8 us -> 1.23 us  [shards(): pl.pallas_call(mlp_kernel, out_shape=[jax.ShapeDtypeStruct((rows_all, wid...]
    ppermute x13 -> x10, starting transfers between devices: 15.4 us -> 14.2 us  [swapped(): return lax.ppermute(x, 'req', [(i, i ^ far) for i in range(count)])]
  transfers between devices with their start and end apart: 13 -> 10, of which waited for: 8 -> 4; matrix products, arithmetic and copies ran while one was open for 0% -> 0% of each run, Pallas kernels for 5% -> 4%
where the time goes in v2:
time: 93.5 us; the launch traced here: 91.9 us
  blocking collectives  24.5 us (26%)
  Pallas kernels  22.8 us (24%)
  waiting for transfers between devices  19.7 us (21%)
  starting transfers between devices  14.2 us (15%)
  local copies, waits for them, and re-layouts  8.65 us (9%)
  between operations  1.6 us (2%)
    ppermute x10, waiting for transfers between devices, swapped(): return lax.ppermute(x, 'req', [(i, i ^ far) for i in range(count)])  19.7 us
    all_gather x2, blocking collectives, summed(): mine = lax.all_gather(mine, 'tp', axis=0, axis_index_groups=chips)  15 us
    ppermute x10, starting transfers between devices, swapped(): return lax.ppermute(x, 'req', [(i, i ^ far) for i in range(count)])  14.2 us
    pallas_call x1, Pallas kernels, shards(): pl.pallas_call(functools.partial(pack_kernel, heads, count, pair_cap, tp_...  10.3 us
    pallas_call x1, Pallas kernels, settled(): pl.pallas_call(functools.partial(settle_kernel, heads, count, pair_cap, d...  7.15 us
    unnamed x28, local copies, waits for them, and re-layouts  7 us
    all_gather x2, blocking collectives, summed(): both = lax.all_gather(part, 'tp', axis=0, axis_index_groups=cores)  5.19 us
    all_gather x2, blocking collectives, summed(): lax.all_gather(mine, 'tp', axis=0, tiled=True, axis_index_groups=cores)  4.27 us
  transfers between devices with their start and end apart: 10, of which 4 were waited for; matrix products, arithmetic and copies ran while one was open for 0% of the time, Pallas kernels for 4%

profile of v2, /device:TPU:8, one launch (start us, length us, event | category | flops | bytes accessed | tf_op | source)
XLA Modules:
  0.0 91.9 jit_solution(270357111243289488)
XLA Ops:
  0.6 0.0 copy-start.5
  0.7 0.0 copy-start.9
  0.7 10.3 %pack.1 = (bf16[2,976,128]{2,1,0:T(8,128)(2,1)}, bf16[2,976,128]{2,1,0:T(8,128)(2,1)}, bf16[2,976,128]{2,1,0:T(8,128)(2,1)}, bf16[2,976,128]{2,1,0:T(8,128)(2,1)...) custom-call(f32[1911,4,128]{2,1,0:T(4,128)} %bitcast.17, ...), custom_call_target="tpu_custom_call" | custom-call | bytes 2880 | tf_op jit(solution)/shard_map/pack/pallas_call | solution.py:489
  11.0 3.6 %collective-permute-start.1 = (bf16[1,976,128]{2,1,0:T(8,128)(2,1)}, bf16[1,976,128]{2,1,0:T(8,128)(2,1)S(1)}, u32[]{:S(2)}, u32[]{:S(2)}) collective-permute-start(bf16[1,976,128]{2,1,0:T(8,128)(2,1)} %get-tuple-element.105), channel_id=1, source_target_pairs={{0,20},{4,16},{8,28},{12,24},{16,4},{20,0},{24,12},{28,8},{1,21},{... | collective-permute-start | bytes 749576 | tf_op jit(solution)/shard_map/ppermute | solution.py:527
  14.6 0.3 collective-permute-start
  14.9 0.5 collective-permute-start.2
  15.4 0.3 collective-permute-start.3
  15.7 2.7 %collective-permute-start.4 = (bf16[2,976,128]{2,1,0:T(8,128)(2,1)}, bf16[2,976,128]{2,1,0:T(8,128)(2,1)}, u32[]{:S(2)}, u32[]{:S(2)}) collective-permute-start(bf16[2,976,128]{2,1,0:T(8,128)(2,1)} %get-tuple-element.108), channel_id=1, source_target_pairs={{0,12},{4,8},{8,4},{12,0},{16,28},{20,24},{24,20},{28,16},{1,13},{... | collective-permute-start | bytes 1499144 | tf_op jit(solution)/shard_map/ppermute | solution.py:527
  18.4 0.0 copy-start
  18.4 1.5 %copy-done = bf16[8,4,240,128]{3,2,1,0:T(8,128)(2,1)S(1)} copy-done((bf16[8,4,240,128]{3,2,1,0:T(8,128)(2,1)S(1)}, bf16[8,4,240,128]{3,2,1,0:T(8,128)(2,1)}, u32[]{:S(2)}) %copy-start) | copy-done | bytes 1966104
  20.0 0.9 copy-done.8
  20.9 0.8 copy-done.10
  21.6 0.8 copy-done.11
  22.4 2.6 %attend.1 = bf16[128,1792]{1,0:T(8,128)(2,1)S(1)} custom-call(bf16[128,64]{1,0:T(8,128)(2,1)S(1)} %copy-done.10, bf16[128,64]{1,0:T(8,128)(2,1)S(1)} %copy-done.11, bf16[128,448]{1,0:T(8,128)(2,1)S(1)} %copy-done.8, bf16[8,4,240,128]{3,2,1,0:T(8,128)(2,1)S(1)} %copy-done, f32[4,8,273]{2,1,0:T(8,128)S(1)} %copy-done.7, bf16[448,1792]{1,0:T(8,128)(2,1)S(1)} %copy-done.6, ...), custom_call_target="tpu_custom_call" | custom-call | bytes 1080 | tf_op jit(solution)/shard_map/attend/pallas_call | solution.py:555
  25.0 0.0 copy-start.1
  25.0 0.0 copy-start.2
  25.0 0.0 copy-start.12
  25.0 2.6 %all-gather = bf16[256,1792]{1,0:T(8,128)(2,1)S(1)} all-gather(bf16[128,1792]{1,0:T(8,128)(2,1)S(1)} %attend.1), channel_id=2, replica_groups={{0,1},{2,3},{4,5},{6,7},{8,9},{10,11},{12,13},{14,15},{16,17},{18,19},{..., dimensions={0}, use_global_device_ids=true | all-gather | bytes 1376256 | tf_op jit(solution)/shard_map/all_gather | solution.py:548
  27.6 0.1 dynamic-slice_reduce_fusion.1
  27.7 8.3 %all-gather.1 = bf16[128,1792]{1,0:T(8,128)(2,1)S(1)} all-gather(bf16[64,1792]{1,0:T(8,128)(2,1)S(1)} %dynamic-slice_reduce_fusion.1), channel_id=3, replica_groups={{0,2},{1,3},{4,6},{5,7},{8,10},{9,11},{12,14},{13,15},{16,18},{17,19},{..., dimensions={0}, use_global_device_ids=true | all-gather | bytes 688128 | tf_op jit(solution)/shard_map/all_gather | solution.py:551
  36.0 0.1 reduce_sum.49
  36.1 2.1 %all_gather.34.sum_ref = bf16[128,1792]{1,0:T(8,128)(2,1)S(1)} all-gather(bf16[64,1792]{1,0:T(8,128)(2,1)S(1)} %reduce_sum.49), channel_id=1, replica_groups={{0,1},{2,3},{4,5},{6,7},{8,9},{10,11},{12,13},{14,15},{16,17},{18,19},{..., dimensions={0}, use_global_device_ids=true | all-gather | bytes 688128 | tf_op jit(solution)/shard_map/all_gather | solution.py:553
  38.2 0.0 copy-start.3
  38.3 1.5 %copy-done.3 = bf16[1792,512]{1,0:T(8,128)(2,1)S(1)} copy-done((bf16[1792,512]{1,0:T(8,128)(2,1)S(1)}, bf16[1792,512]{1,0:T(8,128)(2,1)}, u32[]{:S(2)}) %copy-start.3) | copy-done | bytes 1835032
  39.7 1.5 %copy-done.4 = bf16[512,1792]{1,0:T(8,128)(2,1)S(1)} copy-done((bf16[512,1792]{1,0:T(8,128)(2,1)S(1)}, bf16[512,1792]{1,0:T(8,128)(2,1)}, u32[]{:S(2)}) %copy-start.4) | copy-done | bytes 1835032
  41.2 1.2 %mlp.1 = (f32[128,1792]{1,0:T(8,128)S(1)}, bf16[128,1792]{1,0:T(8,128)(2,1)S(1)}) custom-call(bf16[128,1792]{1,0:T(8,128)(2,1)S(1)} %bitcast.16, bf16[128,1792]{1,0:T(8,128)(2,1)S(1)} %all_gather.34.sum_ref, f32[1792]{0:T(1024)S(1)} %copy-done.12, bf16[1792,512]{1,0:T(8,128)(2,1)S(1)} %copy-done.2, bf16[1792,512]{1,0:T(8,128)(2,1)S(1)} %copy-done.3, ...), custom_call_target="tpu_custom_call" | custom-call | bytes 1080 | tf_op jit(solution)/shard_map/mlp/pallas_call | solution.py:568
  42.5 2.6 %all-gather.2 = bf16[256,1792]{1,0:T(8,128)(2,1)S(1)} all-gather(bf16[128,1792]{1,0:T(8,128)(2,1)S(1)} %get-tuple-element.103), channel_id=4, replica_groups={{0,1},{2,3},{4,5},{6,7},{8,9},{10,11},{12,13},{14,15},{16,17},{18,19},{..., dimensions={0}, use_global_device_ids=true | all-gather | bytes 1376256 | tf_op jit(solution)/shard_map/all_gather | solution.py:548
  45.1 0.1 dynamic-slice_reduce_fusion
  45.1 0.0 collective-permute-done.1.rest_5_
  45.2 1.8 %collective-permute-done.rest_4_ = bf16[2,976,128]{2,1,0:T(8,128)(2,1)} collective-permute-done((bf16[2,976,128]{2,1,0:T(8,128)(2,1)}, bf16[2,976,128]{2,1,0:T(8,128)(2,1)}, u32[]{:S(2)}, u32[]{:S(2)}) %collective-permute-start) | collective-permute-done | bytes 499744 | tf_op jit(solution)/shard_map/ppermute | solution.py:527
  47.0 0.0 collective-permute-done.2.rest_2_
  47.0 0.0 collective-permute-done.3.rest_1_
  47.0 6.3 %collective-permute-done.4.rest_3_ = bf16[2,976,128]{2,1,0:T(8,128)(2,1)} collective-permute-done((bf16[2,976,128]{2,1,0:T(8,128)(2,1)}, bf16[2,976,128]{2,1,0:T(8,128)(2,1)}, u32[]{:S(2)}, u32[]{:S(2)}) %collective-permute-start.4) | collective-permute-done | bytes 499744 | tf_op jit(solution)/shard_map/ppermute | solution.py:527
  53.4 1.7 %slice.3 = bf16[1,976,128]{2,1,0:T(8,128)(2,1)} slice(bf16[2,976,128]{2,1,0:T(8,128)(2,1)} %collective-permute-done.rest_4_), slice={[1:2], [0:976], [0:128]} | slice | bytes 499712 | tf_op jit(solution)/shard_map/slice | solution.py:582
  55.0 1.6 %collective-permute-start.7 = (bf16[1,976,128]{2,1,0:T(8,128)(2,1)}, bf16[1,976,128]{2,1,0:T(8,128)(2,1)S(1)}, u32[]{:S(2)}, u32[]{:S(2)}) collective-permute-start(bf16[1,976,128]{2,1,0:T(8,128)(2,1)} %slice.3), channel_id=1, source_target_pairs={{0,12},{4,8},{8,4},{12,0},{16,28},{20,24},{24,20},{28,16},{1,13},{... | collective-permute-start | bytes 749576 | tf_op jit(solution)/shard_map/ppermute | solution.py:527
  56.6 1.4 %collective-permute-start.6 = (bf16[1,976,128]{2,1,0:T(8,128)(2,1)}, bf16[1,976,128]{2,1,0:T(8,128)(2,1)S(1)}, u32[]{:S(2)}, u32[]{:S(2)}) collective-permute-start(bf16[1,976,128]{2,1,0:T(8,128)(2,1)} %slice.3), channel_id=1, source_target_pairs={{0,8},{4,12},{8,0},{12,4},{16,24},{20,28},{24,16},{28,20},{1,9},{5... | collective-permute-start | bytes 749576 | tf_op jit(solution)/shard_map/ppermute | solution.py:527
  58.0 0.5 collective-permute-start.5
  58.5 2.4 %collective-permute-start.8 = (bf16[1,976,128]{2,1,0:T(8,128)(2,1)}, bf16[1,976,128]{2,1,0:T(8,128)(2,1)S(1)}, u32[]{:S(2)}, u32[]{:S(2)}) collective-permute-start(bf16[1,976,128]{2,1,0:T(8,128)(2,1)} %get-tuple-element.113), channel_id=1, source_target_pairs={{0,24},{4,28},{8,16},{12,20},{16,8},{20,12},{24,0},{28,4},{1,25},{... | collective-permute-start | bytes 749576 | tf_op jit(solution)/shard_map/ppermute | solution.py:527
  60.9 0.9 collective-permute-start.9
  61.8 6.7 %all-gather.3 = bf16[128,1792]{1,0:T(8,128)(2,1)S(1)} all-gather(bf16[64,1792]{1,0:T(8,128)(2,1)S(1)} %dynamic-slice_reduce_fusion), channel_id=5, replica_groups={{0,2},{1,3},{4,6},{5,7},{8,10},{9,11},{12,14},{13,15},{16,18},{17,19},{..., dimensions={0}, use_global_device_ids=true | all-gather | bytes 688128 | tf_op jit(solution)/shard_map/all_gather | solution.py:551
  68.5 0.1 reduce_sum.51
  68.6 2.1 %all_gather.39.sum_ref = bf16[128,1792]{1,0:T(8,128)(2,1)S(1)} all-gather(bf16[64,1792]{1,0:T(8,128)(2,1)S(1)} %reduce_sum.51), channel_id=1, replica_groups={{0,1},{2,3},{4,5},{6,7},{8,9},{10,11},{12,13},{14,15},{16,17},{18,19},{..., dimensions={0}, use_global_device_ids=true | all-gather | bytes 688128 | tf_op jit(solution)/shard_map/all_gather | solution.py:553
  70.7 0.0 collective-permute-done.7
  70.7 1.9 %collective-permute-done.5 = bf16[1,976,128]{2,1,0:T(8,128)(2,1)} collective-permute-done((bf16[1,976,128]{2,1,0:T(8,128)(2,1)}, bf16[1,976,128]{2,1,0:T(8,128)(2,1)}, u32[]{:S(2)}, u32[]{:S(2)}) %collective-permute-start.5) | collective-permute-done | bytes 249888 | tf_op jit(solution)/shard_map/ppermute | solution.py:527
  72.6 9.5 %collective-permute-done.9.rest_7_ = bf16[1,976,128]{2,1,0:T(8,128)(2,1)S(1)} collective-permute-done((bf16[1,976,128]{2,1,0:T(8,128)(2,1)}, bf16[1,976,128]{2,1,0:T(8,128)(2,1)S(1)}, u32[]{:S(2)}, u32[]{:S(2)}) %collective-permute-start.9) | collective-permute-done | bytes 249888 | tf_op jit(solution)/shard_map/ppermute | solution.py:527
  82.2 1.5 %close.1 = (bf16[128,1792]{1,0:T(8,128)(2,1)}, s32[1]{0:T(128)}) custom-call(f32[128,1792]{1,0:T(8,128)S(1)} %get-tuple-element.102.residual_ref, bf16[128,1792]{1,0:T(8,128)(2,1)S(1)} %all_gather.39.sum_ref, bf16[2,976,128]{2,1,0:T(8,128)(2,1)S(1)} %copy-done.13, bf16[2,976,128]{2,1,0:T(8,128)(2,1)} %collective-permute-done.3.rest_1_, ...), custom_call_target="tpu_custom_call" | custom-call | bytes 360 | tf_op jit(solution)/shard_map/close/pallas_call | solution.py:594
  84.4 7.3 %conditional.1 = ((f32[3822,4,128]{2,1,0:T(4,128)}, f32[4,16,273]{2,1,0:T(8,128)}, bf16[16,2,448]{2,1,0:T(2,128)(2,1)})) conditional(s32[]{:T(128)} %bitcast.10, (bf16[2,976,128]{2,1,0:T(8,128)(2,1)S(1)}, bf16[2,976,128]{2,1,0:T(8,128)(2,1)}, bf16[2,976,128]{2,1,0:T(8,128)(2,1)}, bf16[2,976,128]{2,1,0:T(8,128)(2,1)}, bf16[2,976,128]{2,1,0:T(8,128)(2,1)}, ...), branch_computations={%region_4.5_spmd, %region_5.6_spmd} | conditional | bytes 4000224 | solution.py:634
  84.4 7.1 %settle.1 = (f32[3822,4,128]{2,1,0:T(4,128)}, f32[4,16,273]{2,1,0:T(8,128)}, bf16[16,2,448]{2,1,0:T(2,128)(2,1)}) custom-call(bf16[2,976,128]{2,1,0:T(8,128)(2,1)S(1)} %get-tuple-element.40.rest_0_, bf16[2,976,128]{2,1,0:T(8,128)(2,1)} %get-tuple-element.41.rest_1_, bf16[2,976,128]{2,1,0:T(8,128)(2,1)} %get-tuple-element.42.rest_2_, ...), custom_call_target="tpu_custom_call" | custom-call | bytes 2520 | tf_op jit(solution)/shard_map/cond/branch_0_fun/settle/pallas_call | solution.py:608
  (17 shorter events, 0.0 us)
Async XLA Ops:
  0.6 17.8 %copy-start.5 = (bf16[128,1792]{1,0:T(8,128)(2,1)S(1)}, bf16[128,1792]{1,0:T(8,128)(2,1)}, u32[]{:S(2)}) copy-start(bf16[128,1792]{1,0:T(8,128)(2,1)} %constant.36.clone.rest_9_.table_ref) | copy-start | bytes 1376260
  0.6 17.8 %copy-start.6 = (bf16[448,1792]{1,0:T(8,128)(2,1)S(1)}, bf16[448,1792]{1,0:T(8,128)(2,1)}, u32[]{:S(2)}) copy-start(bf16[448,1792]{1,0:T(8,128)(2,1)} %wo_ref.1) | copy-start | bytes 4816900
  0.7 17.8 %copy-start.7 = (f32[4,8,273]{2,1,0:T(8,128)S(1)}, f32[4,8,273]{2,1,0:T(8,128)}, u32[]{:S(2)}) copy-start(f32[4,8,273]{2,1,0:T(8,128)} %norm_ref.1) | copy-start | bytes 104836
  0.7 17.8 %copy-start.9 = (f32[8,896]{1,0:T(8,128)S(1)}, f32[8,896]{1,0:T(8,128)}, u32[]{:S(2)}) copy-start(f32[8,896]{1,0:T(8,128)} %constant.37.clone.rest_10_.bias_ref) | copy-start | bytes 86020
  11.0 34.2 %collective-permute-start.1 = (bf16[1,976,128]{2,1,0:T(8,128)(2,1)}, bf16[1,976,128]{2,1,0:T(8,128)(2,1)S(1)}, u32[]{:S(2)}, u32[]{:S(2)}) collective-permute-start(bf16[1,976,128]{2,1,0:T(8,128)(2,1)} %get-tuple-element.105), channel_id=1, source_target_pairs={{0,20},{4,16},{8,28},{12,24},{16,4},{20,0},{24,12},{28,8},{1,21},{... | collective-permute-start | bytes 749576 | tf_op jit(solution)/shard_map/ppermute | solution.py:527
  14.6 32.4 %collective-permute-start = (bf16[2,976,128]{2,1,0:T(8,128)(2,1)}, bf16[2,976,128]{2,1,0:T(8,128)(2,1)}, u32[]{:S(2)}, u32[]{:S(2)}) collective-permute-start(bf16[2,976,128]{2,1,0:T(8,128)(2,1)} %get-tuple-element.104), channel_id=1, source_target_pairs={{0,16},{4,20},{8,24},{12,28},{16,0},{20,4},{24,8},{28,12},{1,17},{... | collective-permute-start | bytes 1499144 | tf_op jit(solution)/shard_map/ppermute | solution.py:527
  14.9 32.1 %collective-permute-start.2 = (bf16[2,976,128]{2,1,0:T(8,128)(2,1)}, bf16[2,976,128]{2,1,0:T(8,128)(2,1)}, u32[]{:S(2)}, u32[]{:S(2)}) collective-permute-start(bf16[2,976,128]{2,1,0:T(8,128)(2,1)} %get-tuple-element.106), channel_id=1, source_target_pairs={{0,8},{4,12},{8,0},{12,4},{16,24},{20,28},{24,16},{28,20},{1,9},{5... | collective-permute-start | bytes 1499144 | tf_op jit(solution)/shard_map/ppermute | solution.py:527
  15.4 31.6 %collective-permute-start.3 = (bf16[2,976,128]{2,1,0:T(8,128)(2,1)}, bf16[2,976,128]{2,1,0:T(8,128)(2,1)}, u32[]{:S(2)}, u32[]{:S(2)}) collective-permute-start(bf16[2,976,128]{2,1,0:T(8,128)(2,1)} %get-tuple-element.107), channel_id=1, source_target_pairs={{0,4},{4,0},{8,12},{12,8},{16,20},{20,16},{24,28},{28,24},{1,5},{5... | collective-permute-start | bytes 1499144 | tf_op jit(solution)/shard_map/ppermute | solution.py:527
  15.7 37.7 %collective-permute-start.4 = (bf16[2,976,128]{2,1,0:T(8,128)(2,1)}, bf16[2,976,128]{2,1,0:T(8,128)(2,1)}, u32[]{:S(2)}, u32[]{:S(2)}) collective-permute-start(bf16[2,976,128]{2,1,0:T(8,128)(2,1)} %get-tuple-element.108), channel_id=1, source_target_pairs={{0,12},{4,8},{8,4},{12,0},{16,28},{20,24},{24,20},{28,16},{1,13},{... | collective-permute-start | bytes 1499144 | tf_op jit(solution)/shard_map/ppermute | solution.py:527
  18.4 1.5 %copy-start = (bf16[8,4,240,128]{3,2,1,0:T(8,128)(2,1)S(1)}, bf16[8,4,240,128]{3,2,1,0:T(8,128)(2,1)}, u32[]{:S(2)}) copy-start(bf16[8,4,240,128]{3,2,1,0:T(8,128)(2,1)} %get-tuple-element.101.start_ref) | copy-start | bytes 5898244
  20.0 0.9 copy-start.8
  20.9 0.8 copy-start.10
  21.6 0.8 copy-start.11
  25.0 13.3 %copy-start.1 = (bf16[8,16,1792]{2,1,0:T(8,128)(2,1)S(1)}, bf16[8,16,1792]{2,1,0:T(8,128)(2,1)}, u32[]{:S(2)}) copy-start(bf16[8,16,1792]{2,1,0:T(8,128)(2,1)} %param.20) | copy-start | bytes 1376260
  25.0 13.2 %copy-start.2 = (bf16[1792,512]{1,0:T(8,128)(2,1)S(1)}, bf16[1792,512]{1,0:T(8,128)(2,1)}, u32[]{:S(2)}) copy-start(bf16[1792,512]{1,0:T(8,128)(2,1)} %wg_ref.1) | copy-start | bytes 5505028
  25.0 13.2 %copy-start.12 = (f32[1792]{0:T(1024)S(1)}, f32[1792]{0:T(1024)}, u32[]{:S(2)}) copy-start(f32[1792]{0:T(1024)} %gain_ref.1) | copy-start | bytes 21508
  38.2 1.5 %copy-start.3 = (bf16[1792,512]{1,0:T(8,128)(2,1)S(1)}, bf16[1792,512]{1,0:T(8,128)(2,1)}, u32[]{:S(2)}) copy-start(bf16[1792,512]{1,0:T(8,128)(2,1)} %wu_ref.1) | copy-start | bytes 5505028
  39.7 1.5 %copy-start.4 = (bf16[512,1792]{1,0:T(8,128)(2,1)S(1)}, bf16[512,1792]{1,0:T(8,128)(2,1)}, u32[]{:S(2)}) copy-start(bf16[512,1792]{1,0:T(8,128)(2,1)} %wd_ref.1) | copy-start | bytes 5505028
  42.5 39.7 %copy-start.13 = (bf16[2,976,128]{2,1,0:T(8,128)(2,1)S(1)}, bf16[2,976,128]{2,1,0:T(8,128)(2,1)}, u32[]{:S(2)}) copy-start(bf16[2,976,128]{2,1,0:T(8,128)(2,1)} %get-tuple-element.116.rest_0_) | copy-start | bytes 1499140
  55.0 15.7 %collective-permute-start.7 = (bf16[1,976,128]{2,1,0:T(8,128)(2,1)}, bf16[1,976,128]{2,1,0:T(8,128)(2,1)S(1)}, u32[]{:S(2)}, u32[]{:S(2)}) collective-permute-start(bf16[1,976,128]{2,1,0:T(8,128)(2,1)} %slice.3), channel_id=1, source_target_pairs={{0,12},{4,8},{8,4},{12,0},{16,28},{20,24},{24,20},{28,16},{1,13},{... | collective-permute-start | bytes 749576 | tf_op jit(solution)/shard_map/ppermute | solution.py:527
  56.6 14.1 %collective-permute-start.6 = (bf16[1,976,128]{2,1,0:T(8,128)(2,1)}, bf16[1,976,128]{2,1,0:T(8,128)(2,1)S(1)}, u32[]{:S(2)}, u32[]{:S(2)}) collective-permute-start(bf16[1,976,128]{2,1,0:T(8,128)(2,1)} %slice.3), channel_id=1, source_target_pairs={{0,8},{4,12},{8,0},{12,4},{16,24},{20,28},{24,16},{28,20},{1,9},{5... | collective-permute-start | bytes 749576 | tf_op jit(solution)/shard_map/ppermute | solution.py:527
  58.0 14.6 %collective-permute-start.5 = (bf16[1,976,128]{2,1,0:T(8,128)(2,1)}, bf16[1,976,128]{2,1,0:T(8,128)(2,1)}, u32[]{:S(2)}, u32[]{:S(2)}) collective-permute-start(bf16[1,976,128]{2,1,0:T(8,128)(2,1)} %slice.3), channel_id=1, source_target_pairs={{0,4},{4,0},{8,12},{12,8},{16,20},{20,16},{24,28},{28,24},{1,5},{5... | collective-permute-start | bytes 749576 | tf_op jit(solution)/shard_map/ppermute | solution.py:527
  58.5 14.1 %collective-permute-start.8 = (bf16[1,976,128]{2,1,0:T(8,128)(2,1)}, bf16[1,976,128]{2,1,0:T(8,128)(2,1)S(1)}, u32[]{:S(2)}, u32[]{:S(2)}) collective-permute-start(bf16[1,976,128]{2,1,0:T(8,128)(2,1)} %get-tuple-element.113), channel_id=1, source_target_pairs={{0,24},{4,28},{8,16},{12,20},{16,8},{20,12},{24,0},{28,4},{1,25},{... | collective-permute-start | bytes 749576 | tf_op jit(solution)/shard_map/ppermute | solution.py:527
  60.9 21.3 %collective-permute-start.9 = (bf16[1,976,128]{2,1,0:T(8,128)(2,1)}, bf16[1,976,128]{2,1,0:T(8,128)(2,1)S(1)}, u32[]{:S(2)}, u32[]{:S(2)}) collective-permute-start(bf16[1,976,128]{2,1,0:T(8,128)(2,1)} %get-tuple-element.114), channel_id=1, source_target_pairs={{0,28},{4,24},{8,20},{12,16},{16,12},{20,8},{24,4},{28,0},{1,29},{... | collective-permute-start | bytes 749576 | tf_op jit(solution)/shard_map/ppermute | solution.py:527

commit v3 on v2

--- a/solution.py
+++ b/solution.py
@@ -117,17 +117,10 @@
     pieces, rest = rest[:made], rest[made:]
     (q_ref, k_ref, v_ref, start_ref), rest = rest[:4], rest[4:]
     held, rest = rest[:loaded], rest[loaded:]
-    flat, padded, mixed, phi, plain, turned, edges, extra, stage, begun, none, state_sem, load_sem, none_sem, out_sem, begun_sem = rest
+    flat, padded, mixed, phi, plain, turned, edges, extra, stage, begun, kept_q, kept_k, kept_v, none, state_sem, load_sem, none_sem, out_sem, begun_sem = rest
     fetches = [pltpu.make_async_copy(fetched[i], held[i], load_sem.at[i]) for i in range(loaded)]
     for fetch in fetches:
         fetch.start()
-    lines = state_ref.shape[0]
-    loads = [
-        pltpu.make_async_copy(state_ref.at[:, h], flat.at[h, pl.ds(0, lines)], state_sem.at[h])
-        for h in range(heads)
-    ]
-    for load in loads:
-        load.start()
     (
         owner_ref, accepted_ref, tokens_ref, edge_ref, gain_ref, conv_ref,
         wq_ref, wk_ref, wv_ref, table_ref, bias_ref, norm_ref,
@@ -171,14 +164,32 @@
         blend = normed + convolved / (1.0 + jnp.exp(-normed))
         mixed[steps * r : steps * (r + 1), :] = blend.astype(BF16)
 
+    lines = state_ref.shape[0]
+    cuts = [0] + [-(-(line_of(r)[0] + 3) // 8) * 8 for r in range(2, requests, 2)] + [lines]
+    loads = [
+        [
+            pltpu.make_async_copy(
+                state_ref.at[pl.ds(begin, end - begin), h], flat.at[h, pl.ds(begin, end - begin)], state_sem.at[i, h]
+            )
+            for h in range(heads)
+        ]
+        for i, (begin, end) in enumerate(zip(cuts, cuts[1:]))
+    ]
+    for part in loads:
+        for load in part:
+            load.start()
     for fetch in fetches[6:]:
         fetch.wait()
     queries = dot_nt(mixed[...], wq_ref[...]).astype(BF16)
     keys = dot_nt(mixed[...], wk_ref[...]).astype(BF16)
     values = dot_nt(mixed[...], wv_ref[...]).astype(BF16)
-    q_ref[...] = queries
-    k_ref[...] = keys
-    v_ref[...] = values
+    keeps = []
+    for i, (place, rows, x) in enumerate(
+        ((q_ref, kept_q, queries), (k_ref, kept_k, keys), (v_ref, kept_v, values))
+    ):
+        rows[...] = x
+        keeps.append(pltpu.make_async_copy(rows, place, begun_sem.at[requests + i]))
+        keeps[-1].start()
 
     for h in range(heads):
         key = keys[:, FD * h : FD * (h + 1)]
@@ -202,13 +213,14 @@
     lane_ids = lax.broadcasted_iota(jnp.int32, (LINES, 128), 1)
     step_ids = lax.broadcasted_iota(jnp.int32, (steps, 1), 0)
     edge_lines = -(-column_width // 128)
-    for load in loads:
-        load.wait()
     for blank in blanks:
         blank.wait()
-    sends, keeps = [], []
+    sends = []
     for r in range(requests):
         owner = owner_ref[r]
+        if r % 2 == 0:
+            for load in loads[r // 2]:
+                load.wait()
         taken = (step_ids < accepted_ref[r]).astype(F32)
         first, shift = line_of(r)
         extra[...] = jnp.zeros((EXTRA, 128), F32)
@@ -253,7 +265,7 @@
         else:
             far = owner ^ lax.axis_index("req")
             routes = [((ranks[r] == 0) & (far == k), pieces[k].at[0]) for k in range(count)]
-            routes += [(seconds[r], pieces[k].at[1]) for k in range(5)]
+            routes += [(seconds[r], pieces[k].at[1]) for k in (0, 1, 2, 4)]
             routes += [(ranks[r] == 1, pieces[count].at[owner])]
         for i, (chosen, place) in enumerate(routes):
             send = pltpu.make_async_copy(stage.at[r], place, out_sem.at[r, i])
@@ -327,6 +339,18 @@
     part_ref[...] = dot_nn(hidden, wd_ref[...]).astype(BF16)
 
 
+def relay_kernel(across_ref, beside_ref, passed_ref, both_ref, sems):
+    moves = [
+        pltpu.make_async_copy(across_ref.at[1], passed_ref.at[0], sems.at[0]),
+        pltpu.make_async_copy(across_ref.at[1], both_ref.at[0], sems.at[1]),
+        pltpu.make_async_copy(beside_ref.at[1], both_ref.at[1], sems.at[2]),
+    ]
+    for move in moves:
+        move.start()
+    for move in moves:
+        move.wait()
+
+
 def close_kernel(residual_ref, sum_ref, *rest):
     marks, (out_ref, several_ref, lines, sems) = rest[:-4], rest[-4:]
     reads = [
@@ -352,11 +376,13 @@
     body = heads * LINES
     here = lax.axis_index("req")
     inputs, rest = rest[:arrivals], rest[arrivals:]
-    state_ref, norm_ref, edge_ref, stage, flat, shifted, table, in_sem, out_sem = rest
-    loads = []
+    state_ref, norm_ref, edge_ref, stage, marks, flat, table, alive, in_sem, mark_sem, out_sem = rest
+    loads, reads = [], []
 
     def load(place, lane):
-        loads.append(pltpu.make_async_copy(place, stage.at[lane], in_sem.at[len(loads)]))
+        at = len(loads)
+        loads.append(pltpu.make_async_copy(place, stage.at[lane], in_sem.at[lane]))
+        reads.append(pltpu.make_async_copy(place.at[pl.ds(body, EXTRA)], marks.at[lane], mark_sem.at[at]))
 
     for i in range(count):
         if pair_cap == 1:
@@ -365,31 +391,32 @@
             source = here ^ i
             load(inputs[i].at[0], 2 * source)
             if direct:
-                load(inputs[i].at[1] if i < 5 else inputs[count + i - 5].at[0], 2 * source + 1)
+                at, j = {3: (count, 1), 5: (count, 0), 6: (count + 1, 0), 7: (count + 2, 0)}.get(i, (i, 1))
+                load(inputs[at].at[j], 2 * source + 1)
             else:
                 load(inputs[count].at[i], 2 * i + 1)
-    for copy in loads:
+    for copy in reads + loads:
         copy.start()
     norm_ref[...] = jnp.zeros(norm_ref.shape, F32)
     edge_ref[...] = jnp.zeros(edge_ref.shape, BF16)
-    for copy in loads:
+    for copy in reads:
         copy.wait()
     one_row = lax.broadcasted_iota(jnp.int32, (EXTRA, 128), 0)
     one_line = lax.broadcasted_iota(jnp.int32, (EXTRA, 128), 1)
     mark = (one_row == EXTRA - 1) & (one_line == 127)
     filled = jnp.int32(0)
     for lane in range(lanes):
-        block = jnp.where(mark, stage[lane, body : body + EXTRA, :].astype(F32), 0.0)
-        live = jnp.sum(block).astype(jnp.int32) == here + 1
+        block = jnp.where(mark, marks[lane].astype(F32), 0.0)
+        live = (jnp.sum(block).astype(jnp.int32) == here + 1).astype(jnp.int32)
         table[filled] = lane
-        filled = filled + live.astype(jnp.int32)
+        alive[lane] = live
+        filled = filled + live
 
     total = state_ref.shape[0]
     width = edge_ref.shape[2]
     edge_lines = -(-width // 128)
     lane_ids = lax.broadcasted_iota(jnp.int32, (LINES, 128), 1)
     head_ids = lax.broadcasted_iota(jnp.int32, (8, 128), 1)
-    head_rows = lax.broadcasted_iota(jnp.int32, (8, 128), 0)
     stores = []
     done = 0
     for s in range(CAP):
@@ -400,7 +427,8 @@
         @pl.when(s < filled)
         def _():
             lane = table[s]
-            extra = stage[lane, body : body + EXTRA, :].astype(F32)
+            pltpu.make_async_copy(stage.at[lane], stage.at[lane], in_sem.at[lane]).wait()
+            extra = marks[lane].astype(F32)
             pairs = [[], []]
             for j in range(2):
                 for c in range(edge_lines):
@@ -421,12 +449,10 @@
                     axis=1,
                 )
                 if shift:
-                    shifted[h, 8 : 8 + LINES, :] = rows
-                    before = shifted[h, 7 : 7 + LINES, :]
-                    rows = pltpu.roll(jnp.where(lane_ids < 128 - shift, rows, before), shift, 1)
-                    old = flat[h, first : first + 1, :]
-                    flat[h, first + 1 : last, :] = rows[1:span]
-                    flat[h, first : first + 1, :] = jnp.where(head_ids[:1] < shift, old, rows[:1])
+                    rows = pltpu.roll(rows, shift, 1)
+                    whole = span if span < LINES else LINES - 1
+                    pltpu.store(flat.at[h, pl.ds(first, whole)], rows[:whole], mask=lane_ids[:whole] >= shift)
+                    pltpu.store(flat.at[h, pl.ds(first + 1, span - 1)], rows[: span - 1], mask=lane_ids[: span - 1] < shift)
                 else:
                     flat[h, first:last, :] = rows[:span]
 
@@ -450,6 +476,10 @@
             store.start()
             stores.append(store)
         done = until
+    for lane in range(lanes):
+        @pl.when(alive[lane] == 0)
+        def _():
+            pltpu.make_async_copy(stage.at[lane], stage.at[lane], in_sem.at[lane]).wait()
     for store in stores:
         store.wait()
 
@@ -480,7 +510,7 @@
 
     flat_tokens = tokens.reshape(rows_all, width)
     lined_state = jnp.swapaxes(state_start.reshape(heads, lines, 128), 0, 1)
-    held = [count] if pair_cap == 1 else [2] * 5 + [1] * 3 + [count]
+    held = [count] if pair_cap == 1 else [2, 2, 2, 1, 2, 1, 1, 1, count]
     piece_shapes = [jax.ShapeDtypeStruct((size, payload, 128), BF16) for size in held]
     fetched = [
         owner, accepted, flat_tokens, conv_edge, attn_gain, conv_weight,
@@ -496,7 +526,7 @@
             jax.ShapeDtypeStruct((requests, heads, LINES, 128), BF16),
         ],
         in_specs=[hbm] * (1 + len(fetched)),
-        out_specs=[anywhere] * len(held) + [vmem] * 3 + [anywhere],
+        out_specs=[anywhere] * (len(held) + 4),
         scratch_shapes=[pltpu.SMEM(x.shape, x.dtype) for x in fetched[:2]]
         + [pltpu.VMEM(x.shape, x.dtype) for x in fetched[2:]]
         + [
@@ -510,12 +540,15 @@
             pltpu.VMEM((EXTRA, 128), F32),
             pltpu.VMEM((requests, payload, 128), BF16),
             pltpu.VMEM((requests, heads, LINES, 128), BF16),
+            pltpu.VMEM((rows_all, heads * FD), BF16),
+            pltpu.VMEM((rows_all, heads * FD), BF16),
+            pltpu.VMEM((rows_all, heads * DV), BF16),
             pltpu.VMEM((EXTRA, 128), BF16),
-            pltpu.SemaphoreType.DMA((heads,)),
+            pltpu.SemaphoreType.DMA((requests // 2, heads)),
             pltpu.SemaphoreType.DMA((len(fetched),)),
             pltpu.SemaphoreType.DMA((sum(held),)),
             pltpu.SemaphoreType.DMA((requests, count + 6)),
-            pltpu.SemaphoreType.DMA((requests,)),
+            pltpu.SemaphoreType.DMA((requests + 3,)),
         ],
         compiler_params=limit(vmem_limit_bytes=60 * 2**20),
         cost_estimate=cost(8),
@@ -578,9 +611,19 @@
 
     def half_way(x):
         if pair_cap > 1:
-            x = wave(x, (4, 5, 2, 1, 3), (4, 5, 2, 1, 3), (6, 7))
-            passed = arrived[4][1:2]
-            forward.update({far: swapped(passed, far) for far in (1, 2, 3)})
+            x = wave(x, (4, 2, 1, 5, 3), (4, 2, 1, 5, 3), (6, 7))
+            passed, both = pl.pallas_call(
+                relay_kernel,
+                out_shape=[jax.ShapeDtypeStruct((size, payload, 128), BF16) for size in (1, 2)],
+                in_specs=[anywhere] * 2,
+                out_specs=[anywhere] * 2,
+                scratch_shapes=[pltpu.SemaphoreType.DMA((3,))],
+                compiler_params=limit(),
+                cost_estimate=cost(1),
+                name="relay",
+            )(arrived[4], arrived[2])
+            forward.update({far: swapped(passed, far) for far in (2, 3)})
+            forward[1] = swapped(both, 1)
         return x
 
     total = summed(part, half_way)
@@ -616,9 +659,11 @@
             out_specs=[anywhere, vmem, vmem],
             scratch_shapes=[
                 pltpu.VMEM((count * pair_cap, payload, 128), BF16),
+                pltpu.VMEM((count * pair_cap, EXTRA, 128), BF16),
                 pltpu.VMEM((heads, out_lines, 128), F32),
-                pltpu.VMEM((heads, LINES + 16, 128), F32),
                 pltpu.SMEM((count * pair_cap + 1,), jnp.int32),
+                pltpu.SMEM((count * pair_cap,), jnp.int32),
+                pltpu.SemaphoreType.DMA((count * pair_cap,)),
                 pltpu.SemaphoreType.DMA((count * pair_cap,)),
                 pltpu.SemaphoreType.DMA((CAP, heads)),
             ],

time: 93.5 us -> 85.5 us (0.914)
  waiting for transfers between devices: 19.7 us -> 14.1 us
  local copies, waits for them, and re-layouts: 8.65 us -> 7 us
    ppermute x10, waiting for transfers between devices: 19.7 us -> 14.1 us  [swapped(): return lax.ppermute(x, 'req', [(i, i ^ far) for i in range(count)])]
    slice x1 -> x0, local copies, waits for them, and re-layouts: 1.66 us -> none  [half_way(): passed = arrived[4][1:2]]
    pallas_call x1, Pallas kernels: 10.3 us -> 8.96 us  [shards(): pl.pallas_call(functools.partial(pack_kernel, heads, count, pair_cap, tp_...]
    pallas_call x0 -> x1, Pallas kernels: none -> 1.21 us  [half_way(): pl.pallas_call(relay_kernel, out_shape=[jax.ShapeDtypeStruct((size, paylo...]
  transfers between devices with their start and end apart: 10 -> 10, of which waited for: 4 -> 4; matrix products, arithmetic and copies ran while one was open for 0% -> 1% of each run, Pallas kernels for 4% -> 4%
where the time goes in v3:
time: 85.5 us; the launch traced here: 84.6 us
  blocking collectives  24.5 us (29%)
  Pallas kernels  22.1 us (26%)
  waiting for transfers between devices  14.1 us (16%)
  starting transfers between devices  13.9 us (16%)
  local copies, waits for them, and re-layouts  7 us (8%)
  between operations  1.62 us (2%)
  other arithmetic  1.02 us (1%)
    all_gather x2, blocking collectives, summed(): mine = lax.all_gather(mine, 'tp', axis=0, axis_index_groups=chips)  15 us
    ppermute x10, waiting for transfers between devices, swapped(): return lax.ppermute(x, 'req', [(i, i ^ far) for i in range(count)])  14.1 us
    ppermute x10, starting transfers between devices, swapped(): return lax.ppermute(x, 'req', [(i, i ^ far) for i in range(count)])  13.9 us
    pallas_call x1, Pallas kernels, shards(): pl.pallas_call(functools.partial(pack_kernel, heads, count, pair_cap, tp_...  8.96 us
    unnamed x28, local copies, waits for them, and re-layouts  7 us
    pallas_call x1, Pallas kernels, settled(): pl.pallas_call(functools.partial(settle_kernel, heads, count, pair_cap, d...  6.6 us
    all_gather x2, blocking collectives, summed(): both = lax.all_gather(part, 'tp', axis=0, axis_index_groups=cores)  5.06 us
    all_gather x2, blocking collectives, summed(): lax.all_gather(mine, 'tp', axis=0, tiled=True, axis_index_groups=cores)  4.47 us
  transfers between devices with their start and end apart: 10, of which 4 were waited for; matrix products, arithmetic and copies ran while one was open for 1% of the time, Pallas kernels for 4%

profile of v3, /device:TPU:8, one launch (start us, length us, event | category | flops | bytes accessed | tf_op | source)
XLA Modules:
  0.0 84.6 jit_solution(9662152700630724488)
XLA Ops:
  0.6 0.0 copy-start.5
  0.7 0.0 copy-start.9
  0.7 9.0 %pack.1 = (bf16[2,976,128]{2,1,0:T(8,128)(2,1)}, bf16[2,976,128]{2,1,0:T(8,128)(2,1)}, bf16[2,976,128]{2,1,0:T(8,128)(2,1)}, bf16[1,976,128]{2,1,0:T(8,128)(2,1)...) custom-call(f32[1911,4,128]{2,1,0:T(4,128)} %bitcast.17, ...), custom_call_target="tpu_custom_call" | custom-call | bytes 2880 | tf_op jit(solution)/shard_map/pack/pallas_call | solution.py:519
  9.6 3.9 %collective-permute-start.3 = (bf16[1,976,128]{2,1,0:T(8,128)(2,1)}, bf16[1,976,128]{2,1,0:T(8,128)(2,1)S(1)}, u32[]{:S(2)}, u32[]{:S(2)}) collective-permute-start(bf16[1,976,128]{2,1,0:T(8,128)(2,1)} %get-tuple-element.109), channel_id=1, source_target_pairs={{0,20},{4,16},{8,28},{12,24},{16,4},{20,0},{24,12},{28,8},{1,21},{... | collective-permute-start | bytes 749576 | tf_op jit(solution)/shard_map/ppermute | solution.py:560
  13.6 0.1 collective-permute-start.4
  13.7 0.3 collective-permute-start
  13.9 1.8 %collective-permute-start.1 = (bf16[2,976,128]{2,1,0:T(8,128)(2,1)}, bf16[2,976,128]{2,1,0:T(8,128)(2,1)}, u32[]{:S(2)}, u32[]{:S(2)}) collective-permute-start(bf16[2,976,128]{2,1,0:T(8,128)(2,1)} %get-tuple-element.107), channel_id=1, source_target_pairs={{0,8},{4,12},{8,0},{12,4},{16,24},{20,28},{24,16},{28,20},{1,9},{5... | collective-permute-start | bytes 1499144 | tf_op jit(solution)/shard_map/ppermute | solution.py:560
  15.7 1.7 %collective-permute-start.2 = (bf16[2,976,128]{2,1,0:T(8,128)(2,1)}, bf16[2,976,128]{2,1,0:T(8,128)(2,1)}, u32[]{:S(2)}, u32[]{:S(2)}) collective-permute-start(bf16[2,976,128]{2,1,0:T(8,128)(2,1)} %get-tuple-element.108), channel_id=1, source_target_pairs={{0,4},{4,0},{8,12},{12,8},{16,20},{20,16},{24,28},{28,24},{1,5},{5... | collective-permute-start | bytes 1499144 | tf_op jit(solution)/shard_map/ppermute | solution.py:560
  17.4 0.0 copy-start
  17.4 1.5 %copy-done = bf16[8,4,240,128]{3,2,1,0:T(8,128)(2,1)S(1)} copy-done((bf16[8,4,240,128]{3,2,1,0:T(8,128)(2,1)S(1)}, bf16[8,4,240,128]{3,2,1,0:T(8,128)(2,1)}, u32[]{:S(2)}) %copy-start) | copy-done | bytes 1966104
  19.0 0.9 %copy-done.8 = bf16[128,448]{1,0:T(8,128)(2,1)S(1)} copy-done((bf16[128,448]{1,0:T(8,128)(2,1)S(1)}, bf16[128,448]{1,0:T(8,128)(2,1)}, u32[]{:S(2)}) %copy-start.8) | copy-done | bytes 114712
  19.9 0.8 copy-done.10
  20.6 0.8 copy-done.11
  21.4 2.6 %attend.1 = bf16[128,1792]{1,0:T(8,128)(2,1)S(1)} custom-call(bf16[128,64]{1,0:T(8,128)(2,1)S(1)} %copy-done.10, bf16[128,64]{1,0:T(8,128)(2,1)S(1)} %copy-done.11, bf16[128,448]{1,0:T(8,128)(2,1)S(1)} %copy-done.8, bf16[8,4,240,128]{3,2,1,0:T(8,128)(2,1)S(1)} %copy-done, f32[4,8,273]{2,1,0:T(8,128)S(1)} %copy-done.7, bf16[448,1792]{1,0:T(8,128)(2,1)S(1)} %copy-done.6, ...), custom_call_target="tpu_custom_call" | custom-call | bytes 1080 | tf_op jit(solution)/shard_map/attend/pallas_call | solution.py:588
  24.0 0.0 copy-start.1
  24.0 0.0 copy-start.2
  24.0 0.0 copy-start.12
  24.0 2.6 %all-gather = bf16[256,1792]{1,0:T(8,128)(2,1)S(1)} all-gather(bf16[128,1792]{1,0:T(8,128)(2,1)S(1)} %attend.1), channel_id=2, replica_groups={{0,1},{2,3},{4,5},{6,7},{8,9},{10,11},{12,13},{14,15},{16,17},{18,19},{..., dimensions={0}, use_global_device_ids=true | all-gather | bytes 1376256 | tf_op jit(solution)/shard_map/all_gather | solution.py:581
  26.6 0.1 dynamic-slice_reduce_fusion.1
  26.7 8.3 %all-gather.1 = bf16[128,1792]{1,0:T(8,128)(2,1)S(1)} all-gather(bf16[64,1792]{1,0:T(8,128)(2,1)S(1)} %dynamic-slice_reduce_fusion.1), channel_id=3, replica_groups={{0,2},{1,3},{4,6},{5,7},{8,10},{9,11},{12,14},{13,15},{16,18},{17,19},{..., dimensions={0}, use_global_device_ids=true | all-gather | bytes 688128 | tf_op jit(solution)/shard_map/all_gather | solution.py:584
  35.0 0.1 reduce_sum.49
  35.1 2.1 %all_gather.34.sum_ref = bf16[128,1792]{1,0:T(8,128)(2,1)S(1)} all-gather(bf16[64,1792]{1,0:T(8,128)(2,1)S(1)} %reduce_sum.49), channel_id=1, replica_groups={{0,1},{2,3},{4,5},{6,7},{8,9},{10,11},{12,13},{14,15},{16,17},{18,19},{..., dimensions={0}, use_global_device_ids=true | all-gather | bytes 688128 | tf_op jit(solution)/shard_map/all_gather | solution.py:586
  37.2 0.0 copy-start.3
  37.2 1.5 %copy-done.3 = bf16[1792,512]{1,0:T(8,128)(2,1)S(1)} copy-done((bf16[1792,512]{1,0:T(8,128)(2,1)S(1)}, bf16[1792,512]{1,0:T(8,128)(2,1)}, u32[]{:S(2)}) %copy-start.3) | copy-done | bytes 1835032
  38.7 1.5 %copy-done.4 = bf16[512,1792]{1,0:T(8,128)(2,1)S(1)} copy-done((bf16[512,1792]{1,0:T(8,128)(2,1)S(1)}, bf16[512,1792]{1,0:T(8,128)(2,1)}, u32[]{:S(2)}) %copy-start.4) | copy-done | bytes 1835032
  40.2 1.2 %mlp.1 = (f32[128,1792]{1,0:T(8,128)S(1)}, bf16[128,1792]{1,0:T(8,128)(2,1)S(1)}) custom-call(bf16[128,1792]{1,0:T(8,128)(2,1)S(1)} %bitcast.16, bf16[128,1792]{1,0:T(8,128)(2,1)S(1)} %all_gather.34.sum_ref, f32[1792]{0:T(1024)S(1)} %copy-done.12, bf16[1792,512]{1,0:T(8,128)(2,1)S(1)} %copy-done.2, bf16[1792,512]{1,0:T(8,128)(2,1)S(1)} %copy-done.3, ...), custom_call_target="tpu_custom_call" | custom-call | bytes 1080 | tf_op jit(solution)/shard_map/mlp/pallas_call | solution.py:601
  41.5 2.5 %all-gather.2 = bf16[256,1792]{1,0:T(8,128)(2,1)S(1)} all-gather(bf16[128,1792]{1,0:T(8,128)(2,1)S(1)} %get-tuple-element.105), channel_id=4, replica_groups={{0,1},{2,3},{4,5},{6,7},{8,9},{10,11},{12,13},{14,15},{16,17},{18,19},{..., dimensions={0}, use_global_device_ids=true | all-gather | bytes 1376256 | tf_op jit(solution)/shard_map/all_gather | solution.py:581
  43.9 0.1 dynamic-slice_reduce_fusion
  44.0 0.0 collective-permute-done.3.rest_5_
  44.0 0.0 collective-permute-done.4.rest_3_
  44.0 1.7 %collective-permute-done.across_ref.rest_4_ = bf16[2,976,128]{2,1,0:T(8,128)(2,1)} collective-permute-done((bf16[2,976,128]{2,1,0:T(8,128)(2,1)}, bf16[2,976,128]{2,1,0:T(8,128)(2,1)}, u32[]{:S(2)}, u32[]{:S(2)}) %collective-permute-start) | collective-permute-done | bytes 499744 | tf_op jit(solution)/shard_map/ppermute | solution.py:560
  45.7 1.4 %collective-permute-done.1.beside_ref.rest_2_ = bf16[2,976,128]{2,1,0:T(8,128)(2,1)} collective-permute-done((bf16[2,976,128]{2,1,0:T(8,128)(2,1)}, bf16[2,976,128]{2,1,0:T(8,128)(2,1)}, u32[]{:S(2)}, u32[]{:S(2)}) %collective-permute-start.1) | collective-permute-done | bytes 499744 | tf_op jit(solution)/shard_map/ppermute | solution.py:560
  47.1 0.0 collective-permute-done.2.rest_1_
  47.1 1.2 %relay.1 = (bf16[1,976,128]{2,1,0:T(8,128)(2,1)S(1)}, bf16[2,976,128]{2,1,0:T(8,128)(2,1)S(1)}) custom-call(bf16[2,976,128]{2,1,0:T(8,128)(2,1)} %collective-permute-done.across_ref.rest_4_, bf16[2,976,128]{2,1,0:T(8,128)(2,1)} %collective-permute-done.1.beside_ref.rest_2_), custom_call_target="tpu_custom_call" | custom-call | bytes 360 | tf_op jit(solution)/shard_map/relay/pallas_call | solution.py:615
  48.3 0.6 collective-permute-start.5
  48.9 1.3 %collective-permute-start.8 = (bf16[1,976,128]{2,1,0:T(8,128)(2,1)}, bf16[1,976,128]{2,1,0:T(8,128)(2,1)S(1)}, u32[]{:S(2)}, u32[]{:S(2)}) collective-permute-start(bf16[1,976,128]{2,1,0:T(8,128)(2,1)} %get-tuple-element.118), channel_id=1, source_target_pairs={{0,24},{4,28},{8,16},{12,20},{16,8},{20,12},{24,0},{28,4},{1,25},{... | collective-permute-start | bytes 749576 | tf_op jit(solution)/shard_map/ppermute | solution.py:560
  50.1 1.7 %collective-permute-start.9 = (bf16[1,976,128]{2,1,0:T(8,128)(2,1)}, bf16[1,976,128]{2,1,0:T(8,128)(2,1)S(1)}, u32[]{:S(2)}, u32[]{:S(2)}) collective-permute-start(bf16[1,976,128]{2,1,0:T(8,128)(2,1)} %get-tuple-element.119), channel_id=1, source_target_pairs={{0,28},{4,24},{8,20},{12,16},{16,12},{20,8},{24,4},{28,0},{1,29},{... | collective-permute-start | bytes 749576 | tf_op jit(solution)/shard_map/ppermute | solution.py:560
  51.8 2.6 %collective-permute-start.7 = (bf16[1,976,128]{2,1,0:T(8,128)(2,1)S(1)}, bf16[1,976,128]{2,1,0:T(8,128)(2,1)}, u32[]{:S(2)}, u32[]{:S(2)}) collective-permute-start(bf16[1,976,128]{2,1,0:T(8,128)(2,1)S(1)} %get-tuple-element.117), channel_id=1, source_target_pairs={{0,12},{4,8},{8,4},{12,0},{16,28},{20,24},{24,20},{28,16},{1,13},{... | collective-permute-start | bytes 749576 | tf_op jit(solution)/shard_map/ppermute | solution.py:560
  54.5 0.0 collective-permute-start.6
  54.5 6.7 %all-gather.3 = bf16[128,1792]{1,0:T(8,128)(2,1)S(1)} all-gather(bf16[64,1792]{1,0:T(8,128)(2,1)S(1)} %dynamic-slice_reduce_fusion), channel_id=5, replica_groups={{0,2},{1,3},{4,6},{5,7},{8,10},{9,11},{12,14},{13,15},{16,18},{17,19},{..., dimensions={0}, use_global_device_ids=true | all-gather | bytes 688128 | tf_op jit(solution)/shard_map/all_gather | solution.py:584
  61.1 0.8 reduce_sum.51
  62.0 2.3 %all_gather.39.sum_ref = bf16[128,1792]{1,0:T(8,128)(2,1)S(1)} all-gather(bf16[64,1792]{1,0:T(8,128)(2,1)} %reduce_sum.51), channel_id=1, replica_groups={{0,1},{2,3},{4,5},{6,7},{8,9},{10,11},{12,13},{14,15},{16,17},{18,19},{..., dimensions={0}, use_global_device_ids=true | all-gather | bytes 688128 | tf_op jit(solution)/shard_map/all_gather | solution.py:586
  64.3 3.6 %collective-permute-done.8.rest_6_ = bf16[1,976,128]{2,1,0:T(8,128)(2,1)S(1)} collective-permute-done((bf16[1,976,128]{2,1,0:T(8,128)(2,1)}, bf16[1,976,128]{2,1,0:T(8,128)(2,1)S(1)}, u32[]{:S(2)}, u32[]{:S(2)}) %collective-permute-start.8) | collective-permute-done | bytes 249888 | tf_op jit(solution)/shard_map/ppermute | solution.py:560
  67.9 7.4 %collective-permute-done.9.rest_7_ = bf16[1,976,128]{2,1,0:T(8,128)(2,1)S(1)} collective-permute-done((bf16[1,976,128]{2,1,0:T(8,128)(2,1)}, bf16[1,976,128]{2,1,0:T(8,128)(2,1)S(1)}, u32[]{:S(2)}, u32[]{:S(2)}) %collective-permute-start.9) | collective-permute-done | bytes 249888 | tf_op jit(solution)/shard_map/ppermute | solution.py:560
  75.3 0.0 collective-permute-done.7
  75.4 1.6 %close.1 = (bf16[128,1792]{1,0:T(8,128)(2,1)}, s32[1]{0:T(128)}) custom-call(f32[128,1792]{1,0:T(8,128)S(1)} %get-tuple-element.104.residual_ref, bf16[128,1792]{1,0:T(8,128)(2,1)S(1)} %all_gather.39.sum_ref, bf16[2,976,128]{2,1,0:T(8,128)(2,1)S(1)} %copy-done.13, bf16[2,976,128]{2,1,0:T(8,128)(2,1)} %collective-permute-done.2.rest_1_, ...), custom_call_target="tpu_custom_call" | custom-call | bytes 360 | tf_op jit(solution)/shard_map/close/pallas_call | solution.py:637
  77.6 6.8 %conditional.1 = ((f32[3822,4,128]{2,1,0:T(4,128)}, f32[4,16,273]{2,1,0:T(8,128)}, bf16[16,2,448]{2,1,0:T(2,128)(2,1)})) conditional(s32[]{:T(128)} %bitcast.10, (bf16[2,976,128]{2,1,0:T(8,128)(2,1)S(1)}, bf16[2,976,128]{2,1,0:T(8,128)(2,1)}, bf16[2,976,128]{2,1,0:T(8,128)(2,1)}, bf16[1,976,128]{2,1,0:T(8,128)(2,1)}, bf16[2,976,128]{2,1,0:T(8,128)(2,1)}, ...), branch_computations={%region_4.5_spmd, %region_5.6_spmd} | conditional | bytes 4000224 | solution.py:679
  77.6 6.6 %settle.1 = (f32[3822,4,128]{2,1,0:T(4,128)}, f32[4,16,273]{2,1,0:T(8,128)}, bf16[16,2,448]{2,1,0:T(2,128)(2,1)}) custom-call(bf16[2,976,128]{2,1,0:T(8,128)(2,1)S(1)} %get-tuple-element.40.rest_0_, bf16[2,976,128]{2,1,0:T(8,128)(2,1)} %get-tuple-element.41.rest_1_, bf16[2,976,128]{2,1,0:T(8,128)(2,1)} %get-tuple-element.42.rest_2_, ...), custom_call_target="tpu_custom_call" | custom-call | bytes 2520 | tf_op jit(solution)/shard_map/cond/branch_0_fun/settle/pallas_call | solution.py:651
  (17 shorter events, 0.0 us)
Async XLA Ops:
  0.6 16.8 %copy-start.5 = (bf16[128,1792]{1,0:T(8,128)(2,1)S(1)}, bf16[128,1792]{1,0:T(8,128)(2,1)}, u32[]{:S(2)}) copy-start(bf16[128,1792]{1,0:T(8,128)(2,1)} %constant.36.clone.rest_9_.table_ref) | copy-start | bytes 1376260
  0.6 16.8 %copy-start.6 = (bf16[448,1792]{1,0:T(8,128)(2,1)S(1)}, bf16[448,1792]{1,0:T(8,128)(2,1)}, u32[]{:S(2)}) copy-start(bf16[448,1792]{1,0:T(8,128)(2,1)} %wo_ref.1) | copy-start | bytes 4816900
  0.7 16.8 %copy-start.7 = (f32[4,8,273]{2,1,0:T(8,128)S(1)}, f32[4,8,273]{2,1,0:T(8,128)}, u32[]{:S(2)}) copy-start(f32[4,8,273]{2,1,0:T(8,128)} %norm_ref.1) | copy-start | bytes 104836
  0.7 16.7 %copy-start.9 = (f32[8,896]{1,0:T(8,128)S(1)}, f32[8,896]{1,0:T(8,128)}, u32[]{:S(2)}) copy-start(f32[8,896]{1,0:T(8,128)} %constant.37.clone.rest_10_.bias_ref) | copy-start | bytes 86020
  9.6 34.4 %collective-permute-start.3 = (bf16[1,976,128]{2,1,0:T(8,128)(2,1)}, bf16[1,976,128]{2,1,0:T(8,128)(2,1)S(1)}, u32[]{:S(2)}, u32[]{:S(2)}) collective-permute-start(bf16[1,976,128]{2,1,0:T(8,128)(2,1)} %get-tuple-element.109), channel_id=1, source_target_pairs={{0,20},{4,16},{8,28},{12,24},{16,4},{20,0},{24,12},{28,8},{1,21},{... | collective-permute-start | bytes 749576 | tf_op jit(solution)/shard_map/ppermute | solution.py:560
  13.6 30.4 %collective-permute-start.4 = (bf16[1,976,128]{2,1,0:T(8,128)(2,1)}, bf16[1,976,128]{2,1,0:T(8,128)(2,1)}, u32[]{:S(2)}, u32[]{:S(2)}) collective-permute-start(bf16[1,976,128]{2,1,0:T(8,128)(2,1)} %get-tuple-element.110), channel_id=1, source_target_pairs={{0,12},{4,8},{8,4},{12,0},{16,28},{20,24},{24,20},{28,16},{1,13},{... | collective-permute-start | bytes 749576 | tf_op jit(solution)/shard_map/ppermute | solution.py:560
  13.7 32.0 %collective-permute-start = (bf16[2,976,128]{2,1,0:T(8,128)(2,1)}, bf16[2,976,128]{2,1,0:T(8,128)(2,1)}, u32[]{:S(2)}, u32[]{:S(2)}) collective-permute-start(bf16[2,976,128]{2,1,0:T(8,128)(2,1)} %get-tuple-element.106), channel_id=1, source_target_pairs={{0,16},{4,20},{8,24},{12,28},{16,0},{20,4},{24,8},{28,12},{1,17},{... | collective-permute-start | bytes 1499144 | tf_op jit(solution)/shard_map/ppermute | solution.py:560
  13.9 33.1 %collective-permute-start.1 = (bf16[2,976,128]{2,1,0:T(8,128)(2,1)}, bf16[2,976,128]{2,1,0:T(8,128)(2,1)}, u32[]{:S(2)}, u32[]{:S(2)}) collective-permute-start(bf16[2,976,128]{2,1,0:T(8,128)(2,1)} %get-tuple-element.107), channel_id=1, source_target_pairs={{0,8},{4,12},{8,0},{12,4},{16,24},{20,28},{24,16},{28,20},{1,9},{5... | collective-permute-start | bytes 1499144 | tf_op jit(solution)/shard_map/ppermute | solution.py:560
  15.7 31.4 %collective-permute-start.2 = (bf16[2,976,128]{2,1,0:T(8,128)(2,1)}, bf16[2,976,128]{2,1,0:T(8,128)(2,1)}, u32[]{:S(2)}, u32[]{:S(2)}) collective-permute-start(bf16[2,976,128]{2,1,0:T(8,128)(2,1)} %get-tuple-element.108), channel_id=1, source_target_pairs={{0,4},{4,0},{8,12},{12,8},{16,20},{20,16},{24,28},{28,24},{1,5},{5... | collective-permute-start | bytes 1499144 | tf_op jit(solution)/shard_map/ppermute | solution.py:560
  17.4 1.5 %copy-start = (bf16[8,4,240,128]{3,2,1,0:T(8,128)(2,1)S(1)}, bf16[8,4,240,128]{3,2,1,0:T(8,128)(2,1)}, u32[]{:S(2)}) copy-start(bf16[8,4,240,128]{3,2,1,0:T(8,128)(2,1)} %get-tuple-element.103.start_ref) | copy-start | bytes 5898244
  19.0 0.9 %copy-start.8 = (bf16[128,448]{1,0:T(8,128)(2,1)S(1)}, bf16[128,448]{1,0:T(8,128)(2,1)}, u32[]{:S(2)}) copy-start(bf16[128,448]{1,0:T(8,128)(2,1)} %get-tuple-element.102.v_ref) | copy-start | bytes 344068
  19.9 0.8 copy-start.10
  20.6 0.8 copy-start.11
  24.0 13.3 %copy-start.1 = (bf16[8,16,1792]{2,1,0:T(8,128)(2,1)S(1)}, bf16[8,16,1792]{2,1,0:T(8,128)(2,1)}, u32[]{:S(2)}) copy-start(bf16[8,16,1792]{2,1,0:T(8,128)(2,1)} %param.20) | copy-start | bytes 1376260
  24.0 13.2 %copy-start.2 = (bf16[1792,512]{1,0:T(8,128)(2,1)S(1)}, bf16[1792,512]{1,0:T(8,128)(2,1)}, u32[]{:S(2)}) copy-start(bf16[1792,512]{1,0:T(8,128)(2,1)} %wg_ref.1) | copy-start | bytes 5505028
  24.0 13.2 %copy-start.12 = (f32[1792]{0:T(1024)S(1)}, f32[1792]{0:T(1024)}, u32[]{:S(2)}) copy-start(f32[1792]{0:T(1024)} %gain_ref.1) | copy-start | bytes 21508
  37.2 1.5 %copy-start.3 = (bf16[1792,512]{1,0:T(8,128)(2,1)S(1)}, bf16[1792,512]{1,0:T(8,128)(2,1)}, u32[]{:S(2)}) copy-start(bf16[1792,512]{1,0:T(8,128)(2,1)} %wu_ref.1) | copy-start | bytes 5505028
  38.7 1.5 %copy-start.4 = (bf16[512,1792]{1,0:T(8,128)(2,1)S(1)}, bf16[512,1792]{1,0:T(8,128)(2,1)}, u32[]{:S(2)}) copy-start(bf16[512,1792]{1,0:T(8,128)(2,1)} %wd_ref.1) | copy-start | bytes 5505028
  43.9 31.4 %copy-start.13 = (bf16[2,976,128]{2,1,0:T(8,128)(2,1)S(1)}, bf16[2,976,128]{2,1,0:T(8,128)(2,1)}, u32[]{:S(2)}) copy-start(bf16[2,976,128]{2,1,0:T(8,128)(2,1)} %get-tuple-element.121.rest_0_) | copy-start | bytes 1499140
  48.3 27.1 %collective-permute-start.5 = (bf16[2,976,128]{2,1,0:T(8,128)(2,1)S(1)}, bf16[2,976,128]{2,1,0:T(8,128)(2,1)}, u32[]{:S(2)}, u32[]{:S(2)}) collective-permute-start(bf16[2,976,128]{2,1,0:T(8,128)(2,1)S(1)} %get-tuple-element.116), channel_id=1, source_target_pairs={{0,4},{4,0},{8,12},{12,8},{16,20},{20,16},{24,28},{28,24},{1,5},{5... | collective-permute-start | bytes 1499144 | tf_op jit(solution)/shard_map/ppermute | solution.py:560
  48.9 19.0 %collective-permute-start.8 = (bf16[1,976,128]{2,1,0:T(8,128)(2,1)}, bf16[1,976,128]{2,1,0:T(8,128)(2,1)S(1)}, u32[]{:S(2)}, u32[]{:S(2)}) collective-permute-start(bf16[1,976,128]{2,1,0:T(8,128)(2,1)} %get-tuple-element.118), channel_id=1, source_target_pairs={{0,24},{4,28},{8,16},{12,20},{16,8},{20,12},{24,0},{28,4},{1,25},{... | collective-permute-start | bytes 749576 | tf_op jit(solution)/shard_map/ppermute | solution.py:560
  50.1 25.2 %collective-permute-start.9 = (bf16[1,976,128]{2,1,0:T(8,128)(2,1)}, bf16[1,976,128]{2,1,0:T(8,128)(2,1)S(1)}, u32[]{:S(2)}, u32[]{:S(2)}) collective-permute-start(bf16[1,976,128]{2,1,0:T(8,128)(2,1)} %get-tuple-element.119), channel_id=1, source_target_pairs={{0,28},{4,24},{8,20},{12,16},{16,12},{20,8},{24,4},{28,0},{1,29},{... | collective-permute-start | bytes 749576 | tf_op jit(solution)/shard_map/ppermute | solution.py:560
  51.8 23.5 %collective-permute-start.7 = (bf16[1,976,128]{2,1,0:T(8,128)(2,1)S(1)}, bf16[1,976,128]{2,1,0:T(8,128)(2,1)}, u32[]{:S(2)}, u32[]{:S(2)}) collective-permute-start(bf16[1,976,128]{2,1,0:T(8,128)(2,1)S(1)} %get-tuple-element.117), channel_id=1, source_target_pairs={{0,12},{4,8},{8,4},{12,0},{16,28},{20,24},{24,20},{28,16},{1,13},{... | collective-permute-start | bytes 749576 | tf_op jit(solution)/shard_map/ppermute | solution.py:560
  54.5 20.9 %collective-permute-start.6 = (bf16[1,976,128]{2,1,0:T(8,128)(2,1)S(1)}, bf16[1,976,128]{2,1,0:T(8,128)(2,1)}, u32[]{:S(2)}, u32[]{:S(2)}) collective-permute-start(bf16[1,976,128]{2,1,0:T(8,128)(2,1)S(1)} %get-tuple-element.117), channel_id=1, source_target_pairs={{0,8},{4,12},{8,0},{12,4},{16,24},{20,28},{24,16},{28,20},{1,9},{5... | collective-permute-start | bytes 749576 | tf_op jit(solution)/shard_map/ppermute | solution.py:560

commit v4 on v3

--- a/solution.py
+++ b/solution.py
@@ -622,13 +622,13 @@
                 cost_estimate=cost(1),
                 name="relay",
             )(arrived[4], arrived[2])
-            forward.update({far: swapped(passed, far) for far in (2, 3)})
             forward[1] = swapped(both, 1)
+            forward.update({far: swapped(passed, far) for far in (3, 2)})
         return x
 
     total = summed(part, half_way)
     if pair_cap > 1:
-        total, forward = wave((total, forward), (6, 7), (6, 7), ())
+        total = wave(total, (6, 7), (6, 7), ())
     firsts, items = [], []
     if pair_cap > 1:
         arrived[0] = pieces[0]

time: 85.5 us -> 85.1 us (level)
  transfers between devices with their start and end apart: 10 -> 10, of which waited for: 4 -> 4; matrix products, arithmetic and copies ran while one was open for 1% -> 1% of each run, Pallas kernels for 4% -> 6%
where the time goes in v4:
time: 85.1 us; the launch traced here: 84.5 us
  blocking collectives  24.5 us (29%)
  Pallas kernels  22.4 us (26%)
  starting transfers between devices  14.3 us (17%)
  waiting for transfers between devices  13.4 us (16%)
  local copies, waits for them, and re-layouts  7 us (8%)
  between operations  1.63 us (2%)
  other arithmetic  1.02 us (1%)
    all_gather x2, blocking collectives, summed(): mine = lax.all_gather(mine, 'tp', axis=0, axis_index_groups=chips)  15 us
    ppermute x10, starting transfers between devices, swapped(): return lax.ppermute(x, 'req', [(i, i ^ far) for i in range(count)])  14.3 us
    ppermute x10, waiting for transfers between devices, swapped(): return lax.ppermute(x, 'req', [(i, i ^ far) for i in range(count)])  13.4 us
    pallas_call x1, Pallas kernels, shards(): pl.pallas_call(functools.partial(pack_kernel, heads, count, pair_cap, tp_...  9.27 us
    unnamed x28, local copies, waits for them, and re-layouts  7 us
    pallas_call x1, Pallas kernels, settled(): pl.pallas_call(functools.partial(settle_kernel, heads, count, pair_cap, d...  6.6 us
    all_gather x2, blocking collectives, summed(): both = lax.all_gather(part, 'tp', axis=0, axis_index_groups=cores)  5.06 us
    all_gather x2, blocking collectives, summed(): lax.all_gather(mine, 'tp', axis=0, tiled=True, axis_index_groups=cores)  4.47 us
  transfers between devices with their start and end apart: 10, of which 4 were waited for; matrix products, arithmetic and copies ran while one was open for 1% of the time, Pallas kernels for 6%

profile of v4, /device:TPU:8, one launch (start us, length us, event | category | flops | bytes accessed | tf_op | source)
XLA Modules:
  0.0 84.5 jit_solution(12716950692331317961)
XLA Ops:
  0.6 0.0 copy-start.5
  0.7 0.0 copy-start.9
  0.7 9.3 %pack.1 = (bf16[2,976,128]{2,1,0:T(8,128)(2,1)}, bf16[2,976,128]{2,1,0:T(8,128)(2,1)}, bf16[2,976,128]{2,1,0:T(8,128)(2,1)}, bf16[1,976,128]{2,1,0:T(8,128)(2,1)...) custom-call(f32[1911,4,128]{2,1,0:T(4,128)} %bitcast.17, ...), custom_call_target="tpu_custom_call" | custom-call | bytes 2880 | tf_op jit(solution)/shard_map/pack/pallas_call | solution.py:519
  10.0 3.3 %collective-permute-start.3 = (bf16[1,976,128]{2,1,0:T(8,128)(2,1)}, bf16[1,976,128]{2,1,0:T(8,128)(2,1)S(1)}, u32[]{:S(2)}, u32[]{:S(2)}) collective-permute-start(bf16[1,976,128]{2,1,0:T(8,128)(2,1)} %get-tuple-element.106), channel_id=1, source_target_pairs={{0,20},{4,16},{8,28},{12,24},{16,4},{20,0},{24,12},{28,8},{1,21},{... | collective-permute-start | bytes 749576 | tf_op jit(solution)/shard_map/ppermute | solution.py:560
  13.3 0.4 collective-permute-start.4
  13.7 0.4 collective-permute-start
  14.1 1.8 %collective-permute-start.1 = (bf16[2,976,128]{2,1,0:T(8,128)(2,1)}, bf16[2,976,128]{2,1,0:T(8,128)(2,1)}, u32[]{:S(2)}, u32[]{:S(2)}) collective-permute-start(bf16[2,976,128]{2,1,0:T(8,128)(2,1)} %get-tuple-element.104), channel_id=1, source_target_pairs={{0,8},{4,12},{8,0},{12,4},{16,24},{20,28},{24,16},{28,20},{1,9},{5... | collective-permute-start | bytes 1499144 | tf_op jit(solution)/shard_map/ppermute | solution.py:560
  15.9 1.5 %collective-permute-start.2 = (bf16[2,976,128]{2,1,0:T(8,128)(2,1)}, bf16[2,976,128]{2,1,0:T(8,128)(2,1)}, u32[]{:S(2)}, u32[]{:S(2)}) collective-permute-start(bf16[2,976,128]{2,1,0:T(8,128)(2,1)} %get-tuple-element.105), channel_id=1, source_target_pairs={{0,4},{4,0},{8,12},{12,8},{16,20},{20,16},{24,28},{28,24},{1,5},{5... | collective-permute-start | bytes 1499144 | tf_op jit(solution)/shard_map/ppermute | solution.py:560
  17.4 0.0 copy-start
  17.4 1.5 %copy-done = bf16[8,4,240,128]{3,2,1,0:T(8,128)(2,1)S(1)} copy-done((bf16[8,4,240,128]{3,2,1,0:T(8,128)(2,1)S(1)}, bf16[8,4,240,128]{3,2,1,0:T(8,128)(2,1)}, u32[]{:S(2)}) %copy-start) | copy-done | bytes 1966104
  19.0 0.9 %copy-done.8 = bf16[128,448]{1,0:T(8,128)(2,1)S(1)} copy-done((bf16[128,448]{1,0:T(8,128)(2,1)S(1)}, bf16[128,448]{1,0:T(8,128)(2,1)}, u32[]{:S(2)}) %copy-start.8) | copy-done | bytes 114712
  19.9 0.8 copy-done.10
  20.6 0.8 copy-done.11
  21.4 2.6 %attend.1 = bf16[128,1792]{1,0:T(8,128)(2,1)S(1)} custom-call(bf16[128,64]{1,0:T(8,128)(2,1)S(1)} %copy-done.10, bf16[128,64]{1,0:T(8,128)(2,1)S(1)} %copy-done.11, bf16[128,448]{1,0:T(8,128)(2,1)S(1)} %copy-done.8, bf16[8,4,240,128]{3,2,1,0:T(8,128)(2,1)S(1)} %copy-done, f32[4,8,273]{2,1,0:T(8,128)S(1)} %copy-done.7, bf16[448,1792]{1,0:T(8,128)(2,1)S(1)} %copy-done.6, ...), custom_call_target="tpu_custom_call" | custom-call | bytes 1080 | tf_op jit(solution)/shard_map/attend/pallas_call | solution.py:588
  24.0 0.0 copy-start.1
  24.0 0.0 copy-start.2
  24.0 0.0 copy-start.12
  24.0 2.6 %all-gather = bf16[256,1792]{1,0:T(8,128)(2,1)S(1)} all-gather(bf16[128,1792]{1,0:T(8,128)(2,1)S(1)} %attend.1), channel_id=2, replica_groups={{0,1},{2,3},{4,5},{6,7},{8,9},{10,11},{12,13},{14,15},{16,17},{18,19},{..., dimensions={0}, use_global_device_ids=true | all-gather | bytes 1376256 | tf_op jit(solution)/shard_map/all_gather | solution.py:581
  26.6 0.1 dynamic-slice_reduce_fusion.1
  26.7 8.3 %all-gather.1 = bf16[128,1792]{1,0:T(8,128)(2,1)S(1)} all-gather(bf16[64,1792]{1,0:T(8,128)(2,1)S(1)} %dynamic-slice_reduce_fusion.1), channel_id=3, replica_groups={{0,2},{1,3},{4,6},{5,7},{8,10},{9,11},{12,14},{13,15},{16,18},{17,19},{..., dimensions={0}, use_global_device_ids=true | all-gather | bytes 688128 | tf_op jit(solution)/shard_map/all_gather | solution.py:584
  35.0 0.1 reduce_sum.49
  35.1 2.1 %all_gather.34.sum_ref = bf16[128,1792]{1,0:T(8,128)(2,1)S(1)} all-gather(bf16[64,1792]{1,0:T(8,128)(2,1)S(1)} %reduce_sum.49), channel_id=1, replica_groups={{0,1},{2,3},{4,5},{6,7},{8,9},{10,11},{12,13},{14,15},{16,17},{18,19},{..., dimensions={0}, use_global_device_ids=true | all-gather | bytes 688128 | tf_op jit(solution)/shard_map/all_gather | solution.py:586
  37.2 0.0 copy-start.3
  37.2 1.5 %copy-done.3 = bf16[1792,512]{1,0:T(8,128)(2,1)S(1)} copy-done((bf16[1792,512]{1,0:T(8,128)(2,1)S(1)}, bf16[1792,512]{1,0:T(8,128)(2,1)}, u32[]{:S(2)}) %copy-start.3) | copy-done | bytes 1835032
  38.7 1.5 %copy-done.4 = bf16[512,1792]{1,0:T(8,128)(2,1)S(1)} copy-done((bf16[512,1792]{1,0:T(8,128)(2,1)S(1)}, bf16[512,1792]{1,0:T(8,128)(2,1)}, u32[]{:S(2)}) %copy-start.4) | copy-done | bytes 1835032
  40.2 1.2 %mlp.1 = (f32[128,1792]{1,0:T(8,128)S(1)}, bf16[128,1792]{1,0:T(8,128)(2,1)S(1)}) custom-call(bf16[128,1792]{1,0:T(8,128)(2,1)S(1)} %bitcast.16, bf16[128,1792]{1,0:T(8,128)(2,1)S(1)} %all_gather.34.sum_ref, f32[1792]{0:T(1024)S(1)} %copy-done.12, bf16[1792,512]{1,0:T(8,128)(2,1)S(1)} %copy-done.2, bf16[1792,512]{1,0:T(8,128)(2,1)S(1)} %copy-done.3, ...), custom_call_target="tpu_custom_call" | custom-call | bytes 1080 | tf_op jit(solution)/shard_map/mlp/pallas_call | solution.py:601
  41.5 2.5 %all-gather.2 = bf16[256,1792]{1,0:T(8,128)(2,1)S(1)} all-gather(bf16[128,1792]{1,0:T(8,128)(2,1)S(1)} %get-tuple-element.102), channel_id=4, replica_groups={{0,1},{2,3},{4,5},{6,7},{8,9},{10,11},{12,13},{14,15},{16,17},{18,19},{..., dimensions={0}, use_global_device_ids=true | all-gather | bytes 1376256 | tf_op jit(solution)/shard_map/all_gather | solution.py:581
  43.9 0.1 dynamic-slice_reduce_fusion
  44.0 0.0 collective-permute-done.3.rest_5_
  44.0 0.0 collective-permute-done.4.rest_3_
  44.0 1.8 %collective-permute-done.rest_4_.across_ref = bf16[2,976,128]{2,1,0:T(8,128)(2,1)} collective-permute-done((bf16[2,976,128]{2,1,0:T(8,128)(2,1)}, bf16[2,976,128]{2,1,0:T(8,128)(2,1)}, u32[]{:S(2)}, u32[]{:S(2)}) %collective-permute-start) | collective-permute-done | bytes 499744 | tf_op jit(solution)/shard_map/ppermute | solution.py:560
  45.8 1.2 %collective-permute-done.1.rest_2_.beside_ref = bf16[2,976,128]{2,1,0:T(8,128)(2,1)} collective-permute-done((bf16[2,976,128]{2,1,0:T(8,128)(2,1)}, bf16[2,976,128]{2,1,0:T(8,128)(2,1)}, u32[]{:S(2)}, u32[]{:S(2)}) %collective-permute-start.1) | collective-permute-done | bytes 499744 | tf_op jit(solution)/shard_map/ppermute | solution.py:560
  47.0 0.0 collective-permute-done.2.rest_1_
  47.1 1.2 %relay.1 = (bf16[1,976,128]{2,1,0:T(8,128)(2,1)S(1)}, bf16[2,976,128]{2,1,0:T(8,128)(2,1)S(1)}) custom-call(bf16[2,976,128]{2,1,0:T(8,128)(2,1)} %collective-permute-done.rest_4_.across_ref, bf16[2,976,128]{2,1,0:T(8,128)(2,1)} %collective-permute-done.1.rest_2_.beside_ref), custom_call_target="tpu_custom_call" | custom-call | bytes 360 | tf_op jit(solution)/shard_map/relay/pallas_call | solution.py:615
  48.3 0.6 collective-permute-start.7
  48.8 1.3 %collective-permute-start.5 = (bf16[1,976,128]{2,1,0:T(8,128)(2,1)}, bf16[1,976,128]{2,1,0:T(8,128)(2,1)S(1)}, u32[]{:S(2)}, u32[]{:S(2)}) collective-permute-start(bf16[1,976,128]{2,1,0:T(8,128)(2,1)} %get-tuple-element.111), channel_id=1, source_target_pairs={{0,24},{4,28},{8,16},{12,20},{16,8},{20,12},{24,0},{28,4},{1,25},{... | collective-permute-start | bytes 749576 | tf_op jit(solution)/shard_map/ppermute | solution.py:560
  50.1 1.7 %collective-permute-start.6 = (bf16[1,976,128]{2,1,0:T(8,128)(2,1)}, bf16[1,976,128]{2,1,0:T(8,128)(2,1)S(1)}, u32[]{:S(2)}, u32[]{:S(2)}) collective-permute-start(bf16[1,976,128]{2,1,0:T(8,128)(2,1)} %get-tuple-element.112), channel_id=1, source_target_pairs={{0,28},{4,24},{8,20},{12,16},{16,12},{20,8},{24,4},{28,0},{1,29},{... | collective-permute-start | bytes 749576 | tf_op jit(solution)/shard_map/ppermute | solution.py:560
  51.8 3.3 %collective-permute-start.9 = (bf16[1,976,128]{2,1,0:T(8,128)(2,1)S(1)}, bf16[1,976,128]{2,1,0:T(8,128)(2,1)}, u32[]{:S(2)}, u32[]{:S(2)}) collective-permute-start(bf16[1,976,128]{2,1,0:T(8,128)(2,1)S(1)} %get-tuple-element.125), channel_id=1, source_target_pairs={{0,12},{4,8},{8,4},{12,0},{16,28},{20,24},{24,20},{28,16},{1,13},{... | collective-permute-start | bytes 749576 | tf_op jit(solution)/shard_map/ppermute | solution.py:560
  55.1 0.0 collective-permute-start.8
  55.1 6.7 %all-gather.3 = bf16[128,1792]{1,0:T(8,128)(2,1)S(1)} all-gather(bf16[64,1792]{1,0:T(8,128)(2,1)S(1)} %dynamic-slice_reduce_fusion), channel_id=5, replica_groups={{0,2},{1,3},{4,6},{5,7},{8,10},{9,11},{12,14},{13,15},{16,18},{17,19},{..., dimensions={0}, use_global_device_ids=true | all-gather | bytes 688128 | tf_op jit(solution)/shard_map/all_gather | solution.py:584
  61.8 0.8 reduce_sum.51
  62.6 2.3 %all_gather.39.sum_ref = bf16[128,1792]{1,0:T(8,128)(2,1)S(1)} all-gather(bf16[64,1792]{1,0:T(8,128)(2,1)} %reduce_sum.51), channel_id=1, replica_groups={{0,1},{2,3},{4,5},{6,7},{8,9},{10,11},{12,13},{14,15},{16,17},{18,19},{..., dimensions={0}, use_global_device_ids=true | all-gather | bytes 688128 | tf_op jit(solution)/shard_map/all_gather | solution.py:586
  64.9 3.0 %collective-permute-done.5.rest_6_ = bf16[1,976,128]{2,1,0:T(8,128)(2,1)S(1)} collective-permute-done((bf16[1,976,128]{2,1,0:T(8,128)(2,1)}, bf16[1,976,128]{2,1,0:T(8,128)(2,1)S(1)}, u32[]{:S(2)}, u32[]{:S(2)}) %collective-permute-start.5) | collective-permute-done | bytes 249888 | tf_op jit(solution)/shard_map/ppermute | solution.py:560
  67.9 7.3 %collective-permute-done.6.rest_7_ = bf16[1,976,128]{2,1,0:T(8,128)(2,1)S(1)} collective-permute-done((bf16[1,976,128]{2,1,0:T(8,128)(2,1)}, bf16[1,976,128]{2,1,0:T(8,128)(2,1)S(1)}, u32[]{:S(2)}, u32[]{:S(2)}) %collective-permute-start.6) | collective-permute-done | bytes 249888 | tf_op jit(solution)/shard_map/ppermute | solution.py:560
  75.2 1.6 %close.1 = (bf16[128,1792]{1,0:T(8,128)(2,1)}, s32[1]{0:T(128)}) custom-call(f32[128,1792]{1,0:T(8,128)S(1)} %get-tuple-element.101.residual_ref, bf16[128,1792]{1,0:T(8,128)(2,1)S(1)} %all_gather.39.sum_ref, bf16[2,976,128]{2,1,0:T(8,128)(2,1)S(1)} %copy-done.13, bf16[2,976,128]{2,1,0:T(8,128)(2,1)} %collective-permute-done.2.rest_1_, ...), custom_call_target="tpu_custom_call" | custom-call | bytes 360 | tf_op jit(solution)/shard_map/close/pallas_call | solution.py:637
  77.5 0.0 collective-permute-done.7
  77.5 6.8 %conditional.1 = ((f32[3822,4,128]{2,1,0:T(4,128)}, f32[4,16,273]{2,1,0:T(8,128)}, bf16[16,2,448]{2,1,0:T(2,128)(2,1)})) conditional(s32[]{:T(128)} %bitcast.10, (bf16[2,976,128]{2,1,0:T(8,128)(2,1)S(1)}, bf16[2,976,128]{2,1,0:T(8,128)(2,1)}, bf16[2,976,128]{2,1,0:T(8,128)(2,1)}, bf16[1,976,128]{2,1,0:T(8,128)(2,1)}, bf16[2,976,128]{2,1,0:T(8,128)(2,1)}, ...), branch_computations={%region_4.5_spmd, %region_5.6_spmd} | conditional | bytes 4000224 | solution.py:679
  77.5 6.6 %settle.1 = (f32[3822,4,128]{2,1,0:T(4,128)}, f32[4,16,273]{2,1,0:T(8,128)}, bf16[16,2,448]{2,1,0:T(2,128)(2,1)}) custom-call(bf16[2,976,128]{2,1,0:T(8,128)(2,1)S(1)} %get-tuple-element.40.rest_0_, bf16[2,976,128]{2,1,0:T(8,128)(2,1)} %get-tuple-element.41.rest_1_, bf16[2,976,128]{2,1,0:T(8,128)(2,1)} %get-tuple-element.42.rest_2_, ...), custom_call_target="tpu_custom_call" | custom-call | bytes 2520 | tf_op jit(solution)/shard_map/cond/branch_0_fun/settle/pallas_call | solution.py:651
  (17 shorter events, 0.0 us)
Async XLA Ops:
  0.6 16.8 %copy-start.5 = (bf16[128,1792]{1,0:T(8,128)(2,1)S(1)}, bf16[128,1792]{1,0:T(8,128)(2,1)}, u32[]{:S(2)}) copy-start(bf16[128,1792]{1,0:T(8,128)(2,1)} %constant.36.clone.rest_9_.table_ref) | copy-start | bytes 1376260
  0.6 16.8 %copy-start.6 = (bf16[448,1792]{1,0:T(8,128)(2,1)S(1)}, bf16[448,1792]{1,0:T(8,128)(2,1)}, u32[]{:S(2)}) copy-start(bf16[448,1792]{1,0:T(8,128)(2,1)} %wo_ref.1) | copy-start | bytes 4816900
  0.7 16.7 %copy-start.7 = (f32[4,8,273]{2,1,0:T(8,128)S(1)}, f32[4,8,273]{2,1,0:T(8,128)}, u32[]{:S(2)}) copy-start(f32[4,8,273]{2,1,0:T(8,128)} %norm_ref.1) | copy-start | bytes 104836
  0.7 16.7 %copy-start.9 = (f32[8,896]{1,0:T(8,128)S(1)}, f32[8,896]{1,0:T(8,128)}, u32[]{:S(2)}) copy-start(f32[8,896]{1,0:T(8,128)} %constant.37.clone.rest_10_.bias_ref) | copy-start | bytes 86020
  10.0 34.0 %collective-permute-start.3 = (bf16[1,976,128]{2,1,0:T(8,128)(2,1)}, bf16[1,976,128]{2,1,0:T(8,128)(2,1)S(1)}, u32[]{:S(2)}, u32[]{:S(2)}) collective-permute-start(bf16[1,976,128]{2,1,0:T(8,128)(2,1)} %get-tuple-element.106), channel_id=1, source_target_pairs={{0,20},{4,16},{8,28},{12,24},{16,4},{20,0},{24,12},{28,8},{1,21},{... | collective-permute-start | bytes 749576 | tf_op jit(solution)/shard_map/ppermute | solution.py:560
  13.3 30.7 %collective-permute-start.4 = (bf16[1,976,128]{2,1,0:T(8,128)(2,1)}, bf16[1,976,128]{2,1,0:T(8,128)(2,1)}, u32[]{:S(2)}, u32[]{:S(2)}) collective-permute-start(bf16[1,976,128]{2,1,0:T(8,128)(2,1)} %get-tuple-element.107), channel_id=1, source_target_pairs={{0,12},{4,8},{8,4},{12,0},{16,28},{20,24},{24,20},{28,16},{1,13},{... | collective-permute-start | bytes 749576 | tf_op jit(solution)/shard_map/ppermute | solution.py:560
  13.7 32.1 %collective-permute-start = (bf16[2,976,128]{2,1,0:T(8,128)(2,1)}, bf16[2,976,128]{2,1,0:T(8,128)(2,1)}, u32[]{:S(2)}, u32[]{:S(2)}) collective-permute-start(bf16[2,976,128]{2,1,0:T(8,128)(2,1)} %get-tuple-element.103), channel_id=1, source_target_pairs={{0,16},{4,20},{8,24},{12,28},{16,0},{20,4},{24,8},{28,12},{1,17},{... | collective-permute-start | bytes 1499144 | tf_op jit(solution)/shard_map/ppermute | solution.py:560
  14.1 33.0 %collective-permute-start.1 = (bf16[2,976,128]{2,1,0:T(8,128)(2,1)}, bf16[2,976,128]{2,1,0:T(8,128)(2,1)}, u32[]{:S(2)}, u32[]{:S(2)}) collective-permute-start(bf16[2,976,128]{2,1,0:T(8,128)(2,1)} %get-tuple-element.104), channel_id=1, source_target_pairs={{0,8},{4,12},{8,0},{12,4},{16,24},{20,28},{24,16},{28,20},{1,9},{5... | collective-permute-start | bytes 1499144 | tf_op jit(solution)/shard_map/ppermute | solution.py:560
  15.9 31.2 %collective-permute-start.2 = (bf16[2,976,128]{2,1,0:T(8,128)(2,1)}, bf16[2,976,128]{2,1,0:T(8,128)(2,1)}, u32[]{:S(2)}, u32[]{:S(2)}) collective-permute-start(bf16[2,976,128]{2,1,0:T(8,128)(2,1)} %get-tuple-element.105), channel_id=1, source_target_pairs={{0,4},{4,0},{8,12},{12,8},{16,20},{20,16},{24,28},{28,24},{1,5},{5... | collective-permute-start | bytes 1499144 | tf_op jit(solution)/shard_map/ppermute | solution.py:560
  17.4 1.5 %copy-start = (bf16[8,4,240,128]{3,2,1,0:T(8,128)(2,1)S(1)}, bf16[8,4,240,128]{3,2,1,0:T(8,128)(2,1)}, u32[]{:S(2)}) copy-start(bf16[8,4,240,128]{3,2,1,0:T(8,128)(2,1)} %get-tuple-element.100.start_ref) | copy-start | bytes 5898244
  19.0 0.9 %copy-start.8 = (bf16[128,448]{1,0:T(8,128)(2,1)S(1)}, bf16[128,448]{1,0:T(8,128)(2,1)}, u32[]{:S(2)}) copy-start(bf16[128,448]{1,0:T(8,128)(2,1)} %get-tuple-element.99.v_ref) | copy-start | bytes 344068
  19.9 0.8 copy-start.10
  20.6 0.8 copy-start.11
  24.0 13.3 %copy-start.1 = (bf16[8,16,1792]{2,1,0:T(8,128)(2,1)S(1)}, bf16[8,16,1792]{2,1,0:T(8,128)(2,1)}, u32[]{:S(2)}) copy-start(bf16[8,16,1792]{2,1,0:T(8,128)(2,1)} %param.20) | copy-start | bytes 1376260
  24.0 13.2 %copy-start.2 = (bf16[1792,512]{1,0:T(8,128)(2,1)S(1)}, bf16[1792,512]{1,0:T(8,128)(2,1)}, u32[]{:S(2)}) copy-start(bf16[1792,512]{1,0:T(8,128)(2,1)} %wg_ref.1) | copy-start | bytes 5505028
  24.0 13.2 %copy-start.12 = (f32[1792]{0:T(1024)S(1)}, f32[1792]{0:T(1024)}, u32[]{:S(2)}) copy-start(f32[1792]{0:T(1024)} %gain_ref.1) | copy-start | bytes 21508
  37.2 1.5 %copy-start.3 = (bf16[1792,512]{1,0:T(8,128)(2,1)S(1)}, bf16[1792,512]{1,0:T(8,128)(2,1)}, u32[]{:S(2)}) copy-start(bf16[1792,512]{1,0:T(8,128)(2,1)} %wu_ref.1) | copy-start | bytes 5505028
  38.7 1.5 %copy-start.4 = (bf16[512,1792]{1,0:T(8,128)(2,1)S(1)}, bf16[512,1792]{1,0:T(8,128)(2,1)}, u32[]{:S(2)}) copy-start(bf16[512,1792]{1,0:T(8,128)(2,1)} %wd_ref.1) | copy-start | bytes 5505028
  43.9 31.3 %copy-start.13 = (bf16[2,976,128]{2,1,0:T(8,128)(2,1)S(1)}, bf16[2,976,128]{2,1,0:T(8,128)(2,1)}, u32[]{:S(2)}) copy-start(bf16[2,976,128]{2,1,0:T(8,128)(2,1)} %get-tuple-element.114.rest_0_) | copy-start | bytes 1499140
  48.3 29.2 %collective-permute-start.7 = (bf16[2,976,128]{2,1,0:T(8,128)(2,1)S(1)}, bf16[2,976,128]{2,1,0:T(8,128)(2,1)}, u32[]{:S(2)}, u32[]{:S(2)}) collective-permute-start(bf16[2,976,128]{2,1,0:T(8,128)(2,1)S(1)} %get-tuple-element.124), channel_id=1, source_target_pairs={{0,4},{4,0},{8,12},{12,8},{16,20},{20,16},{24,28},{28,24},{1,5},{5... | collective-permute-start | bytes 1499144 | tf_op jit(solution)/shard_map/ppermute | solution.py:560
  48.8 19.1 %collective-permute-start.5 = (bf16[1,976,128]{2,1,0:T(8,128)(2,1)}, bf16[1,976,128]{2,1,0:T(8,128)(2,1)S(1)}, u32[]{:S(2)}, u32[]{:S(2)}) collective-permute-start(bf16[1,976,128]{2,1,0:T(8,128)(2,1)} %get-tuple-element.111), channel_id=1, source_target_pairs={{0,24},{4,28},{8,16},{12,20},{16,8},{20,12},{24,0},{28,4},{1,25},{... | collective-permute-start | bytes 749576 | tf_op jit(solution)/shard_map/ppermute | solution.py:560
  50.1 25.1 %collective-permute-start.6 = (bf16[1,976,128]{2,1,0:T(8,128)(2,1)}, bf16[1,976,128]{2,1,0:T(8,128)(2,1)S(1)}, u32[]{:S(2)}, u32[]{:S(2)}) collective-permute-start(bf16[1,976,128]{2,1,0:T(8,128)(2,1)} %get-tuple-element.112), channel_id=1, source_target_pairs={{0,28},{4,24},{8,20},{12,16},{16,12},{20,8},{24,4},{28,0},{1,29},{... | collective-permute-start | bytes 749576 | tf_op jit(solution)/shard_map/ppermute | solution.py:560
  51.8 25.6 %collective-permute-start.9 = (bf16[1,976,128]{2,1,0:T(8,128)(2,1)S(1)}, bf16[1,976,128]{2,1,0:T(8,128)(2,1)}, u32[]{:S(2)}, u32[]{:S(2)}) collective-permute-start(bf16[1,976,128]{2,1,0:T(8,128)(2,1)S(1)} %get-tuple-element.125), channel_id=1, source_target_pairs={{0,12},{4,8},{8,4},{12,0},{16,28},{20,24},{24,20},{28,16},{1,13},{... | collective-permute-start | bytes 749576 | tf_op jit(solution)/shard_map/ppermute | solution.py:560
  55.1 22.4 %collective-permute-start.8 = (bf16[1,976,128]{2,1,0:T(8,128)(2,1)S(1)}, bf16[1,976,128]{2,1,0:T(8,128)(2,1)}, u32[]{:S(2)}, u32[]{:S(2)}) collective-permute-start(bf16[1,976,128]{2,1,0:T(8,128)(2,1)S(1)} %get-tuple-element.125), channel_id=1, source_target_pairs={{0,8},{4,12},{8,0},{12,4},{16,24},{20,28},{24,16},{28,20},{1,9},{5... | collective-permute-start | bytes 749576 | tf_op jit(solution)/shard_map/ppermute | solution.py:560
